TPU v7x, 128 devices: a whole 4x4x4 slice. The times are simulated.
128 devices in a mesh: space: 32 (over z, x, core), segment: 4 (over y).
Axes of the slice: x: 4, y: 4, z: 4, core: 2. Of those that a mesh axis runs over, the one named last changes fastest.
Arguments:
- features: bfloat16 [4, 32768, 128], P('segment', 'space'), may hold values from -6 to 6
- weights: bfloat16 [4, 27, 128, 128], P('segment'), may hold values from -0.109375 to 0.109375
- cotangent: bfloat16 [4, 32768, 128], P('segment', 'space'), may hold values from -6 to 6
- local_map: int32 [32768, 27], P('space'), may hold values from 0 to 1024, as said below
- send_map: int32 [36864, 27], P('space'), may hold values from 0 to 1024, as said below
- recv_map: int32 [36864], P('space'), may hold values from 0 to 1024, as said below
Outputs:
- mixed: bfloat16 [4, 32768, 128], P('segment', 'space')
- input_grad: bfloat16 [4, 32768, 128], P('segment', 'space')
- weight_grad: float32 [4, 27, 128, 128], P('segment')
Inputs may be any that keep to these rules, and one draw needn't show every extreme that they name: Each tile is a block of 8 x 8 x 32 cells of a grid of 4 x 8 tiles, of which exactly 1024 cells are occupied. local_map[p, v, k] is the row of the occupied cell at offset (k // 9 - 1, (k // 3) % 3 - 1, k % 3 - 1) from voxel v inside the same tile, else 1024; offset 13 is the voxel itself, and local_map[p, v, k] = u < 1024 exactly when local_map[p, u, 26 - k] = v. For tile p and direction d, the slots list the cells of the neighbouring tile p + delta(d) that touch tile p (a face of 256 cells, or a vertical edge of 32 cells for a diagonal direction); send_map[p, d, c, k] is the row in tile p of the occupied cell at offset k from slot c's cell, else 1024. A direction without a neighbouring tile has only 1024. recv_map[q, d, c] is the row in tile q of the cell of slot c of the list that tile q - delta(d) holds for direction d, or 1024 where that cell is empty or that tile does not exist.
All inputs are finite; a program needn't handle non-finite values.
Results may differ from a plain program's by a relative error of at most 0.0051.
Values may be sent and summed in bfloat16 or wider, within the bound.
No kernel may reach another device: no remote copies, remote signals or barrier semaphores. Data moves between devices by JAX's collectives and lax.ppermute only.
A program may use at most 64 MiB of HBM per device.

v0:
```python
import functools

import jax
import jax.numpy as jnp
from jax import lax
from jax.experimental import pallas as pl
from jax.experimental.pallas import tpu as pltpu
from jax.sharding import PartitionSpec as P

TZ = 32
TILES_X = 4
CAP = 256
ROWS = 1024
C = 128
HALO = 1152

DIRECTIONS = ((-1, -1), (-1, 0), (-1, 1), (0, -1), (0, 1), (1, -1), (1, 0), (1, 1))
BF = jnp.bfloat16
F32 = jnp.float32


def spans():
    result = []
    start = 0
    for step_x, step_y in DIRECTIONS:
        length = TZ if step_x != 0 and step_y != 0 else CAP
        result.append((start, length))
        start = start + length
    return result


SPANS = spans()
FACES = [n for n, (a, b) in enumerate(DIRECTIONS) if a == 0 or b == 0]
CORNERS = [n for n, (a, b) in enumerate(DIRECTIONS) if a != 0 and b != 0]


def toward(step_x, step_y):
    picked = []
    for offset in range(27):
        along_x = offset // 9 - 1
        along_y = offset // 3 % 3 - 1
        if (step_x == 0 or along_x == -step_x) and (step_y == 0 or along_y == -step_y):
            picked.append(offset)
    return picked


def dot(a, b, dims=((1,), (0,))):
    return lax.dot_general(a, b, (dims, ((), ())), preferred_element_type=F32)


def hot(row, rows):
    pos = lax.broadcasted_iota(jnp.int32, (256, 128), 0).astype(jnp.int16)
    count = row.shape[1]
    blocks = []
    for base in range(0, rows, 256):
        rel = (row - base).astype(jnp.int16)
        parts = [
            jnp.where(rel[:, t : t + 128] == pos, BF(1), BF(0)) for t in range(0, count, 128)
        ]
        blocks.append(jnp.concatenate(parts, 1))
    return jnp.concatenate(blocks, 0)


def match(column, row):
    return jnp.where(column == row.astype(jnp.int16), BF(1), BF(0))


def spread(column, count):
    kept = jnp.where(column == ROWS, -1, column)
    return jnp.broadcast_to(kept, (column.shape[0], count)).astype(jnp.int16)


def corner_mask(position, axis, shape):
    lane = lax.broadcasted_iota(jnp.int32, shape, axis)
    return (lane // TZ) == position


def lists_of(number):
    return SPANS[number]


def face_match(number, offset, column, sm_ref):
    start, length = SPANS[number]
    return match(column, sm_ref[offset, :, start : start + length])


def corner_row(place, sm_ref):
    pieces = []
    for number in CORNERS:
        start, length = SPANS[number]
        offset = toward(*DIRECTIONS[number])[place]
        pieces.append(sm_ref[offset, :, start : start + length])
    return jnp.concatenate(pieces, 1)


def corner_column(rc_ref, count):
    pieces = []
    for number in CORNERS:
        start, length = SPANS[7 - number]
        pieces.append(rc_ref[start : start + length, :])
    return spread(jnp.concatenate(pieces, 0), count)


def start_kernel(x_ref, rr_ref, rc_ref, sm_ref, w_ref, part_ref, face_g_ref, corner_g_ref):
    x_t = x_ref[...].astype(F32).T.astype(BF)
    selector = hot(rr_ref[...], ROWS)
    listed = dot(x_t, selector).astype(BF)
    for place, number in enumerate(FACES):
        start, length = SPANS[number]
        other, _ = SPANS[7 - number]
        column = spread(rc_ref[other : other + length, :], length)
        source = listed[:, other : other + length]
        picked = toward(*DIRECTIONS[number])
        gathered = []
        for offset in picked:
            chosen = face_match(number, offset, column, sm_ref)
            gathered.append(dot(source, chosen).astype(BF))
        gathered = jnp.concatenate(gathered, 0)
        face_g_ref[place] = gathered
        weight = jnp.concatenate([w_ref[offset] for offset in picked], 0)
        total = dot(weight, gathered, ((0,), (0,)))
        part_ref[start : start + length, :] = total.T.astype(BF)
    column = corner_column(rc_ref, 4 * TZ)
    source = jnp.concatenate(
        [listed[:, SPANS[7 - n][0] : SPANS[7 - n][0] + TZ] for n in CORNERS], 1
    )
    gathered = []
    for step in range(3):
        chosen = match(column, corner_row(step, sm_ref))
        gathered.append(dot(source, chosen).astype(BF))
    masked = []
    weights = []
    for place, number in enumerate(CORNERS):
        inside = corner_mask(place, 1, (C, 4 * TZ))
        for step in range(3):
            masked.append(jnp.where(inside, gathered[step], BF(0)))
            weights.append(w_ref[toward(*DIRECTIONS[number])[step]])
    masked = jnp.concatenate(masked, 0)
    corner_g_ref[...] = masked
    total = dot(jnp.concatenate(weights, 0), masked, ((0,), (0,))).T.astype(BF)
    for place, number in enumerate(CORNERS):
        start, length = SPANS[number]
        part_ref[start : start + length, :] = total[place * TZ : (place + 1) * TZ, :]


def pair_of(step):
    first = jnp.where(2 * step >= 13, 2 * step + 1, 2 * step)
    second = jnp.where(2 * step + 1 >= 13, 2 * step + 2, 2 * step + 1)
    return first, second


def forward_kernel(x_ref, lm_ref, w_ref, g_ref, pre_ref, x_t, total, *, width):
    step = pl.program_id(0)

    @pl.when(step == 0)
    def _():
        x_t[...] = x_ref[...].astype(F32).T.astype(BF)
        total[...] = dot(w_ref[13], x_t[...], ((0,), (0,)))

    pair = pair_of(step)
    weight = jnp.concatenate([w_ref[k] for k in pair], 0)
    for begin in range(0, ROWS, width):
        cols = slice(begin, begin + width)
        gathered = [dot(x_t[...], hot(lm_ref[k, :, cols], ROWS)).astype(BF) for k in pair]
        gathered = jnp.concatenate(gathered, 0)
        g_ref[:, cols] = gathered
        total[:, cols] += dot(weight, gathered, ((0,), (0,)))

    @pl.when(step == 12)
    def _():
        pre_ref[...] = total[...].T


def activate_kernel(pre_ref, part_ref, rr_ref, cot_ref, pair_ref, act_ref, grad_ref, out_ref):
    selector = hot(rr_ref[...], ROWS)
    pre = pre_ref[...] + dot(selector, part_ref[...])
    gate = 1.0 / (1.0 + jnp.exp(-pre))
    act_ref[...] = (pre * gate).astype(BF)
    upstream = cot_ref[...].astype(F32) + pair_ref[...].astype(F32)
    grad = upstream * gate * (1.0 + pre * (1.0 - gate))
    grad_ref[...] = grad.astype(BF)
    grad_t = grad.T.astype(BF)
    out_ref[...] = dot(grad_t, selector).T.astype(BF)


def weight_kernel(g_ref, grad_ref, x_ref, dw_ref):
    step = pl.program_id(0)
    first, second = pair_of(step)

    @pl.when(step == 0)
    def _():
        dw_ref[13] = dot(x_ref[...], grad_ref[...], ((0,), (0,)))

    both = dot(g_ref[...], grad_ref[...])
    dw_ref[first] = both[:C]
    dw_ref[second] = both[C:]


def return_kernel(back_ref, rc_ref, sm_ref, w_ref, face_g_ref, corner_g_ref, dw_in_ref, dw_ref, placed_ref, total):
    total[...] = dw_in_ref[...]
    for place, number in enumerate(FACES):
        start, length = SPANS[number]
        other, _ = SPANS[7 - number]
        column = spread(rc_ref[other : other + length, :], length)
        back = back_ref[start : start + length, :]
        picked = toward(*DIRECTIONS[number])
        pieces = []
        for offset in picked:
            chosen = face_match(number, offset, column, sm_ref)
            pieces.append(dot(chosen, back).astype(BF))
        pieces = jnp.concatenate(pieces, 1)
        weight = jnp.concatenate([w_ref[offset] for offset in picked], 1)
        placed_ref[other : other + length, :] = dot(pieces, weight, ((1,), (1,)))
        kernel_part = dot(face_g_ref[place], back)
        for index, offset in enumerate(picked):
            total[offset] += kernel_part[index * C : (index + 1) * C, :]
    column = corner_column(rc_ref, 4 * TZ)
    back = jnp.concatenate([back_ref[SPANS[n][0] : SPANS[n][0] + TZ, :] for n in CORNERS], 0)
    kernel_part = dot(corner_g_ref[...], back)
    pieces = []
    weights = []
    spots = [dot(match(column, corner_row(step, sm_ref)), back).astype(BF) for step in range(3)]
    for place, number in enumerate(CORNERS):
        inside = corner_mask(place, 0, (4 * TZ, C))
        for step in range(3):
            offset = toward(*DIRECTIONS[number])[step]
            row = (place * 3 + step) * C
            total[offset] += kernel_part[row : row + C, :]
            pieces.append(jnp.where(inside, spots[step], BF(0)))
            weights.append(w_ref[offset])
    result = dot(jnp.concatenate(pieces, 1), jnp.concatenate(weights, 1), ((1,), (1,)))
    for place, number in enumerate(CORNERS):
        other, length = SPANS[7 - number]
        placed_ref[other : other + length, :] = result[place * TZ : (place + 1) * TZ, :]
    dw_ref[...] = total[...].astype(BF)


def backward_kernel(grad_ref, own_ref, lm_ref, w_ref, out_ref, grad_t, total):
    step = pl.program_id(0)

    @pl.when(step == 0)
    def _():
        grad_t[...] = grad_ref[...].astype(F32).T.astype(BF)
        total[...] = dot(w_ref[13], own_ref[...].astype(F32).T.astype(BF))

    pair = pair_of(step)
    weight = jnp.concatenate([w_ref[k] for k in pair], 1)
    gathered = [dot(grad_t[...], hot(lm_ref[26 - k], ROWS)).astype(BF) for k in pair]
    total[...] += dot(weight, jnp.concatenate(gathered, 0))

    @pl.when(step == 12)
    def _():
        out_ref[...] = total[...].T


def final_kernel(local_ref, placed_ref, rr_ref, act_ref, pair_ref, mixed_ref, out_ref):
    placed = placed_ref[...]
    high = placed.astype(BF)
    low = (placed - high.astype(F32)).astype(BF)
    both = dot(hot(rr_ref[...], ROWS), jnp.concatenate([high, low], 1))
    out_ref[...] = (local_ref[...] + both[:, :C] + both[:, C:]).astype(BF)
    mixed_ref[...] = (act_ref[...].astype(F32) + pair_ref[...].astype(F32)).astype(BF)


PARAMS = pltpu.CompilerParams(vmem_limit_bytes=48 * 2**20)


def shape(dims, dtype):
    return jax.ShapeDtypeStruct(dims, dtype)


def whole(dims):
    return pl.BlockSpec(dims, lambda *ids: (0,) * len(dims))


def shifted(value, steps):
    count = lax.axis_size("space")
    initial, last = (max(0, -steps), min(count, count - steps))
    return lax.ppermute(value, "space", [(i, i + steps) for i in range(initial, last)])


def exchange(lists, orient):
    received = []
    for number, (step_x, step_y) in enumerate(DIRECTIONS):
        start, length = SPANS[number]
        received.append(
            shifted(lists[start : start + length], orient * (step_x + TILES_X * step_y))
        )
    return jnp.concatenate(received, 0)


def swapped(array):
    return lax.ppermute(array, "segment", [(i, i ^ 1) for i in range(lax.axis_size("segment"))])


def xor_send(value, bits):
    return lax.ppermute(value, "space", [(i, i ^ bits) for i in range(lax.axis_size("space"))])


def add_up(pieces):
    total = pieces[0].astype(F32)
    for piece in pieces[1:]:
        total = total + piece.astype(F32)
    return total.astype(BF)


def reduce_weights(dw):
    me = lax.axis_index("space")
    core, x_at = me % 2, me // 2 % 4
    halves = dw.reshape(2, -1, C)
    pick = functools.partial(lax.dynamic_index_in_dim, axis=0, keepdims=False)
    half = add_up([pick(halves, core), xor_send(pick(halves, 1 - core), 1)])
    quarters = half.reshape(4, -1, C)
    got = [pick(quarters, x_at)]
    for bits in (1, 2, 3):
        got.append(xor_send(pick(quarters, x_at ^ bits), bits * 2))
    quarter = add_up(got)
    got = [xor_send(quarter, bits * 8) for bits in (1, 2, 3)]
    z_at = me // 8
    stacked = jnp.stack([quarter] + got)
    quarter = add_up([pick(stacked, z_at ^ index) for index in range(4)])
    got = jnp.stack([quarter] + [xor_send(quarter, bits * 2) for bits in (1, 2, 3)])
    half = jnp.stack([pick(got, x_at ^ index) for index in range(4)])
    got = jnp.stack([half, xor_send(half, 1)])
    both = jnp.stack([pick(got, core), pick(got, 1 - core)])
    return both.reshape(dw.shape).astype(F32)


def on_device(features, weights, cotangent, local_map, send_map, recv_map):
    x = features[0]
    w = weights[0]
    cot = cotangent[0]
    lm = local_map.T.reshape(27, 1, ROWS)
    sm = send_map.T.reshape(27, 1, HALO)
    rr = recv_map.reshape(1, HALO)
    rc = recv_map.reshape(HALO, 1)
    part, face_g, corner_g = pl.pallas_call(
        start_kernel,
        out_shape=[shape((HALO, C), BF), shape((4, 9 * C, CAP), BF), shape((12 * C, 4 * TZ), BF)],
        compiler_params=PARAMS,
        name="start",
    )(x, rr, rc, sm, w)
    arrived = exchange(part, 1)
    cot_pair = swapped(cot)
    gathered, pre = pl.pallas_call(
        functools.partial(forward_kernel, width=512),
        grid=(13,),
        in_specs=[whole((ROWS, C)), whole((27, 1, ROWS)), whole((27, C, C))],
        out_specs=[pl.BlockSpec((2 * C, ROWS), lambda j: (j, 0)), whole((ROWS, C))],
        out_shape=[shape((26 * C, ROWS), BF), shape((ROWS, C), F32)],
        scratch_shapes=[pltpu.VMEM((C, ROWS), BF), pltpu.VMEM((C, ROWS), F32)],
        compiler_params=PARAMS,
        name="forward",
    )(x, lm, w)
    act, grad, outgoing = pl.pallas_call(
        activate_kernel,
        out_shape=[shape((ROWS, C), BF), shape((ROWS, C), BF), shape((HALO, C), BF)],
        compiler_params=PARAMS,
        name="activate",
    )(pre, arrived, rr, cot, cot_pair)
    returned = exchange(outgoing, -1)
    act_pair = swapped(act)
    dw_local = pl.pallas_call(
        weight_kernel,
        grid=(13,),
        in_specs=[pl.BlockSpec((2 * C, ROWS), lambda j: (j, 0)), whole((ROWS, C)), whole((ROWS, C))],
        out_specs=whole((27, C, C)),
        out_shape=shape((27, C, C), F32),
        compiler_params=PARAMS,
        name="weight",
    )(gathered, grad, x)
    dw, placed = pl.pallas_call(
        return_kernel,
        out_shape=[shape((27, C, C), BF), shape((HALO, C), F32)],
        scratch_shapes=[pltpu.VMEM((27, C, C), F32)],
        compiler_params=PARAMS,
        name="returning",
    )(returned, rc, sm, w, face_g, corner_g, dw_local)
    weight_grad = reduce_weights(dw)
    parts = []
    size = ROWS // 2
    for begin in range(0, ROWS, size):
        parts.append(
            pl.pallas_call(
                backward_kernel,
                grid=(13,),
                in_specs=[whole((ROWS, C)), pl.BlockSpec((size, C), lambda j, at=begin // size: (at, 0)),
                          pl.BlockSpec((27, 1, size), lambda j, at=begin // size: (0, 0, at)), whole((27, C, C))],
                out_specs=whole((size, C)),
                out_shape=shape((size, C), F32),
                scratch_shapes=[pltpu.VMEM((C, ROWS), BF), pltpu.VMEM((C, size), F32)],
                compiler_params=PARAMS,
                name="backward",
            )(grad, grad, lm, w)
        )
    local = jnp.concatenate(parts, 0)
    mixed, input_grad = pl.pallas_call(
        final_kernel,
        out_shape=[shape((ROWS, C), BF), shape((ROWS, C), BF)],
        compiler_params=PARAMS,
        name="final",
    )(local, placed, rr, act, act_pair)
    return (mixed[None], input_grad[None], weight_grad[None])


def solution(mesh):
    in_specs = (
        P("segment", "space", None),
        P("segment", None, None, None),
        P("segment", "space", None),
        P("space", None),
        P("space", None),
        P("space"),
    )
    out_specs = (
        P("segment", "space", None),
        P("segment", "space", None),
        P("segment", None, None, None),
    )
    return jax.shard_map(
        on_device, mesh=mesh, in_specs=in_specs, out_specs=out_specs, check_vma=False
    )
```

profile of v0, /device:TPU:1, one launch (start us, length us, event | category | flops | bytes accessed | tf_op | source)
XLA Modules:
  0.0 175.6 jit_solution(13648340389277796922)
XLA Ops:
  0.6 0.8 reshape.50.rr_ref
  1.4 0.9 reshape.58.rc_ref
  2.3 1.0 reshape.52.sm_ref
  3.3 1.2 copy-done
  4.5 0.9 copy-done.2
  5.5 4.2 %start.1 = (bf16[1152,128]{1,0:T(8,128)(2,1)S(1)}, bf16[4,1152,256]{2,1,0:T(8,128)(2,1)S(1)}, bf16[1536,128]{1,0:T(8,128)(2,1)S(1)}) custom-call(bf16[1024,128]{1,0:T(8,128)(2,1)S(1)} %bitcast.42, s32[1,1152]{1,0:T(1,128)S(1)} %reshape.50.rr_ref, s32[1152,1]{1,0:T(8,128)S(1)} %reshape.58.rc_ref, s32[27,1,1152]{2,1,0:T(1,128)S(1)} %reshape.52.sm_ref, ...), custom_call_target="tpu_custom_call" | custom-call | tf_op jit(solution)/shard_map/start/pallas_call | solution.py:337
  9.6 1.5 copy-done.4
  11.1 1.3 collective-permute-start
  12.4 3.3 %collective-permute-start.1 = (bf16[256,128]{1,0:T(8,128)(2,1)S(1)}, bf16[256,128]{1,0:T(8,128)(2,1)}, u32[]{:S(2)}, u32[]{:S(2)}) collective-permute-start(bf16[256,128]{1,0:T(8,128)(2,1)S(1)} %get-tuple-element.53), channel_id=1, source_target_pairs={{4,0},{8,4},{12,8},{16,12},{20,16},{24,20},{28,24},{32,28},{36,32}... | collective-permute-start | bytes 196616 | tf_op jit(solution)/shard_map/ppermute | solution.py:279
  15.8 4.6 %collective-permute-start.2 = (bf16[32,128]{1,0:T(8,128)(2,1)S(1)}, bf16[32,128]{1,0:T(8,128)(2,1)S(1)}, u32[]{:S(2)}, u32[]{:S(2)}) collective-permute-start(bf16[32,128]{1,0:T(8,128)(2,1)S(1)} %get-tuple-element.48), channel_id=1, source_target_pairs={{0,12},{4,16},{8,20},{12,24},{16,28},{20,32},{24,36},{28,40},{32,4... | collective-permute-start | bytes 24584 | tf_op jit(solution)/shard_map/ppermute | solution.py:279
  20.4 1.3 collective-permute-start.3
  21.7 8.2 %collective-permute-start.4 = (bf16[256,128]{1,0:T(8,128)(2,1)S(1)}, bf16[256,128]{1,0:T(8,128)(2,1)S(1)}, u32[]{:S(2)}, u32[]{:S(2)}) collective-permute-start(bf16[256,128]{1,0:T(8,128)(2,1)S(1)} %get-tuple-element.51), channel_id=1, source_target_pairs={{0,16},{4,20},{8,24},{12,28},{16,32},{20,36},{24,40},{28,44},{32,4... | collective-permute-start | bytes 196616 | tf_op jit(solution)/shard_map/ppermute | solution.py:279
  29.9 0.1 reshape.49.lm_ref
  30.0 15.3 %forward.1 = (bf16[3328,1024]{1,0:T(8,128)(2,1)}, f32[1024,128]{1,0:T(8,128)S(1)}) custom-call(bf16[1024,128]{1,0:T(8,128)(2,1)S(1)} %bitcast.43, s32[27,1,1024]{2,1,0:T(1,128)S(1)} %reshape.49.lm_ref, bf16[27,128,128]{2,1,0:T(8,128)(2,1)S(1)} %bitcast.38), custom_call_target="tpu_custom_call" | custom-call | tf_op jit(solution)/shard_map/forward/pallas_call | solution.py:345
  45.3 1.3 collective-permute-start.5
  46.6 1.9 %collective-permute-start.6 = (bf16[256,128]{1,0:T(8,128)(2,1)S(1)}, bf16[256,128]{1,0:T(8,128)(2,1)S(1)}, u32[]{:S(2)}, u32[]{:S(2)}) collective-permute-start(bf16[256,128]{1,0:T(8,128)(2,1)S(1)} %get-tuple-element.50), channel_id=1, source_target_pairs={{0,4},{4,8},{8,12},{12,16},{16,20},{20,24},{24,28},{28,32},{32,36}... | collective-permute-start | bytes 196616 | tf_op jit(solution)/shard_map/ppermute | solution.py:279
  48.5 0.9 constant_dynamic-update-slice_fusion.6
  49.4 6.8 %collective-permute-start.7 = (bf16[32,128]{1,0:T(8,128)(2,1)S(1)}, bf16[32,128]{1,0:T(8,128)(2,1)S(1)}, u32[]{:S(2)}, u32[]{:S(2)}) collective-permute-start(bf16[32,128]{1,0:T(8,128)(2,1)S(1)} %get-tuple-element.46), channel_id=1, source_target_pairs={{0,20},{4,24},{8,28},{12,32},{16,36},{20,40},{24,44},{28,48},{32,5... | collective-permute-start | bytes 24584 | tf_op jit(solution)/shard_map/ppermute | solution.py:279
  56.2 1.4 collective-permute-start.8
  57.6 0.9 constant_dynamic-update-slice_fusion.4
  58.6 5.0 %collective-permute-done.8.pair_ref = bf16[1024,128]{1,0:T(8,128)(2,1)S(1)} collective-permute-done((bf16[1024,128]{1,0:T(8,128)(2,1)S(1)}, bf16[1024,128]{1,0:T(8,128)(2,1)S(1)}, u32[]{:S(2)}, u32[]{:S(2)}) %collective-permute-start.8) | collective-permute-done | bytes 262176 | tf_op jit(solution)/shard_map/ppermute | solution.py:293
  63.6 0.9 copy-done.8
  64.6 2.0 %activate.1 = (bf16[1024,128]{1,0:T(8,128)(2,1)S(1)}, bf16[1024,128]{1,0:T(8,128)(2,1)S(1)}, bf16[1152,128]{1,0:T(8,128)(2,1)S(1)}) custom-call(f32[1024,128]{1,0:T(8,128)S(1)} %get-tuple-element.15.pre_ref, bf16[1152,128]{1,0:T(8,128)(2,1)S(1)} %constant_dynamic-update-slice_fusion.part_ref, s32[1,1152]{1,0:T(1,128)S(1)} %reshape.50.rr_ref, ...), custom_call_target="tpu_custom_call" | custom-call | tf_op jit(solution)/shard_map/activate/pallas_call | solution.py:355
  66.6 6.3 %collective-permute-start.9 = (bf16[32,128]{1,0:T(8,128)(2,1)S(1)}, bf16[32,128]{1,0:T(8,128)(2,1)S(1)}, u32[]{:S(2)}, u32[]{:S(2)}) collective-permute-start(bf16[32,128]{1,0:T(8,128)(2,1)S(1)} %get-tuple-element.41), channel_id=1, source_target_pairs={{0,20},{4,24},{8,28},{12,32},{16,36},{20,40},{24,44},{28,48},{32,5... | collective-permute-start | bytes 24584 | tf_op jit(solution)/shard_map/ppermute | solution.py:279
  72.9 2.5 %collective-permute-start.10 = (bf16[256,128]{1,0:T(8,128)(2,1)S(1)}, bf16[256,128]{1,0:T(8,128)(2,1)S(1)}, u32[]{:S(2)}, u32[]{:S(2)}) collective-permute-start(bf16[256,128]{1,0:T(8,128)(2,1)S(1)} %get-tuple-element.45), channel_id=1, source_target_pairs={{0,4},{4,8},{8,12},{12,16},{16,20},{20,24},{24,28},{28,32},{32,36}... | collective-permute-start | bytes 196616 | tf_op jit(solution)/shard_map/ppermute | solution.py:279
  75.4 1.3 collective-permute-start.11
  76.7 4.3 %collective-permute-start.12 = (bf16[256,128]{1,0:T(8,128)(2,1)S(1)}, bf16[256,128]{1,0:T(8,128)(2,1)S(1)}, u32[]{:S(2)}, u32[]{:S(2)}) collective-permute-start(bf16[256,128]{1,0:T(8,128)(2,1)S(1)} %get-tuple-element.44), channel_id=1, source_target_pairs={{0,16},{4,20},{8,24},{12,28},{16,32},{20,36},{24,40},{28,44},{32,4... | collective-permute-start | bytes 196616 | tf_op jit(solution)/shard_map/ppermute | solution.py:279
  81.0 1.3 collective-permute-start.13
  82.3 9.8 %weight.1.dw_in_ref = f32[27,128,128]{2,1,0:T(8,128)S(1)} custom-call(bf16[3328,1024]{1,0:T(8,128)(2,1)} %get-tuple-element.21.g_ref, bf16[1024,128]{1,0:T(8,128)(2,1)S(1)} %get-tuple-element.17.grad_ref.own_ref, bf16[1024,128]{1,0:T(8,128)(2,1)S(1)} %bitcast.44), custom_call_target="tpu_custom_call" | custom-call | tf_op jit(solution)/shard_map/weight/pallas_call | solution.py:363
  92.1 7.5 %collective-permute-start.14 = (bf16[32,128]{1,0:T(8,128)(2,1)S(1)}, bf16[32,128]{1,0:T(8,128)(2,1)S(1)}, u32[]{:S(2)}, u32[]{:S(2)}) collective-permute-start(bf16[32,128]{1,0:T(8,128)(2,1)S(1)} %get-tuple-element.39), channel_id=1, source_target_pairs={{0,12},{4,16},{8,20},{12,24},{16,28},{20,32},{24,36},{28,40},{32,4... | collective-permute-start | bytes 24584 | tf_op jit(solution)/shard_map/ppermute | solution.py:279
  99.6 1.9 %collective-permute-start.15 = (bf16[256,128]{1,0:T(8,128)(2,1)S(1)}, bf16[256,128]{1,0:T(8,128)(2,1)S(1)}, u32[]{:S(2)}, u32[]{:S(2)}) collective-permute-start(bf16[256,128]{1,0:T(8,128)(2,1)S(1)} %get-tuple-element.42), channel_id=1, source_target_pairs={{4,0},{8,4},{12,8},{16,12},{20,16},{24,20},{28,24},{32,28},{36,32}... | collective-permute-start | bytes 196616 | tf_op jit(solution)/shard_map/ppermute | solution.py:279
  101.6 1.3 collective-permute-start.16
  103.0 2.2 %collective-permute-done.15 = bf16[256,128]{1,0:T(8,128)(2,1)S(1)} collective-permute-done((bf16[256,128]{1,0:T(8,128)(2,1)S(1)}, bf16[256,128]{1,0:T(8,128)(2,1)S(1)}, u32[]{:S(2)}, u32[]{:S(2)}) %collective-permute-start.15) | collective-permute-done | bytes 65568 | tf_op jit(solution)/shard_map/ppermute | solution.py:279
  105.2 3.7 %collective-permute-done.16 = bf16[32,128]{1,0:T(8,128)(2,1)S(1)} collective-permute-done((bf16[32,128]{1,0:T(8,128)(2,1)S(1)}, bf16[32,128]{1,0:T(8,128)(2,1)S(1)}, u32[]{:S(2)}, u32[]{:S(2)}) %collective-permute-start.16) | collective-permute-done | bytes 8224 | tf_op jit(solution)/shard_map/ppermute | solution.py:279
  108.9 5.2 %returning.1 = (bf16[27,128,128]{2,1,0:T(8,128)(2,1)S(1)}, f32[1152,128]{1,0:T(8,128)S(1)}) custom-call(bf16[1152,128]{1,0:T(8,128)(2,1)S(1)} %constant_dynamic-update-slice_fusion.8.back_ref, s32[1152,1]{1,0:T(8,128)S(1)} %reshape.58.rc_ref, s32[27,1,1152]{2,1,0:T(1,128)S(1)} %reshape.52.sm_ref, bf16[27,128,128]{2,1,0:T(8,128)(2,1)S(1)} %bitcast.39, ...), custom_call_target="tpu_custom_call" | custom-call | tf_op jit(solution)/shard_map/returning/pallas_call | solution.py:372
  114.1 0.8 copy-done.5
  114.9 0.3 collective-permute-start.18
  115.3 1.9 %collective-permute-done.18 = bf16[1728,128]{1,0:T(8,128)(2,1)} collective-permute-done((bf16[1728,128]{1,0:T(8,128)(2,1)S(1)}, bf16[1728,128]{1,0:T(8,128)(2,1)}, u32[]{:S(2)}, u32[]{:S(2)}) %collective-permute-start.18) | collective-permute-done | bytes 442400 | tf_op jit(solution)/shard_map/ppermute | solution.py:297
  117.1 1.1 fusion
  118.3 1.9 %collective-permute-start.19 = (bf16[432,128]{1,0:T(8,128)(2,1)S(1)}, bf16[432,128]{1,0:T(8,128)(2,1)S(1)}, u32[]{:S(2)}, u32[]{:S(2)}) collective-permute-start(bf16[432,128]{1,0:T(8,128)(2,1)S(1)} %get-tuple-element.35), channel_id=1, source_target_pairs={{0,8},{4,12},{8,0},{12,4},{16,24},{20,28},{24,16},{28,20},{32,40},... | collective-permute-start | bytes 331784 | tf_op jit(solution)/shard_map/ppermute | solution.py:297
  120.2 3.3 %collective-permute-start.20 = (bf16[432,128]{1,0:T(8,128)(2,1)S(1)}, bf16[432,128]{1,0:T(8,128)(2,1)S(1)}, u32[]{:S(2)}, u32[]{:S(2)}) collective-permute-start(bf16[432,128]{1,0:T(8,128)(2,1)S(1)} %get-tuple-element.37), channel_id=1, source_target_pairs={{0,16},{4,20},{8,24},{12,28},{16,0},{20,4},{24,8},{28,12},{32,48},... | collective-permute-start | bytes 331784 | tf_op jit(solution)/shard_map/ppermute | solution.py:297
  123.5 5.1 %collective-permute-done.20 = bf16[432,128]{1,0:T(8,128)(2,1)S(1)} collective-permute-done((bf16[432,128]{1,0:T(8,128)(2,1)S(1)}, bf16[432,128]{1,0:T(8,128)(2,1)S(1)}, u32[]{:S(2)}, u32[]{:S(2)}) %collective-permute-start.20) | collective-permute-done | bytes 110624 | tf_op jit(solution)/shard_map/ppermute | solution.py:297
  128.6 2.6 %collective-permute-done.21 = bf16[432,128]{1,0:T(8,128)(2,1)S(1)} collective-permute-done((bf16[432,128]{1,0:T(8,128)(2,1)S(1)}, bf16[432,128]{1,0:T(8,128)(2,1)S(1)}, u32[]{:S(2)}, u32[]{:S(2)}) %collective-permute-start.21) | collective-permute-done | bytes 110624 | tf_op jit(solution)/shard_map/ppermute | solution.py:297
  131.3 1.7 collective-permute-start.22
  133.0 1.3 collective-permute-start.23
  134.3 1.2 collective-permute-start.24
  135.5 0.1 collective-permute-done.22
  135.6 3.7 %collective-permute-done.23 = bf16[432,128]{1,0:T(8,128)(2,1)S(1)} collective-permute-done((bf16[432,128]{1,0:T(8,128)(2,1)S(1)}, bf16[432,128]{1,0:T(8,128)(2,1)S(1)}, u32[]{:S(2)}, u32[]{:S(2)}) %collective-permute-start.23) | collective-permute-done | bytes 110624 | tf_op jit(solution)/shard_map/ppermute | solution.py:297
  139.3 3.0 %collective-permute-done.24 = bf16[432,128]{1,0:T(8,128)(2,1)S(1)} collective-permute-done((bf16[432,128]{1,0:T(8,128)(2,1)S(1)}, bf16[432,128]{1,0:T(8,128)(2,1)S(1)}, u32[]{:S(2)}, u32[]{:S(2)}) %collective-permute-start.24) | collective-permute-done | bytes 110624 | tf_op jit(solution)/shard_map/ppermute | solution.py:297
  142.3 0.1 fusion.11
  142.3 0.1 collective-permute-start.25
  142.4 2.5 %collective-permute-start.26 = (bf16[432,128]{1,0:T(8,128)(2,1)S(1)}, bf16[432,128]{1,0:T(8,128)(2,1)S(1)}, u32[]{:S(2)}, u32[]{:S(2)}) collective-permute-start(bf16[432,128]{1,0:T(8,128)(2,1)S(1)} %fusion.11), channel_id=1, source_target_pairs={{0,16},{4,20},{8,24},{12,28},{16,0},{20,4},{24,8},{28,12},{32,48},... | collective-permute-start | bytes 331784 | tf_op jit(solution)/shard_map/ppermute | solution.py:297
  145.0 1.3 collective-permute-start.27
  146.4 2.7 %collective-permute-done.26 = bf16[432,128]{1,0:T(8,128)(2,1)S(1)} collective-permute-done((bf16[432,128]{1,0:T(8,128)(2,1)S(1)}, bf16[432,128]{1,0:T(8,128)(2,1)S(1)}, u32[]{:S(2)}, u32[]{:S(2)}) %collective-permute-start.26) | collective-permute-done | bytes 110624 | tf_op jit(solution)/shard_map/ppermute | solution.py:297
  149.1 2.8 %collective-permute-done.27 = bf16[432,128]{1,0:T(8,128)(2,1)S(1)} collective-permute-done((bf16[432,128]{1,0:T(8,128)(2,1)S(1)}, bf16[432,128]{1,0:T(8,128)(2,1)S(1)}, u32[]{:S(2)}, u32[]{:S(2)}) %collective-permute-start.27) | collective-permute-done | bytes 110624 | tf_op jit(solution)/shard_map/ppermute | solution.py:297
  152.0 0.1 pad_maximum_fusion.4
  152.1 1.3 collective-permute-start.28
  153.4 1.3 collective-permute-start.17
  154.7 8.6 %backward.2 = f32[512,128]{1,0:T(8,128)S(1)} custom-call(bf16[1024,128]{1,0:T(8,128)(2,1)S(1)} %get-tuple-element.17.grad_ref.own_ref, bf16[1024,128]{1,0:T(8,128)(2,1)S(1)} %get-tuple-element.17.grad_ref.own_ref, s32[27,1,1024]{2,1,0:T(1,128)S(1)} %reshape.49.lm_ref, bf16[27,128,128]{2,1,0:T(8,128)(2,1)S(1)} %bitcast.40), custom_call_target="tpu_custom_call" | custom-call | tf_op jit(solution)/shard_map/backward/pallas_call | solution.py:384
  163.4 8.7 %backward.3 = f32[512,128]{1,0:T(8,128)S(1)} custom-call(bf16[1024,128]{1,0:T(8,128)(2,1)S(1)} %get-tuple-element.17.grad_ref.own_ref, bf16[1024,128]{1,0:T(8,128)(2,1)S(1)} %get-tuple-element.17.grad_ref.own_ref, s32[27,1,1024]{2,1,0:T(1,128)S(1)} %reshape.49.lm_ref, bf16[27,128,128]{2,1,0:T(8,128)(2,1)S(1)} %bitcast.41), custom_call_target="tpu_custom_call" | custom-call | tf_op jit(solution)/shard_map/backward/pallas_call | solution.py:384
  172.1 1.7 final.1
  173.8 0.3 fusion.2
  174.1 0.1 pad_maximum_fusion
  174.2 1.4 convert.6
  (64 shorter events, 0.8 us)
Async XLA Ops:
  0.6 29.4 %copy-start.1 = (bf16[1,27,128,128]{3,2,1,0:T(8,128)(2,1)S(1)}, bf16[1,27,128,128]{3,2,1,0:T(8,128)(2,1)}, u32[]{:S(2)}) copy-start(bf16[1,27,128,128]{3,2,1,0:T(8,128)(2,1)} %param.7) | copy-start | bytes 2654212
  3.3 1.2 copy-start
  4.5 0.9 copy-start.2
  5.5 24.4 %copy-start.11 = (s32[1024,27]{0,1:T(8,128)S(1)}, s32[1024,27]{0,1:T(8,128)}, u32[]{:S(2)}) copy-start(s32[1024,27]{0,1:T(8,128)} %param.9) | copy-start | bytes 331780
  5.5 24.5 %copy-start.3 = (bf16[1,1024,128]{2,1,0:T(8,128)(2,1)S(1)}, bf16[1,1024,128]{2,1,0:T(8,128)(2,1)}, u32[]{:S(2)}) copy-start(bf16[1,1024,128]{2,1,0:T(8,128)(2,1)} %param.6) | copy-start | bytes 786436
  5.5 50.8 %copy-start.7 = (bf16[1,1024,128]{2,1,0:T(8,128)(2,1)S(1)}, bf16[1,1024,128]{2,1,0:T(8,128)(2,1)}, u32[]{:S(2)}) copy-start(bf16[1,1024,128]{2,1,0:T(8,128)(2,1)} %param.8) | copy-start | bytes 786436
  9.6 1.5 copy-start.4
  11.1 34.1 %collective-permute-start = (bf16[32,128]{1,0:T(8,128)(2,1)S(1)}, bf16[32,128]{1,0:T(8,128)(2,1)S(1)}, u32[]{:S(2)}, u32[]{:S(2)}) collective-permute-start(bf16[32,128]{1,0:T(8,128)(2,1)S(1)} %get-tuple-element.49), channel_id=1, source_target_pairs={{20,0},{24,4},{28,8},{32,12},{36,16},{40,20},{44,24},{48,28},{52,3... | collective-permute-start | bytes 24584 | tf_op jit(solution)/shard_map/ppermute | solution.py:279
  12.4 34.1 %collective-permute-start.1 = (bf16[256,128]{1,0:T(8,128)(2,1)S(1)}, bf16[256,128]{1,0:T(8,128)(2,1)}, u32[]{:S(2)}, u32[]{:S(2)}) collective-permute-start(bf16[256,128]{1,0:T(8,128)(2,1)S(1)} %get-tuple-element.53), channel_id=1, source_target_pairs={{4,0},{8,4},{12,8},{16,12},{20,16},{24,20},{28,24},{32,28},{36,32}... | collective-permute-start | bytes 196616 | tf_op jit(solution)/shard_map/ppermute | solution.py:279
  15.8 33.6 %collective-permute-start.2 = (bf16[32,128]{1,0:T(8,128)(2,1)S(1)}, bf16[32,128]{1,0:T(8,128)(2,1)S(1)}, u32[]{:S(2)}, u32[]{:S(2)}) collective-permute-start(bf16[32,128]{1,0:T(8,128)(2,1)S(1)} %get-tuple-element.48), channel_id=1, source_target_pairs={{0,12},{4,16},{8,20},{12,24},{16,28},{20,32},{24,36},{28,40},{32,4... | collective-permute-start | bytes 24584 | tf_op jit(solution)/shard_map/ppermute | solution.py:279
  20.4 35.8 %collective-permute-start.3 = (bf16[256,128]{1,0:T(8,128)(2,1)S(1)}, bf16[256,128]{1,0:T(8,128)(2,1)}, u32[]{:S(2)}, u32[]{:S(2)}) collective-permute-start(bf16[256,128]{1,0:T(8,128)(2,1)S(1)} %get-tuple-element.52), channel_id=1, source_target_pairs={{16,0},{20,4},{24,8},{28,12},{32,16},{36,20},{40,24},{44,28},{48,3... | collective-permute-start | bytes 196616 | tf_op jit(solution)/shard_map/ppermute | solution.py:279
  21.7 36.7 %collective-permute-start.4 = (bf16[256,128]{1,0:T(8,128)(2,1)S(1)}, bf16[256,128]{1,0:T(8,128)(2,1)S(1)}, u32[]{:S(2)}, u32[]{:S(2)}) collective-permute-start(bf16[256,128]{1,0:T(8,128)(2,1)S(1)} %get-tuple-element.51), channel_id=1, source_target_pairs={{0,16},{4,20},{8,24},{12,28},{16,32},{20,36},{24,40},{28,44},{32,4... | collective-permute-start | bytes 196616 | tf_op jit(solution)/shard_map/ppermute | solution.py:279
  45.3 13.2 %collective-permute-start.5 = (bf16[32,128]{1,0:T(8,128)(2,1)S(1)}, bf16[32,128]{1,0:T(8,128)(2,1)S(1)}, u32[]{:S(2)}, u32[]{:S(2)}) collective-permute-start(bf16[32,128]{1,0:T(8,128)(2,1)S(1)} %get-tuple-element.47), channel_id=1, source_target_pairs={{12,0},{16,4},{20,8},{24,12},{28,16},{32,20},{36,24},{40,28},{44,3... | collective-permute-start | bytes 24584 | tf_op jit(solution)/shard_map/ppermute | solution.py:279
  46.6 11.9 %collective-permute-start.6 = (bf16[256,128]{1,0:T(8,128)(2,1)S(1)}, bf16[256,128]{1,0:T(8,128)(2,1)S(1)}, u32[]{:S(2)}, u32[]{:S(2)}) collective-permute-start(bf16[256,128]{1,0:T(8,128)(2,1)S(1)} %get-tuple-element.50), channel_id=1, source_target_pairs={{0,4},{4,8},{8,12},{12,16},{16,20},{20,24},{24,28},{28,32},{32,36}... | collective-permute-start | bytes 196616 | tf_op jit(solution)/shard_map/ppermute | solution.py:279
  49.4 9.2 %collective-permute-start.7 = (bf16[32,128]{1,0:T(8,128)(2,1)S(1)}, bf16[32,128]{1,0:T(8,128)(2,1)S(1)}, u32[]{:S(2)}, u32[]{:S(2)}) collective-permute-start(bf16[32,128]{1,0:T(8,128)(2,1)S(1)} %get-tuple-element.46), channel_id=1, source_target_pairs={{0,20},{4,24},{8,28},{12,32},{16,36},{20,40},{24,44},{28,48},{32,5... | collective-permute-start | bytes 24584 | tf_op jit(solution)/shard_map/ppermute | solution.py:279
  56.2 7.4 %collective-permute-start.8 = (bf16[1024,128]{1,0:T(8,128)(2,1)S(1)}, bf16[1024,128]{1,0:T(8,128)(2,1)S(1)}, u32[]{:S(2)}, u32[]{:S(2)}) collective-permute-start(bf16[1024,128]{1,0:T(8,128)(2,1)S(1)} %bitcast.47), channel_id=1, source_target_pairs={{0,1},{1,0},{2,3},{3,2},{4,5},{5,4},{6,7},{7,6},{8,9},{9,8},{10,11... | collective-permute-start | bytes 786440 | tf_op jit(solution)/shard_map/ppermute | solution.py:293
  63.6 1.0 copy-start.8
  66.5 25.5 %copy-start.9 = (bf16[1024,128]{1,0:T(8,128)(2,1)}, bf16[1024,128]{1,0:T(8,128)(2,1)S(1)}, u32[]{:S(2)}) copy-start(bf16[1024,128]{1,0:T(8,128)(2,1)S(1)} %get-tuple-element.23.act_ref) | copy-start | bytes 786436
  66.6 25.5 %collective-permute-start.9 = (bf16[32,128]{1,0:T(8,128)(2,1)S(1)}, bf16[32,128]{1,0:T(8,128)(2,1)S(1)}, u32[]{:S(2)}, u32[]{:S(2)}) collective-permute-start(bf16[32,128]{1,0:T(8,128)(2,1)S(1)} %get-tuple-element.41), channel_id=1, source_target_pairs={{0,20},{4,24},{8,28},{12,32},{16,36},{20,40},{24,44},{28,48},{32,5... | collective-permute-start | bytes 24584 | tf_op jit(solution)/shard_map/ppermute | solution.py:279
  72.9 26.7 %collective-permute-start.10 = (bf16[256,128]{1,0:T(8,128)(2,1)S(1)}, bf16[256,128]{1,0:T(8,128)(2,1)S(1)}, u32[]{:S(2)}, u32[]{:S(2)}) collective-permute-start(bf16[256,128]{1,0:T(8,128)(2,1)S(1)} %get-tuple-element.45), channel_id=1, source_target_pairs={{0,4},{4,8},{8,12},{12,16},{16,20},{20,24},{24,28},{28,32},{32,36}... | collective-permute-start | bytes 196616 | tf_op jit(solution)/shard_map/ppermute | solution.py:279
  75.4 26.2 %collective-permute-start.11 = (bf16[32,128]{1,0:T(8,128)(2,1)S(1)}, bf16[32,128]{1,0:T(8,128)(2,1)S(1)}, u32[]{:S(2)}, u32[]{:S(2)}) collective-permute-start(bf16[32,128]{1,0:T(8,128)(2,1)S(1)} %get-tuple-element.40), channel_id=1, source_target_pairs={{12,0},{16,4},{20,8},{24,12},{28,16},{32,20},{36,24},{40,28},{44,3... | collective-permute-start | bytes 24584 | tf_op jit(solution)/shard_map/ppermute | solution.py:279
  76.7 26.2 %collective-permute-start.12 = (bf16[256,128]{1,0:T(8,128)(2,1)S(1)}, bf16[256,128]{1,0:T(8,128)(2,1)S(1)}, u32[]{:S(2)}, u32[]{:S(2)}) collective-permute-start(bf16[256,128]{1,0:T(8,128)(2,1)S(1)} %get-tuple-element.44), channel_id=1, source_target_pairs={{0,16},{4,20},{8,24},{12,28},{16,32},{20,36},{24,40},{28,44},{32,4... | collective-permute-start | bytes 196616 | tf_op jit(solution)/shard_map/ppermute | solution.py:279
  81.0 21.9 %collective-permute-start.13 = (bf16[256,128]{1,0:T(8,128)(2,1)S(1)}, bf16[256,128]{1,0:T(8,128)(2,1)S(1)}, u32[]{:S(2)}, u32[]{:S(2)}) collective-permute-start(bf16[256,128]{1,0:T(8,128)(2,1)S(1)} %get-tuple-element.43), channel_id=1, source_target_pairs={{16,0},{20,4},{24,8},{28,12},{32,16},{36,20},{40,24},{44,28},{48,3... | collective-permute-start | bytes 196616 | tf_op jit(solution)/shard_map/ppermute | solution.py:279
  92.1 10.9 %collective-permute-start.14 = (bf16[32,128]{1,0:T(8,128)(2,1)S(1)}, bf16[32,128]{1,0:T(8,128)(2,1)S(1)}, u32[]{:S(2)}, u32[]{:S(2)}) collective-permute-start(bf16[32,128]{1,0:T(8,128)(2,1)S(1)} %get-tuple-element.39), channel_id=1, source_target_pairs={{0,12},{4,16},{8,20},{12,24},{16,28},{20,32},{24,36},{28,40},{32,4... | collective-permute-start | bytes 24584 | tf_op jit(solution)/shard_map/ppermute | solution.py:279
  99.6 5.6 %collective-permute-start.15 = (bf16[256,128]{1,0:T(8,128)(2,1)S(1)}, bf16[256,128]{1,0:T(8,128)(2,1)S(1)}, u32[]{:S(2)}, u32[]{:S(2)}) collective-permute-start(bf16[256,128]{1,0:T(8,128)(2,1)S(1)} %get-tuple-element.42), channel_id=1, source_target_pairs={{4,0},{8,4},{12,8},{16,12},{20,16},{24,20},{28,24},{32,28},{36,32}... | collective-permute-start | bytes 196616 | tf_op jit(solution)/shard_map/ppermute | solution.py:279
  101.6 7.3 %collective-permute-start.16 = (bf16[32,128]{1,0:T(8,128)(2,1)S(1)}, bf16[32,128]{1,0:T(8,128)(2,1)S(1)}, u32[]{:S(2)}, u32[]{:S(2)}) collective-permute-start(bf16[32,128]{1,0:T(8,128)(2,1)S(1)} %get-tuple-element.38), channel_id=1, source_target_pairs={{20,0},{24,4},{28,8},{32,12},{36,16},{40,20},{44,24},{48,28},{52,3... | collective-permute-start | bytes 24584 | tf_op jit(solution)/shard_map/ppermute | solution.py:279
  114.1 0.8 copy-start.5
  114.9 2.2 %collective-permute-start.18 = (bf16[1728,128]{1,0:T(8,128)(2,1)S(1)}, bf16[1728,128]{1,0:T(8,128)(2,1)}, u32[]{:S(2)}, u32[]{:S(2)}) collective-permute-start(bf16[1728,128]{1,0:T(8,128)(2,1)S(1)} %dynamic-slice_bitcast_fusion), channel_id=1, source_target_pairs={{0,4},{4,0},{8,12},{12,8},{16,20},{20,16},{24,28},{28,24},{32,36},... | collective-permute-start | bytes 1327112 | tf_op jit(solution)/shard_map/ppermute | solution.py:297
  118.3 5.2 %collective-permute-start.19 = (bf16[432,128]{1,0:T(8,128)(2,1)S(1)}, bf16[432,128]{1,0:T(8,128)(2,1)S(1)}, u32[]{:S(2)}, u32[]{:S(2)}) collective-permute-start(bf16[432,128]{1,0:T(8,128)(2,1)S(1)} %get-tuple-element.35), channel_id=1, source_target_pairs={{0,8},{4,12},{8,0},{12,4},{16,24},{20,28},{24,16},{28,20},{32,40},... | collective-permute-start | bytes 331784 | tf_op jit(solution)/shard_map/ppermute | solution.py:297
  120.2 8.4 %collective-permute-start.20 = (bf16[432,128]{1,0:T(8,128)(2,1)S(1)}, bf16[432,128]{1,0:T(8,128)(2,1)S(1)}, u32[]{:S(2)}, u32[]{:S(2)}) collective-permute-start(bf16[432,128]{1,0:T(8,128)(2,1)S(1)} %get-tuple-element.37), channel_id=1, source_target_pairs={{0,16},{4,20},{8,24},{12,28},{16,0},{20,4},{24,8},{28,12},{32,48},... | collective-permute-start | bytes 331784 | tf_op jit(solution)/shard_map/ppermute | solution.py:297
  123.4 7.8 %collective-permute-start.21 = (bf16[432,128]{1,0:T(8,128)(2,1)S(1)}, bf16[432,128]{1,0:T(8,128)(2,1)S(1)}, u32[]{:S(2)}, u32[]{:S(2)}) collective-permute-start(bf16[432,128]{1,0:T(8,128)(2,1)S(1)} %get-tuple-element.36), channel_id=1, source_target_pairs={{0,24},{4,28},{8,16},{12,20},{16,8},{20,12},{24,0},{28,4},{32,56},... | collective-permute-start | bytes 331784 | tf_op jit(solution)/shard_map/ppermute | solution.py:297
  131.3 4.3 %collective-permute-start.22 = (bf16[432,128]{1,0:T(8,128)(2,1)S(1)}, bf16[432,128]{1,0:T(8,128)(2,1)S(1)}, u32[]{:S(2)}, u32[]{:S(2)}) collective-permute-start(bf16[432,128]{1,0:T(8,128)(2,1)S(1)} %fusion.5), channel_id=1, source_target_pairs={{0,32},{4,36},{8,40},{12,44},{16,48},{20,52},{24,56},{28,60},{32,0... | collective-permute-start | bytes 331784 | tf_op jit(solution)/shard_map/ppermute | solution.py:297
  133.0 6.3 %collective-permute-start.23 = (bf16[432,128]{1,0:T(8,128)(2,1)S(1)}, bf16[432,128]{1,0:T(8,128)(2,1)S(1)}, u32[]{:S(2)}, u32[]{:S(2)}) collective-permute-start(bf16[432,128]{1,0:T(8,128)(2,1)S(1)} %fusion.5), channel_id=1, source_target_pairs={{0,64},{4,68},{8,72},{12,76},{16,80},{20,84},{24,88},{28,92},{32,9... | collective-permute-start | bytes 331784 | tf_op jit(solution)/shard_map/ppermute | solution.py:297
  134.3 7.9 %collective-permute-start.24 = (bf16[432,128]{1,0:T(8,128)(2,1)S(1)}, bf16[432,128]{1,0:T(8,128)(2,1)S(1)}, u32[]{:S(2)}, u32[]{:S(2)}) collective-permute-start(bf16[432,128]{1,0:T(8,128)(2,1)S(1)} %fusion.5), channel_id=1, source_target_pairs={{0,96},{4,100},{8,104},{12,108},{16,112},{20,116},{24,120},{28,124... | collective-permute-start | bytes 331784 | tf_op jit(solution)/shard_map/ppermute | solution.py:297
  142.2 11.2 %copy-start.10 = (bf16[1024,128]{1,0:T(8,128)(2,1)S(1)}, bf16[1024,128]{1,0:T(8,128)(2,1)}, u32[]{:S(2)}) copy-start(bf16[1024,128]{1,0:T(8,128)(2,1)} %copy-done.9) | copy-start | bytes 786436
  142.3 4.1 %collective-permute-start.25 = (bf16[432,128]{1,0:T(8,128)(2,1)S(1)}, bf16[432,128]{1,0:T(8,128)(2,1)S(1)}, u32[]{:S(2)}, u32[]{:S(2)}) collective-permute-start(bf16[432,128]{1,0:T(8,128)(2,1)S(1)} %fusion.11), channel_id=1, source_target_pairs={{0,8},{4,12},{8,0},{12,4},{16,24},{20,28},{24,16},{28,20},{32,40},... | collective-permute-start | bytes 331784 | tf_op jit(solution)/shard_map/ppermute | solution.py:297
  142.4 6.7 %collective-permute-start.26 = (bf16[432,128]{1,0:T(8,128)(2,1)S(1)}, bf16[432,128]{1,0:T(8,128)(2,1)S(1)}, u32[]{:S(2)}, u32[]{:S(2)}) collective-permute-start(bf16[432,128]{1,0:T(8,128)(2,1)S(1)} %fusion.11), channel_id=1, source_target_pairs={{0,16},{4,20},{8,24},{12,28},{16,0},{20,4},{24,8},{28,12},{32,48},... | collective-permute-start | bytes 331784 | tf_op jit(solution)/shard_map/ppermute | solution.py:297
  145.0 6.9 %collective-permute-start.27 = (bf16[432,128]{1,0:T(8,128)(2,1)S(1)}, bf16[432,128]{1,0:T(8,128)(2,1)S(1)}, u32[]{:S(2)}, u32[]{:S(2)}) collective-permute-start(bf16[432,128]{1,0:T(8,128)(2,1)S(1)} %fusion.11), channel_id=1, source_target_pairs={{0,24},{4,28},{8,16},{12,20},{16,8},{20,12},{24,0},{28,4},{32,56},... | collective-permute-start | bytes 331784 | tf_op jit(solution)/shard_map/ppermute | solution.py:297
  152.1 20.0 %copy-start.6 = (f32[1152,128]{1,0:T(8,128)S(1)}, f32[1152,128]{1,0:T(8,128)}, u32[]{:S(2)}) copy-start(f32[1152,128]{1,0:T(8,128)} %copy-done.5) | copy-start | bytes 1769476
  152.1 21.6 %collective-permute-start.28 = (bf16[4,432,128]{2,1,0:T(8,128)(2,1)S(1)}, bf16[4,432,128]{2,1,0:T(8,128)(2,1)S(1)}, u32[]{:S(2)}, u32[]{:S(2)}) collective-permute-start(bf16[4,432,128]{2,1,0:T(8,128)(2,1)S(1)} %get-tuple-element.29), channel_id=1, source_target_pairs={{0,4},{4,0},{8,12},{12,8},{16,20},{20,16},{24,28},{28,24},{32,36},... | collective-permute-start | bytes 1327112 | tf_op jit(solution)/shard_map/ppermute | solution.py:297
  153.4 18.7 %collective-permute-start.17 = (bf16[1024,128]{1,0:T(8,128)(2,1)S(1)}, bf16[1024,128]{1,0:T(8,128)(2,1)S(1)}, u32[]{:S(2)}, u32[]{:S(2)}) collective-permute-start(bf16[1024,128]{1,0:T(8,128)(2,1)S(1)} %copy-done.10), channel_id=1, source_target_pairs={{0,1},{1,0},{2,3},{3,2},{4,5},{5,4},{6,7},{7,6},{8,9},{9,8},{10,11... | collective-permute-start | bytes 786440 | tf_op jit(solution)/shard_map/ppermute | solution.py:293
where the time goes:
time: 177 us; the launch traced here: 176 us
  starting transfers between devices  72.5 us (41%)
  Pallas kernels  55.3 us (31%)
  waiting for transfers between devices  32.9 us (19%)
  local copies, waits for them, and re-layouts  10.2 us (6%)
  other arithmetic  3.38 us (2%)
    ppermute x16, starting transfers between devices, shifted(): lax.ppermute(value, 'space', [(i, i + steps) for i in range(initial, last)])  55.1 us
    ppermute x11, waiting for transfers between devices, xor_send(): lax.ppermute(value, 'space', [(i, i ^ bits) for i in range(lax.axis_size(...  21.9 us
    pallas_call x2, Pallas kernels, on_device(): pl.pallas_call(backward_kernel, grid=(13,), in_specs=[whole((ROWS, C)), p...  17.3 us
    pallas_call x1, Pallas kernels, on_device(): pl.pallas_call(functools.partial(forward_kernel, width=512), grid=(13,),...  15.3 us
    ppermute x11, starting transfers between devices, xor_send(): lax.ppermute(value, 'space', [(i, i ^ bits) for i in range(lax.axis_size(...  14.8 us
    pallas_call x1, Pallas kernels, on_device(): pl.pallas_call(weight_kernel, grid=(13,), in_specs=[pl.BlockSpec((2 * C,...  9.77 us
    unnamed x38, local copies, waits for them, and re-layouts  7.21 us
    ppermute x16, waiting for transfers between devices, shifted(): lax.ppermute(value, 'space', [(i, i + steps) for i in range(initial, last)])  5.97 us
  transfers between devices with their start and end apart: 29, of which 12 were waited for; matrix products, arithmetic and copies ran while one was open for 1% of the time, Pallas kernels for 25%

commit v1 on v0

--- a/solution.py
+++ b/solution.py
@@ -101,7 +101,46 @@
     return spread(jnp.concatenate(pieces, 0), count)
 
 
-def start_kernel(x_ref, rr_ref, rc_ref, sm_ref, w_ref, part_ref, face_g_ref, corner_g_ref):
+def number_of(step_x, step_y):
+    return DIRECTIONS.index((step_x, step_y))
+
+
+def pack_sides(lists, orient, sides, xa_ref, xb_ref, ya_ref, yb_ref):
+    x_odd, y_odd = sides[0] == 1, sides[1] == 1
+
+    def x_side(side):
+        picked = [(orient * side, 0), (orient * side, -orient), (orient * side, orient)]
+        return jnp.concatenate([lists[number_of(*d)] for d in picked], 0)
+
+    plus, minus = x_side(1), x_side(-1)
+    xa_ref[...] = jnp.where(x_odd, minus, plus)
+    xb_ref[...] = jnp.where(x_odd, plus, minus)
+    plus, minus = lists[number_of(0, orient)], lists[number_of(0, -orient)]
+    ya_ref[...] = jnp.where(y_odd, minus, plus)
+    yb_ref[...] = jnp.where(y_odd, plus, minus)
+
+
+def unpack_sides(orient, sides, xa, xb, ya, yb):
+    x_odd, y_odd = sides[0] == 1, sides[1] == 1
+
+    def of_side(side, odd, a, b):
+        return jnp.where(odd, b, a) if side == 1 else jnp.where(odd, a, b)
+
+    lists = []
+    for step_x, step_y in DIRECTIONS:
+        if step_y == 0:
+            lists.append(of_side(-orient * step_x, x_odd, xa[:CAP], xb[:CAP]))
+        elif step_x == 0:
+            lists.append(of_side(-orient * step_y, y_odd, ya[:CAP], yb[:CAP]))
+        else:
+            first = of_side(-orient * step_y, y_odd, ya[CAP : CAP + TZ], yb[CAP : CAP + TZ])
+            second = of_side(-orient * step_y, y_odd, ya[CAP + TZ :], yb[CAP + TZ :])
+            lists.append(of_side(-orient * step_x, x_odd, first, second))
+    return lists
+
+
+def start_kernel(side_ref, x_ref, rr_ref, rc_ref, sm_ref, w_ref, xa_ref, xb_ref, ya_ref, yb_ref, face_g_ref, corner_g_ref):
+    lists = [None] * 8
     x_t = x_ref[...].astype(F32).T.astype(BF)
     selector = hot(rr_ref[...], ROWS)
     listed = dot(x_t, selector).astype(BF)
@@ -119,7 +158,7 @@
         face_g_ref[place] = gathered
         weight = jnp.concatenate([w_ref[offset] for offset in picked], 0)
         total = dot(weight, gathered, ((0,), (0,)))
-        part_ref[start : start + length, :] = total.T.astype(BF)
+        lists[number] = total.T.astype(BF)
     column = corner_column(rc_ref, 4 * TZ)
     source = jnp.concatenate(
         [listed[:, SPANS[7 - n][0] : SPANS[7 - n][0] + TZ] for n in CORNERS], 1
@@ -139,8 +178,8 @@
     corner_g_ref[...] = masked
     total = dot(jnp.concatenate(weights, 0), masked, ((0,), (0,))).T.astype(BF)
     for place, number in enumerate(CORNERS):
-        start, length = SPANS[number]
-        part_ref[start : start + length, :] = total[place * TZ : (place + 1) * TZ, :]
+        lists[number] = total[place * TZ : (place + 1) * TZ, :]
+    pack_sides(lists, 1, (side_ref[0], side_ref[1]), xa_ref, xb_ref, ya_ref, yb_ref)
 
 
 def pair_of(step):
@@ -171,38 +210,44 @@
         pre_ref[...] = total[...].T
 
 
-def activate_kernel(pre_ref, part_ref, rr_ref, cot_ref, pair_ref, act_ref, grad_ref, out_ref):
+def activate_kernel(
+    side_ref, pre_ref, ixa_ref, ixb_ref, iya_ref, iyb_ref, rr_ref, cot_ref, pair_ref,
+    act_ref, grad_ref, xa_ref, xb_ref, ya_ref, yb_ref,
+):
+    sides = (side_ref[0], side_ref[1])
+    arrived = unpack_sides(1, sides, ixa_ref[...], ixb_ref[...], iya_ref[...], iyb_ref[...])
     selector = hot(rr_ref[...], ROWS)
-    pre = pre_ref[...] + dot(selector, part_ref[...])
+    pre = pre_ref[...] + dot(selector, jnp.concatenate(arrived, 0))
     gate = 1.0 / (1.0 + jnp.exp(-pre))
     act_ref[...] = (pre * gate).astype(BF)
     upstream = cot_ref[...].astype(F32) + pair_ref[...].astype(F32)
     grad = upstream * gate * (1.0 + pre * (1.0 - gate))
     grad_ref[...] = grad.astype(BF)
-    grad_t = grad.T.astype(BF)
-    out_ref[...] = dot(grad_t, selector).T.astype(BF)
+    listed = dot(grad.T.astype(BF), selector).T.astype(BF)
+    lists = [listed[start : start + length] for start, length in SPANS]
+    pack_sides(lists, -1, sides, xa_ref, xb_ref, ya_ref, yb_ref)
 
 
 def weight_kernel(g_ref, grad_ref, x_ref, dw_ref):
     step = pl.program_id(0)
-    first, second = pair_of(step)
 
     @pl.when(step == 0)
     def _():
         dw_ref[13] = dot(x_ref[...], grad_ref[...], ((0,), (0,)))
 
-    both = dot(g_ref[...], grad_ref[...])
-    dw_ref[first] = both[:C]
-    dw_ref[second] = both[C:]
-
-
-def return_kernel(back_ref, rc_ref, sm_ref, w_ref, face_g_ref, corner_g_ref, dw_in_ref, dw_ref, placed_ref, total):
+    total = dot(g_ref[...], grad_ref[...])
+    dw_ref[pl.ds(14 * step, 13)] = total.reshape(13, C, C)
+
+
+def return_kernel(side_ref, ixa_ref, ixb_ref, iya_ref, iyb_ref, rc_ref, sm_ref, w_ref, face_g_ref, corner_g_ref, dw_in_ref, dw_ref, placed_ref, total):
     total[...] = dw_in_ref[...]
+    sides = (side_ref[0], side_ref[1])
+    returned = unpack_sides(-1, sides, ixa_ref[...], ixb_ref[...], iya_ref[...], iyb_ref[...])
     for place, number in enumerate(FACES):
         start, length = SPANS[number]
         other, _ = SPANS[7 - number]
         column = spread(rc_ref[other : other + length, :], length)
-        back = back_ref[start : start + length, :]
+        back = returned[number]
         picked = toward(*DIRECTIONS[number])
         pieces = []
         for offset in picked:
@@ -215,7 +260,7 @@
         for index, offset in enumerate(picked):
             total[offset] += kernel_part[index * C : (index + 1) * C, :]
     column = corner_column(rc_ref, 4 * TZ)
-    back = jnp.concatenate([back_ref[SPANS[n][0] : SPANS[n][0] + TZ, :] for n in CORNERS], 0)
+    back = jnp.concatenate([returned[n] for n in CORNERS], 0)
     kernel_part = dot(corner_g_ref[...], back)
     pieces = []
     weights = []
@@ -273,20 +318,32 @@
     return pl.BlockSpec(dims, lambda *ids: (0,) * len(dims))
 
 
-def shifted(value, steps):
-    count = lax.axis_size("space")
-    initial, last = (max(0, -steps), min(count, count - steps))
-    return lax.ppermute(value, "space", [(i, i + steps) for i in range(initial, last)])
-
-
-def exchange(lists, orient):
-    received = []
-    for number, (step_x, step_y) in enumerate(DIRECTIONS):
-        start, length = SPANS[number]
-        received.append(
-            shifted(lists[start : start + length], orient * (step_x + TILES_X * step_y))
-        )
-    return jnp.concatenate(received, 0)
+def pairing(axis, which):
+    pairs = []
+    for tile in range(lax.axis_size("space")):
+        at_x, at_y = tile % TILES_X, tile // TILES_X
+        tiles_y = lax.axis_size("space") // TILES_X
+        if axis == "x":
+            move = 1 if (at_x + which) % 2 == 0 else -1
+            at_x = (at_x + move) % TILES_X
+        else:
+            move = 1 if (at_y + which) % 2 == 0 else -1
+            at_y = (at_y + move) % tiles_y
+        pairs.append((tile, at_y * TILES_X + at_x))
+    return pairs
+
+
+def exchange_x(xa, xb):
+    return [lax.ppermute(v, "space", pairing("x", n)) for n, v in enumerate((xa, xb))]
+
+
+def exchange_y(ya, yb, xa, xb, sides):
+    sent = []
+    for which, own in enumerate((ya, yb)):
+        down = sides[1] != which
+        corners = [jnp.where(down, v[CAP : CAP + TZ], v[CAP + TZ :]) for v in (xa, xb)]
+        sent.append(jnp.concatenate([own] + corners, 0))
+    return [lax.ppermute(v, "space", pairing("y", n)) for n, v in enumerate(sent)]
 
 
 def swapped(array):
@@ -304,26 +361,16 @@
     return total.astype(BF)
 
 
-def reduce_weights(dw):
-    me = lax.axis_index("space")
-    core, x_at = me % 2, me // 2 % 4
-    halves = dw.reshape(2, -1, C)
-    pick = functools.partial(lax.dynamic_index_in_dim, axis=0, keepdims=False)
-    half = add_up([pick(halves, core), xor_send(pick(halves, 1 - core), 1)])
-    quarters = half.reshape(4, -1, C)
-    got = [pick(quarters, x_at)]
-    for bits in (1, 2, 3):
-        got.append(xor_send(pick(quarters, x_at ^ bits), bits * 2))
-    quarter = add_up(got)
-    got = [xor_send(quarter, bits * 8) for bits in (1, 2, 3)]
-    z_at = me // 8
-    stacked = jnp.stack([quarter] + got)
-    quarter = add_up([pick(stacked, z_at ^ index) for index in range(4)])
-    got = jnp.stack([quarter] + [xor_send(quarter, bits * 2) for bits in (1, 2, 3)])
-    half = jnp.stack([pick(got, x_at ^ index) for index in range(4)])
-    got = jnp.stack([half, xor_send(half, 1)])
-    both = jnp.stack([pick(got, core), pick(got, 1 - core)])
-    return both.reshape(dw.shape).astype(F32)
+def pick(array, index):
+    return lax.dynamic_index_in_dim(array, index, 0, False)
+
+
+def cost(flops, data):
+    return pl.CostEstimate(flops=int(flops), bytes_accessed=int(data), transcendentals=0)
+
+
+def tie(value, other):
+    return lax.optimization_barrier((value, other))[0]
 
 
 def on_device(features, weights, cotangent, local_map, send_map, recv_map):
@@ -334,14 +381,22 @@
     sm = send_map.T.reshape(27, 1, HALO)
     rr = recv_map.reshape(1, HALO)
     rc = recv_map.reshape(HALO, 1)
-    part, face_g, corner_g = pl.pallas_call(
+    me = lax.axis_index("space")
+    sides = jnp.stack([me % 2, me // TILES_X % 2]).astype(jnp.int32)
+    smem = pl.BlockSpec(memory_space=pltpu.SMEM)
+    vmem = pl.BlockSpec(memory_space=pltpu.VMEM)
+    out_lists = [shape((CAP + 2 * TZ, C), BF)] * 2 + [shape((CAP, C), BF)] * 2
+    xa, xb, ya, yb, face_g, corner_g = pl.pallas_call(
         start_kernel,
-        out_shape=[shape((HALO, C), BF), shape((4, 9 * C, CAP), BF), shape((12 * C, 4 * TZ), BF)],
+        in_specs=[smem] + [vmem] * 5,
+        out_shape=out_lists + [shape((4, 9 * C, CAP), BF), shape((12 * C, 4 * TZ), BF)],
         compiler_params=PARAMS,
+        cost_estimate=cost(2e9, 4e6),
         name="start",
-    )(x, rr, rc, sm, w)
-    arrived = exchange(part, 1)
+    )(sides, x, rr, rc, sm, w)
     cot_pair = swapped(cot)
+    in_x = exchange_x(xa, xb)
+    in_y = exchange_y(ya, yb, *in_x, sides)
     gathered, pre = pl.pallas_call(
         functools.partial(forward_kernel, width=512),
         grid=(13,),
@@ -350,56 +405,84 @@
         out_shape=[shape((26 * C, ROWS), BF), shape((ROWS, C), F32)],
         scratch_shapes=[pltpu.VMEM((C, ROWS), BF), pltpu.VMEM((C, ROWS), F32)],
         compiler_params=PARAMS,
+        cost_estimate=cost(15e9, 9e6),
         name="forward",
     )(x, lm, w)
-    act, grad, outgoing = pl.pallas_call(
+    act, grad, xa, xb, ya, yb = pl.pallas_call(
         activate_kernel,
-        out_shape=[shape((ROWS, C), BF), shape((ROWS, C), BF), shape((HALO, C), BF)],
+        in_specs=[smem] + [vmem] * 8,
+        out_shape=[shape((ROWS, C), BF)] * 2 + out_lists,
         compiler_params=PARAMS,
+        cost_estimate=cost(1.5e9, 3e6),
         name="activate",
-    )(pre, arrived, rr, cot, cot_pair)
-    returned = exchange(outgoing, -1)
-    act_pair = swapped(act)
+    )(sides, pre, *in_x, *in_y, rr, cot, cot_pair)
+    in_x = exchange_x(xa, xb)
+    in_y = exchange_y(ya, yb, *in_x, sides)
     dw_local = pl.pallas_call(
         weight_kernel,
-        grid=(13,),
-        in_specs=[pl.BlockSpec((2 * C, ROWS), lambda j: (j, 0)), whole((ROWS, C)), whole((ROWS, C))],
+        grid=(2,),
+        in_specs=[pl.BlockSpec((13 * C, ROWS), lambda j: (j, 0)), whole((ROWS, C)), whole((ROWS, C))],
         out_specs=whole((27, C, C)),
         out_shape=shape((27, C, C), F32),
         compiler_params=PARAMS,
+        cost_estimate=cost(4e9, 9e6),
         name="weight",
     )(gathered, grad, x)
+
+    size = ROWS // 4
+
+    def backward(index, grad):
+        return pl.pallas_call(
+            backward_kernel,
+            grid=(13,),
+            in_specs=[whole((ROWS, C)), pl.BlockSpec((size, C), lambda j: (index, 0)),
+                      pl.BlockSpec((27, 1, size), lambda j: (0, 0, index)), whole((27, C, C))],
+            out_specs=whole((size, C)),
+            out_shape=shape((size, C), F32),
+            scratch_shapes=[pltpu.VMEM((C, ROWS), BF), pltpu.VMEM((C, size), F32)],
+            compiler_params=PARAMS,
+            cost_estimate=cost(5e9, 2e6),
+            name="backward",
+        )(grad, grad, lm, w)
+
+    locals_ = [backward(0, tie(grad, dw_local))]
     dw, placed = pl.pallas_call(
         return_kernel,
+        in_specs=[smem] + [vmem] * 10,
         out_shape=[shape((27, C, C), BF), shape((HALO, C), F32)],
         scratch_shapes=[pltpu.VMEM((27, C, C), F32)],
         compiler_params=PARAMS,
+        cost_estimate=cost(3e9, 4e6),
         name="returning",
-    )(returned, rc, sm, w, face_g, corner_g, dw_local)
-    weight_grad = reduce_weights(dw)
-    parts = []
-    size = ROWS // 2
-    for begin in range(0, ROWS, size):
-        parts.append(
-            pl.pallas_call(
-                backward_kernel,
-                grid=(13,),
-                in_specs=[whole((ROWS, C)), pl.BlockSpec((size, C), lambda j, at=begin // size: (at, 0)),
-                          pl.BlockSpec((27, 1, size), lambda j, at=begin // size: (0, 0, at)), whole((27, C, C))],
-                out_specs=whole((size, C)),
-                out_shape=shape((size, C), F32),
-                scratch_shapes=[pltpu.VMEM((C, ROWS), BF), pltpu.VMEM((C, size), F32)],
-                compiler_params=PARAMS,
-                name="backward",
-            )(grad, grad, lm, w)
-        )
-    local = jnp.concatenate(parts, 0)
+    )(sides, *in_x, *in_y, rc, sm, w, face_g, corner_g, tie(dw_local, locals_[0]))
+    act_pair = swapped(tie(act, dw))
+
+    core, x_at, z_at = me % 2, me // 2 % 4, me // 8
+    halves = dw.reshape(2, -1, C)
+    got = xor_send(pick(halves, 1 - core), 1)
+    locals_.append(backward(1, tie(grad, dw)))
+    half = add_up([pick(halves, core), tie(got, locals_[1])])
+    quarters = half.reshape(4, -1, C)
+    got = [xor_send(pick(quarters, x_at ^ bits), bits * 2) for bits in (1, 2, 3)]
+    locals_.append(backward(2, tie(grad, half)))
+    quarter = add_up([pick(quarters, x_at)] + [tie(v, locals_[2]) for v in got])
+    got = [xor_send(quarter, bits * 8) for bits in (1, 2, 3)]
+    locals_.append(backward(3, tie(grad, quarter)))
+    stacked = jnp.stack([quarter] + [tie(v, locals_[3]) for v in got])
+    quarter = add_up([pick(stacked, z_at ^ index) for index in range(4)])
+    got = jnp.stack([quarter] + [xor_send(quarter, bits * 2) for bits in (1, 2, 3)])
+    local = tie(jnp.concatenate(locals_, 0), quarter)
     mixed, input_grad = pl.pallas_call(
         final_kernel,
         out_shape=[shape((ROWS, C), BF), shape((ROWS, C), BF)],
         compiler_params=PARAMS,
+        cost_estimate=cost(1e9, 3e6),
         name="final",
     )(local, placed, rr, act, act_pair)
+    half = jnp.stack([pick(got, x_at ^ index) for index in range(4)])
+    got = jnp.stack([half, xor_send(half, 1)])
+    both = jnp.stack([pick(got, core), pick(got, 1 - core)])
+    weight_grad = both.reshape(dw.shape).astype(F32)
     return (mixed[None], input_grad[None], weight_grad[None])
 
 

time: 177 us -> 120 us (0.68)
  starting transfers between devices: 72.5 us -> 31.2 us
  waiting for transfers between devices: 32.9 us -> 17.5 us
  Pallas kernels: 55.3 us -> 59.8 us
  local copies, waits for them, and re-layouts: 10.2 us -> 7.17 us
    ppermute x16 -> x8, starting transfers between devices: 55.1 us -> 13.6 us  [the longest x4 9.81 us: exchange_y(): lax.ppermute(v, 'space', pairing('y', n))]
    ppermute x11, waiting for transfers between devices: 21.9 us -> 5.95 us  [xor_send(): lax.ppermute(value, 'space', [(i, i ^ bits) for i in range(lax.axis_size(...]
    pallas_call x6 -> x8, Pallas kernels: 38.4 us -> 42.8 us  [the longest x4 26.1 us: backward(): pl.pallas_call(backward_kernel, grid=(13,), in_specs=[whole((ROWS, C)), p...]
    unnamed x38 -> x18, local copies, waits for them, and re-layouts: 7.21 us -> 4.37 us
    ppermute x16 -> x8, waiting for transfers between devices: 5.97 us -> 5.04 us  [the longest x4 5.03 us: exchange_x(): lax.ppermute(v, 'space', pairing('x', n))]
  transfers between devices with their start and end apart: 29 -> 21, of which waited for: 12 -> 6; matrix products, arithmetic and copies ran while one was open for 1% -> 1% of each run, Pallas kernels for 25% -> 40%
where the time goes in v1:
time: 120 us
  Pallas kernels  59.8 us (50%)
  starting transfers between devices  31.2 us (26%)
  waiting for transfers between devices  17.5 us (15%)
  local copies, waits for them, and re-layouts  7.17 us (6%)
  other arithmetic  3.14 us (3%)
    pallas_call x4, Pallas kernels, backward(): pl.pallas_call(backward_kernel, grid=(13,), in_specs=[whole((ROWS, C)), p...  26.1 us
    pallas_call x1, Pallas kernels, on_device(): pl.pallas_call(functools.partial(forward_kernel, width=512), grid=(13,),...  15.3 us
    ppermute x11, starting transfers between devices, xor_send(): lax.ppermute(value, 'space', [(i, i ^ bits) for i in range(lax.axis_size(...  15 us
    ppermute x4, starting transfers between devices, exchange_y(): lax.ppermute(v, 'space', pairing('y', n))  9.81 us
    ppermute x2, waiting for transfers between devices, swapped(): lax.ppermute(array, 'segment', [(i, i ^ 1) for i in range(lax.axis_size('...  6.51 us
    ppermute x11, waiting for transfers between devices, xor_send(): lax.ppermute(value, 'space', [(i, i ^ bits) for i in range(lax.axis_size(...  5.95 us
    pallas_call x1, Pallas kernels, on_device(): pl.pallas_call(return_kernel, in_specs=[smem] + [vmem] * 10, out_shape=[s...  5.07 us
    ppermute x4, waiting for transfers between devices, exchange_x(): lax.ppermute(v, 'space', pairing('x', n))  5.03 us
  transfers between devices with their start and end apart: 21, of which 6 were waited for; matrix products, arithmetic and copies ran while one was open for 1% of the time, Pallas kernels for 40%

profile of v1, /device:TPU:1, one launch (start us, length us, event | category | flops | bytes accessed | tf_op | source)
XLA Modules:
  0.0 119.7 jit_solution(13802466463873073840)
XLA Ops:
  0.7 0.7 reshape.50.rr_ref
  1.4 0.9 reshape.58.rc_ref
  2.3 1.0 reshape.52.sm_ref
  3.3 0.1 pad_add_fusion.side_ref
  3.4 1.2 copy-done
  4.5 0.9 copy-done.3
  5.5 4.7 %start.1 = (bf16[320,128]{1,0:T(8,128)(2,1)S(1)}, bf16[320,128]{1,0:T(8,128)(2,1)S(1)}, bf16[256,128]{1,0:T(8,128)(2,1)S(1)}, bf16[256,128]{1,0:T(8,128)(2,1)S(1...) custom-call(s32[2]{0:T(128)S(1)} %pad_add_fusion.side_ref, bf16[1024,128]{1,0:T(8,128)(2,1)S(1)} %bitcast.50, ...), custom_call_target="tpu_custom_call" | custom-call | flops 2000000000 | bytes 4000000 | tf_op jit(solution)/shard_map/start/pallas_call | solution.py:389
  10.2 1.5 %copy-done.5 = bf16[4,1152,256]{2,1,0:T(8,128)(2,1)} copy-done((bf16[4,1152,256]{2,1,0:T(8,128)(2,1)}, bf16[4,1152,256]{2,1,0:T(8,128)(2,1)S(1)}, u32[]{:S(2)}) %copy-start.5) | copy-done | bytes 2359320
  11.7 0.7 copy-done.6
  12.4 1.4 %collective-permute-start = (bf16[320,128]{1,0:T(8,128)(2,1)S(1)}, bf16[320,128]{1,0:T(8,128)(2,1)S(1)}, u32[]{:S(2)}, u32[]{:S(2)}) collective-permute-start(bf16[320,128]{1,0:T(8,128)(2,1)S(1)} %get-tuple-element.36), channel_id=1, source_target_pairs={{0,4},{4,0},{8,12},{12,8},{16,20},{20,16},{24,28},{28,24},{32,36},... | collective-permute-start | bytes 245768 | tf_op jit(solution)/shard_map/ppermute | solution.py:337
  13.9 1.2 collective-permute-start.1
  15.1 1.3 %collective-permute-start.4 = (bf16[1024,128]{1,0:T(8,128)(2,1)S(1)}, bf16[1024,128]{1,0:T(8,128)(2,1)S(1)}, u32[]{:S(2)}, u32[]{:S(2)}) collective-permute-start(bf16[1024,128]{1,0:T(8,128)(2,1)S(1)} %bitcast.48), channel_id=1, source_target_pairs={{0,1},{1,0},{2,3},{3,2},{4,5},{5,4},{6,7},{7,6},{8,9},{9,8},{10,11... | collective-permute-start | bytes 786440 | tf_op jit(solution)/shard_map/ppermute | solution.py:350
  16.4 0.1 reshape.49.lm_ref
  16.4 0.0 collective-permute-done.ixa_ref
  16.5 1.5 %collective-permute-done.1.ixb_ref = bf16[320,128]{1,0:T(8,128)(2,1)S(1)} collective-permute-done((bf16[320,128]{1,0:T(8,128)(2,1)S(1)}, bf16[320,128]{1,0:T(8,128)(2,1)S(1)}, u32[]{:S(2)}, u32[]{:S(2)}) %collective-permute-start.1) | collective-permute-done | bytes 81952 | tf_op jit(solution)/shard_map/ppermute | solution.py:337
  17.9 6.4 %collective-permute-start.3 = (bf16[320,128]{1,0:T(8,128)(2,1)S(1)}, bf16[320,128]{1,0:T(8,128)(2,1)S(1)}, u32[]{:S(2)}, u32[]{:S(2)}) collective-permute-start(bf16[320,128]{1,0:T(8,128)(2,1)S(1)} %pad_maximum_fusion.6), channel_id=1, source_target_pairs={{0,112},{4,116},{8,120},{12,124},{16,32},{20,36},{24,40},{28,44},{... | collective-permute-start | bytes 245768 | tf_op jit(solution)/shard_map/ppermute | solution.py:346
  24.3 0.6 pad_maximum_fusion.5
  25.0 0.0 collective-permute-start.2
  25.0 15.3 %forward.1 = (bf16[3328,1024]{1,0:T(8,128)(2,1)}, f32[1024,128]{1,0:T(8,128)S(1)}) custom-call(bf16[1024,128]{1,0:T(8,128)(2,1)S(1)} %bitcast.51, s32[27,1,1024]{2,1,0:T(1,128)S(1)} %reshape.49.lm_ref, bf16[27,128,128]{2,1,0:T(8,128)(2,1)S(1)} %bitcast.42), custom_call_target="tpu_custom_call" | custom-call | flops 15000000512 | bytes 9000000 | tf_op jit(solution)/shard_map/forward/pallas_call | solution.py:400
  40.3 0.0 collective-permute-done.4.pair_ref
  40.3 2.5 %activate.1 = (bf16[1024,128]{1,0:T(8,128)(2,1)S(1)}, bf16[1024,128]{1,0:T(8,128)(2,1)S(1)}, bf16[320,128]{1,0:T(8,128)(2,1)S(1)}, bf16[320,128]{1,0:T(8,128)(2,...) custom-call(s32[2]{0:T(128)S(1)} %pad_add_fusion.side_ref, ...), custom_call_target="tpu_custom_call" | custom-call | flops 1500000000 | bytes 3000000 | tf_op jit(solution)/shard_map/activate/pallas_call | solution.py:411
  42.8 0.4 collective-permute-start.5
  43.2 4.4 %weight.1.dw_in_ref = f32[27,128,128]{2,1,0:T(8,128)S(1)} custom-call(bf16[3328,1024]{1,0:T(8,128)(2,1)} %get-tuple-element.41.g_ref, bf16[1024,128]{1,0:T(8,128)(2,1)S(1)} %get-tuple-element.57.grad_ref.own_ref, bf16[1024,128]{1,0:T(8,128)(2,1)S(1)} %bitcast.52), custom_call_target="tpu_custom_call" | custom-call | flops 4000000000 | bytes 9000000 | tf_op jit(solution)/shard_map/weight/pallas_call | solution.py:421
  47.6 0.8 collective-permute-start.6
  48.4 3.6 %collective-permute-done.6.ixb_ref = bf16[320,128]{1,0:T(8,128)(2,1)S(1)} collective-permute-done((bf16[320,128]{1,0:T(8,128)(2,1)S(1)}, bf16[320,128]{1,0:T(8,128)(2,1)S(1)}, u32[]{:S(2)}, u32[]{:S(2)}) %collective-permute-start.6) | collective-permute-done | bytes 81952 | tf_op jit(solution)/shard_map/ppermute | solution.py:337
  52.0 3.0 %collective-permute-start.8 = (bf16[320,128]{1,0:T(8,128)(2,1)S(1)}, bf16[320,128]{1,0:T(8,128)(2,1)S(1)}, u32[]{:S(2)}, u32[]{:S(2)}) collective-permute-start(bf16[320,128]{1,0:T(8,128)(2,1)S(1)} %pad_maximum_fusion.8), channel_id=1, source_target_pairs={{0,112},{4,116},{8,120},{12,124},{16,32},{20,36},{24,40},{28,44},{... | collective-permute-start | bytes 245768 | tf_op jit(solution)/shard_map/ppermute | solution.py:346
  54.9 0.4 collective-permute-start.7
  55.4 6.6 %backward.4 = f32[256,128]{1,0:T(8,128)S(1)} custom-call(bf16[1024,128]{1,0:T(8,128)(2,1)S(1)} %get-tuple-element.57.grad_ref.own_ref, bf16[1024,128]{1,0:T(8,128)(2,1)S(1)} %get-tuple-element.57.grad_ref.own_ref, s32[27,1,1024]{2,1,0:T(1,128)S(1)} %reshape.49.lm_ref, bf16[27,128,128]{2,1,0:T(8,128)(2,1)S(1)} %bitcast.43), custom_call_target="tpu_custom_call" | custom-call | flops 5000000000 | bytes 2000000 | tf_op jit(solution)/shard_map/backward/pallas_call | solution.py:435
  62.0 0.0 collective-permute-done.7.iya_ref
  62.0 5.1 %returning.1 = (bf16[27,128,128]{2,1,0:T(8,128)(2,1)S(1)}, f32[1152,128]{1,0:T(8,128)S(1)}) custom-call(s32[2]{0:T(128)S(1)} %pad_add_fusion.side_ref, bf16[320,128]{1,0:T(8,128)(2,1)S(1)} %collective-permute-done.5.ixa_ref, bf16[320,128]{1,0:T(8,128)(2,1)S(1)} %collective-permute-done.6.ixb_ref, bf16[320,128]{1,0:T(8,128)(2,1)S(1)} %collective-permute-done.7.iya_ref, ...), custom_call_target="tpu_custom_call" | custom-call | flops 3000000000 | bytes 4000000 | tf_op jit(solution)/shard_map/returning/pallas_call | solution.py:449
  67.1 0.3 collective-permute-start.9
  67.5 6.5 %backward.5 = f32[256,128]{1,0:T(8,128)S(1)} custom-call(bf16[1024,128]{1,0:T(8,128)(2,1)S(1)} %get-tuple-element.57.grad_ref.own_ref, bf16[1024,128]{1,0:T(8,128)(2,1)S(1)} %get-tuple-element.57.grad_ref.own_ref, s32[27,1,1024]{2,1,0:T(1,128)S(1)} %reshape.49.lm_ref, bf16[27,128,128]{2,1,0:T(8,128)(2,1)S(1)} %bitcast.45), custom_call_target="tpu_custom_call" | custom-call | flops 5000000000 | bytes 2000000 | tf_op jit(solution)/shard_map/backward/pallas_call | solution.py:435
  74.0 0.0 collective-permute-done.9
  74.0 0.1 fusion
  74.1 1.6 %collective-permute-start.10 = (bf16[432,128]{1,0:T(8,128)(2,1)S(1)}, bf16[432,128]{1,0:T(8,128)(2,1)S(1)}, u32[]{:S(2)}, u32[]{:S(2)}) collective-permute-start(bf16[432,128]{1,0:T(8,128)(2,1)S(1)} %get-tuple-element.75), channel_id=1, source_target_pairs={{0,8},{4,12},{8,0},{12,4},{16,24},{20,28},{24,16},{28,20},{32,40},... | collective-permute-start | bytes 331784 | tf_op jit(solution)/shard_map/ppermute | solution.py:354
  75.7 2.8 %collective-permute-start.11 = (bf16[432,128]{1,0:T(8,128)(2,1)S(1)}, bf16[432,128]{1,0:T(8,128)(2,1)S(1)}, u32[]{:S(2)}, u32[]{:S(2)}) collective-permute-start(bf16[432,128]{1,0:T(8,128)(2,1)S(1)} %get-tuple-element.77), channel_id=1, source_target_pairs={{0,16},{4,20},{8,24},{12,28},{16,0},{20,4},{24,8},{28,12},{32,48},... | collective-permute-start | bytes 331784 | tf_op jit(solution)/shard_map/ppermute | solution.py:354
  78.6 6.5 %backward.6 = f32[256,128]{1,0:T(8,128)S(1)} custom-call(bf16[1024,128]{1,0:T(8,128)(2,1)S(1)} %get-tuple-element.57.grad_ref.own_ref, bf16[1024,128]{1,0:T(8,128)(2,1)S(1)} %get-tuple-element.57.grad_ref.own_ref, s32[27,1,1024]{2,1,0:T(1,128)S(1)} %reshape.49.lm_ref, bf16[27,128,128]{2,1,0:T(8,128)(2,1)S(1)} %bitcast.46), custom_call_target="tpu_custom_call" | custom-call | flops 5000000000 | bytes 2000000 | tf_op jit(solution)/shard_map/backward/pallas_call | solution.py:435
  85.1 0.0 collective-permute-done.11
  85.1 1.5 %collective-permute-done.12 = bf16[432,128]{1,0:T(8,128)(2,1)S(1)} collective-permute-done((bf16[432,128]{1,0:T(8,128)(2,1)S(1)}, bf16[432,128]{1,0:T(8,128)(2,1)S(1)}, u32[]{:S(2)}, u32[]{:S(2)}) %collective-permute-start.12) | collective-permute-done | bytes 110624 | tf_op jit(solution)/shard_map/ppermute | solution.py:354
  86.6 0.1 fusion.5
  86.6 1.5 %collective-permute-start.13 = (bf16[432,128]{1,0:T(8,128)(2,1)S(1)}, bf16[432,128]{1,0:T(8,128)(2,1)S(1)}, u32[]{:S(2)}, u32[]{:S(2)}) collective-permute-start(bf16[432,128]{1,0:T(8,128)(2,1)S(1)} %fusion.5), channel_id=1, source_target_pairs={{0,32},{4,36},{8,40},{12,44},{16,48},{20,52},{24,56},{28,60},{32,0... | collective-permute-start | bytes 331784 | tf_op jit(solution)/shard_map/ppermute | solution.py:354
  88.2 0.6 collective-permute-start.14
  88.8 1.9 %collective-permute-start.15 = (bf16[432,128]{1,0:T(8,128)(2,1)S(1)}, bf16[432,128]{1,0:T(8,128)(2,1)S(1)}, u32[]{:S(2)}, u32[]{:S(2)}) collective-permute-start(bf16[432,128]{1,0:T(8,128)(2,1)S(1)} %fusion.5), channel_id=1, source_target_pairs={{0,96},{4,100},{8,104},{12,108},{16,112},{20,116},{24,120},{28,124... | collective-permute-start | bytes 331784 | tf_op jit(solution)/shard_map/ppermute | solution.py:354
  90.7 6.6 %backward.7 = f32[256,128]{1,0:T(8,128)S(1)} custom-call(bf16[1024,128]{1,0:T(8,128)(2,1)S(1)} %get-tuple-element.57.grad_ref.own_ref, bf16[1024,128]{1,0:T(8,128)(2,1)S(1)} %get-tuple-element.57.grad_ref.own_ref, s32[27,1,1024]{2,1,0:T(1,128)S(1)} %reshape.49.lm_ref, bf16[27,128,128]{2,1,0:T(8,128)(2,1)S(1)} %bitcast.47), custom_call_target="tpu_custom_call" | custom-call | flops 5000000000 | bytes 2000000 | tf_op jit(solution)/shard_map/backward/pallas_call | solution.py:435
  97.3 0.0 collective-permute-done.13
  97.3 0.0 collective-permute-done.15
  97.3 0.1 pad_maximum_fusion.2
  97.4 0.1 fusion.7
  97.4 0.1 collective-permute-start.17
  97.5 2.3 %collective-permute-start.18 = (bf16[432,128]{1,0:T(8,128)(2,1)S(1)}, bf16[432,128]{1,0:T(8,128)(2,1)S(1)}, u32[]{:S(2)}, u32[]{:S(2)}) collective-permute-start(bf16[432,128]{1,0:T(8,128)(2,1)S(1)} %fusion.7), channel_id=1, source_target_pairs={{0,16},{4,20},{8,24},{12,28},{16,0},{20,4},{24,8},{28,12},{32,48},... | collective-permute-start | bytes 331784 | tf_op jit(solution)/shard_map/ppermute | solution.py:354
  99.9 1.5 %collective-permute-start.19 = (bf16[432,128]{1,0:T(8,128)(2,1)S(1)}, bf16[432,128]{1,0:T(8,128)(2,1)S(1)}, u32[]{:S(2)}, u32[]{:S(2)}) collective-permute-start(bf16[432,128]{1,0:T(8,128)(2,1)S(1)} %fusion.7), channel_id=1, source_target_pairs={{0,24},{4,28},{8,16},{12,20},{16,8},{20,12},{24,0},{28,4},{32,56},... | collective-permute-start | bytes 331784 | tf_op jit(solution)/shard_map/ppermute | solution.py:354
  101.4 0.1 add_convert_fusion
  101.5 0.0 collective-permute-done.17
  101.5 1.9 %collective-permute-done.18 = bf16[432,128]{1,0:T(8,128)(2,1)S(1)} collective-permute-done((bf16[432,128]{1,0:T(8,128)(2,1)S(1)}, bf16[432,128]{1,0:T(8,128)(2,1)S(1)}, u32[]{:S(2)}, u32[]{:S(2)}) %collective-permute-start.18) | collective-permute-done | bytes 110624 | tf_op jit(solution)/shard_map/ppermute | solution.py:354
  103.4 2.5 %collective-permute-done.19 = bf16[432,128]{1,0:T(8,128)(2,1)S(1)} collective-permute-done((bf16[432,128]{1,0:T(8,128)(2,1)S(1)}, bf16[432,128]{1,0:T(8,128)(2,1)S(1)}, u32[]{:S(2)}, u32[]{:S(2)}) %collective-permute-start.19) | collective-permute-done | bytes 110624 | tf_op jit(solution)/shard_map/ppermute | solution.py:354
  105.9 0.1 pad_maximum_fusion.3
  106.0 0.1 pad_maximum_fusion.4
  106.1 2.2 %collective-permute-start.20 = (bf16[4,432,128]{2,1,0:T(8,128)(2,1)S(1)}, bf16[4,432,128]{2,1,0:T(8,128)(2,1)S(1)}, u32[]{:S(2)}, u32[]{:S(2)}) collective-permute-start(bf16[4,432,128]{2,1,0:T(8,128)(2,1)S(1)} %get-tuple-element.69), channel_id=1, source_target_pairs={{0,4},{4,0},{8,12},{12,8},{16,20},{20,16},{24,28},{28,24},{32,36},... | collective-permute-start | bytes 1327112 | tf_op jit(solution)/shard_map/ppermute | solution.py:354
  108.4 1.3 %collective-permute-start.16 = (bf16[1024,128]{1,0:T(8,128)(2,1)S(1)}, bf16[1024,128]{1,0:T(8,128)(2,1)S(1)}, u32[]{:S(2)}, u32[]{:S(2)}) collective-permute-start(bf16[1024,128]{1,0:T(8,128)(2,1)S(1)} %get-tuple-element.64.act_ref), channel_id=1, source_target_pairs={{0,1},{1,0},{2,3},{3,2},{4,5},{5,4},{6,7},{7,6},{8,9},{9,8},{10,11... | collective-permute-start | bytes 786440 | tf_op jit(solution)/shard_map/ppermute | solution.py:350
  109.7 6.5 %collective-permute-done.16.pair_ref = bf16[1024,128]{1,0:T(8,128)(2,1)S(1)} collective-permute-done((bf16[1024,128]{1,0:T(8,128)(2,1)S(1)}, bf16[1024,128]{1,0:T(8,128)(2,1)S(1)}, u32[]{:S(2)}, u32[]{:S(2)}) %collective-permute-start.16) | collective-permute-done | bytes 262176 | tf_op jit(solution)/shard_map/ppermute | solution.py:350
  116.2 1.7 %final.1 = (bf16[1024,128]{1,0:T(8,128)(2,1)}, bf16[1024,128]{1,0:T(8,128)(2,1)}) custom-call(f32[1024,128]{1,0:T(8,128)S(1)} %pad_maximum_fusion.1.local_ref, f32[1152,128]{1,0:T(8,128)S(1)} %get-tuple-element.62.placed_ref, s32[1,1152]{1,0:T(1,128)S(1)} %reshape.50.rr_ref, bf16[1024,128]{1,0:T(8,128)(2,1)S(1)} %get-tuple-element.64.act_ref, ...), custom_call_target="tpu_custom_call" | custom-call | flops 1000000000 | bytes 3000000 | tf_op jit(solution)/shard_map/final/pallas_call | solution.py:475
  117.9 0.3 fusion.2
  118.2 0.1 pad_maximum_fusion
  118.3 1.4 %convert.9 = f32[1,27,128,128]{3,2,1,0:T(8,128)} convert(bf16[1,27,128,128]{3,2,1,0:T(8,128)(2,1)S(1)} %bitcast.53) | non-fusion elementwise | flops 442368 | bytes 2654208 | tf_op jit(solution)/shard_map/convert_element_type | solution.py:485
  (33 shorter events, 0.2 us)
Async XLA Ops:
  3.4 1.2 copy-start
  4.5 0.9 copy-start.3
  5.5 9.6 %copy-start.2 = (bf16[1,1024,128]{2,1,0:T(8,128)(2,1)S(1)}, bf16[1,1024,128]{2,1,0:T(8,128)(2,1)}, u32[]{:S(2)}) copy-start(bf16[1,1024,128]{2,1,0:T(8,128)(2,1)} %param.8) | copy-start | bytes 786436
  5.5 10.9 %copy-start.8 = (s32[1024,27]{0,1:T(8,128)S(1)}, s32[1024,27]{0,1:T(8,128)}, u32[]{:S(2)}) copy-start(s32[1024,27]{0,1:T(8,128)} %param.9) | copy-start | bytes 331780
  5.5 19.5 %copy-start.1 = (bf16[1,27,128,128]{3,2,1,0:T(8,128)(2,1)S(1)}, bf16[1,27,128,128]{3,2,1,0:T(8,128)(2,1)}, u32[]{:S(2)}) copy-start(bf16[1,27,128,128]{3,2,1,0:T(8,128)(2,1)} %param.7) | copy-start | bytes 2654212
  5.5 19.5 %copy-start.4 = (bf16[1,1024,128]{2,1,0:T(8,128)(2,1)S(1)}, bf16[1,1024,128]{2,1,0:T(8,128)(2,1)}, u32[]{:S(2)}) copy-start(bf16[1,1024,128]{2,1,0:T(8,128)(2,1)} %param.6) | copy-start | bytes 786436
  10.2 1.5 %copy-start.5 = (bf16[4,1152,256]{2,1,0:T(8,128)(2,1)}, bf16[4,1152,256]{2,1,0:T(8,128)(2,1)S(1)}, u32[]{:S(2)}) copy-start(bf16[4,1152,256]{2,1,0:T(8,128)(2,1)S(1)} %get-tuple-element.47.face_g_ref) | copy-start | bytes 7077892
  11.7 0.7 copy-start.6
  12.4 4.0 %collective-permute-start = (bf16[320,128]{1,0:T(8,128)(2,1)S(1)}, bf16[320,128]{1,0:T(8,128)(2,1)S(1)}, u32[]{:S(2)}, u32[]{:S(2)}) collective-permute-start(bf16[320,128]{1,0:T(8,128)(2,1)S(1)} %get-tuple-element.36), channel_id=1, source_target_pairs={{0,4},{4,0},{8,12},{12,8},{16,20},{20,16},{24,28},{28,24},{32,36},... | collective-permute-start | bytes 245768 | tf_op jit(solution)/shard_map/ppermute | solution.py:337
  13.9 4.1 %collective-permute-start.1 = (bf16[320,128]{1,0:T(8,128)(2,1)S(1)}, bf16[320,128]{1,0:T(8,128)(2,1)S(1)}, u32[]{:S(2)}, u32[]{:S(2)}) collective-permute-start(bf16[320,128]{1,0:T(8,128)(2,1)S(1)} %get-tuple-element.37), channel_id=1, source_target_pairs={{0,12},{4,8},{8,4},{12,0},{16,28},{20,24},{24,20},{28,16},{32,44},... | collective-permute-start | bytes 245768 | tf_op jit(solution)/shard_map/ppermute | solution.py:337
  15.1 25.2 %collective-permute-start.4 = (bf16[1024,128]{1,0:T(8,128)(2,1)S(1)}, bf16[1024,128]{1,0:T(8,128)(2,1)S(1)}, u32[]{:S(2)}, u32[]{:S(2)}) collective-permute-start(bf16[1024,128]{1,0:T(8,128)(2,1)S(1)} %bitcast.48), channel_id=1, source_target_pairs={{0,1},{1,0},{2,3},{3,2},{4,5},{5,4},{6,7},{7,6},{8,9},{9,8},{10,11... | collective-permute-start | bytes 786440 | tf_op jit(solution)/shard_map/ppermute | solution.py:350
  17.9 22.3 %collective-permute-start.3 = (bf16[320,128]{1,0:T(8,128)(2,1)S(1)}, bf16[320,128]{1,0:T(8,128)(2,1)S(1)}, u32[]{:S(2)}, u32[]{:S(2)}) collective-permute-start(bf16[320,128]{1,0:T(8,128)(2,1)S(1)} %pad_maximum_fusion.6), channel_id=1, source_target_pairs={{0,112},{4,116},{8,120},{12,124},{16,32},{20,36},{24,40},{28,44},{... | collective-permute-start | bytes 245768 | tf_op jit(solution)/shard_map/ppermute | solution.py:346
  25.0 15.3 %collective-permute-start.2 = (bf16[320,128]{1,0:T(8,128)(2,1)}, bf16[320,128]{1,0:T(8,128)(2,1)S(1)}, u32[]{:S(2)}, u32[]{:S(2)}) collective-permute-start(bf16[320,128]{1,0:T(8,128)(2,1)} %pad_maximum_fusion.5), channel_id=1, source_target_pairs={{0,16},{4,20},{8,24},{12,28},{16,0},{20,4},{24,8},{28,12},{32,48},... | collective-permute-start | bytes 245768 | tf_op jit(solution)/shard_map/ppermute | solution.py:346
  42.8 5.5 %collective-permute-start.5 = (bf16[320,128]{1,0:T(8,128)(2,1)S(1)}, bf16[320,128]{1,0:T(8,128)(2,1)S(1)}, u32[]{:S(2)}, u32[]{:S(2)}) collective-permute-start(bf16[320,128]{1,0:T(8,128)(2,1)S(1)} %get-tuple-element.43), channel_id=1, source_target_pairs={{0,4},{4,0},{8,12},{12,8},{16,20},{20,16},{24,28},{28,24},{32,36},... | collective-permute-start | bytes 245768 | tf_op jit(solution)/shard_map/ppermute | solution.py:337
  47.6 4.3 %collective-permute-start.6 = (bf16[320,128]{1,0:T(8,128)(2,1)S(1)}, bf16[320,128]{1,0:T(8,128)(2,1)S(1)}, u32[]{:S(2)}, u32[]{:S(2)}) collective-permute-start(bf16[320,128]{1,0:T(8,128)(2,1)S(1)} %get-tuple-element.44), channel_id=1, source_target_pairs={{0,12},{4,8},{8,4},{12,0},{16,28},{20,24},{24,20},{28,16},{32,44},... | collective-permute-start | bytes 245768 | tf_op jit(solution)/shard_map/ppermute | solution.py:337
  52.0 10.0 %collective-permute-start.8 = (bf16[320,128]{1,0:T(8,128)(2,1)S(1)}, bf16[320,128]{1,0:T(8,128)(2,1)S(1)}, u32[]{:S(2)}, u32[]{:S(2)}) collective-permute-start(bf16[320,128]{1,0:T(8,128)(2,1)S(1)} %pad_maximum_fusion.8), channel_id=1, source_target_pairs={{0,112},{4,116},{8,120},{12,124},{16,32},{20,36},{24,40},{28,44},{... | collective-permute-start | bytes 245768 | tf_op jit(solution)/shard_map/ppermute | solution.py:346
  54.9 7.1 %copy-start.7 = (bf16[1536,128]{1,0:T(8,128)(2,1)S(1)}, bf16[1536,128]{1,0:T(8,128)(2,1)}, u32[]{:S(2)}) copy-start(bf16[1536,128]{1,0:T(8,128)(2,1)} %copy-done.6) | copy-start | bytes 1179652
  54.9 7.1 %collective-permute-start.7 = (bf16[320,128]{1,0:T(8,128)(2,1)S(1)}, bf16[320,128]{1,0:T(8,128)(2,1)S(1)}, u32[]{:S(2)}, u32[]{:S(2)}) collective-permute-start(bf16[320,128]{1,0:T(8,128)(2,1)S(1)} %pad_maximum_fusion.7), channel_id=1, source_target_pairs={{0,16},{4,20},{8,24},{12,28},{16,0},{20,4},{24,8},{28,12},{32,48},... | collective-permute-start | bytes 245768 | tf_op jit(solution)/shard_map/ppermute | solution.py:346
  67.1 6.8 %collective-permute-start.9 = (bf16[1728,128]{1,0:T(8,128)(2,1)S(1)}, bf16[1728,128]{1,0:T(8,128)(2,1)S(1)}, u32[]{:S(2)}, u32[]{:S(2)}) collective-permute-start(bf16[1728,128]{1,0:T(8,128)(2,1)S(1)} %dynamic-slice_bitcast_fusion), channel_id=1, source_target_pairs={{0,4},{4,0},{8,12},{12,8},{16,20},{20,16},{24,28},{28,24},{32,36},... | collective-permute-start | bytes 1327112 | tf_op jit(solution)/shard_map/ppermute | solution.py:354
  74.1 10.9 %collective-permute-start.10 = (bf16[432,128]{1,0:T(8,128)(2,1)S(1)}, bf16[432,128]{1,0:T(8,128)(2,1)S(1)}, u32[]{:S(2)}, u32[]{:S(2)}) collective-permute-start(bf16[432,128]{1,0:T(8,128)(2,1)S(1)} %get-tuple-element.75), channel_id=1, source_target_pairs={{0,8},{4,12},{8,0},{12,4},{16,24},{20,28},{24,16},{28,20},{32,40},... | collective-permute-start | bytes 331784 | tf_op jit(solution)/shard_map/ppermute | solution.py:354
  75.7 9.4 %collective-permute-start.11 = (bf16[432,128]{1,0:T(8,128)(2,1)S(1)}, bf16[432,128]{1,0:T(8,128)(2,1)S(1)}, u32[]{:S(2)}, u32[]{:S(2)}) collective-permute-start(bf16[432,128]{1,0:T(8,128)(2,1)S(1)} %get-tuple-element.77), channel_id=1, source_target_pairs={{0,16},{4,20},{8,24},{12,28},{16,0},{20,4},{24,8},{28,12},{32,48},... | collective-permute-start | bytes 331784 | tf_op jit(solution)/shard_map/ppermute | solution.py:354
  78.6 8.0 %collective-permute-start.12 = (bf16[432,128]{1,0:T(8,128)(2,1)S(1)}, bf16[432,128]{1,0:T(8,128)(2,1)S(1)}, u32[]{:S(2)}, u32[]{:S(2)}) collective-permute-start(bf16[432,128]{1,0:T(8,128)(2,1)S(1)} %get-tuple-element.76), channel_id=1, source_target_pairs={{0,24},{4,28},{8,16},{12,20},{16,8},{20,12},{24,0},{28,4},{32,56},... | collective-permute-start | bytes 331784 | tf_op jit(solution)/shard_map/ppermute | solution.py:354
  86.6 10.6 %collective-permute-start.13 = (bf16[432,128]{1,0:T(8,128)(2,1)S(1)}, bf16[432,128]{1,0:T(8,128)(2,1)S(1)}, u32[]{:S(2)}, u32[]{:S(2)}) collective-permute-start(bf16[432,128]{1,0:T(8,128)(2,1)S(1)} %fusion.5), channel_id=1, source_target_pairs={{0,32},{4,36},{8,40},{12,44},{16,48},{20,52},{24,56},{28,60},{32,0... | collective-permute-start | bytes 331784 | tf_op jit(solution)/shard_map/ppermute | solution.py:354
  88.2 9.1 %collective-permute-start.14 = (bf16[432,128]{1,0:T(8,128)(2,1)S(1)}, bf16[432,128]{1,0:T(8,128)(2,1)S(1)}, u32[]{:S(2)}, u32[]{:S(2)}) collective-permute-start(bf16[432,128]{1,0:T(8,128)(2,1)S(1)} %fusion.5), channel_id=1, source_target_pairs={{0,64},{4,68},{8,72},{12,76},{16,80},{20,84},{24,88},{28,92},{32,9... | collective-permute-start | bytes 331784 | tf_op jit(solution)/shard_map/ppermute | solution.py:354
  88.8 8.5 %collective-permute-start.15 = (bf16[432,128]{1,0:T(8,128)(2,1)S(1)}, bf16[432,128]{1,0:T(8,128)(2,1)S(1)}, u32[]{:S(2)}, u32[]{:S(2)}) collective-permute-start(bf16[432,128]{1,0:T(8,128)(2,1)S(1)} %fusion.5), channel_id=1, source_target_pairs={{0,96},{4,100},{8,104},{12,108},{16,112},{20,116},{24,120},{28,124... | collective-permute-start | bytes 331784 | tf_op jit(solution)/shard_map/ppermute | solution.py:354
  97.4 4.0 %collective-permute-start.17 = (bf16[432,128]{1,0:T(8,128)(2,1)S(1)}, bf16[432,128]{1,0:T(8,128)(2,1)S(1)}, u32[]{:S(2)}, u32[]{:S(2)}) collective-permute-start(bf16[432,128]{1,0:T(8,128)(2,1)S(1)} %fusion.7), channel_id=1, source_target_pairs={{0,8},{4,12},{8,0},{12,4},{16,24},{20,28},{24,16},{28,20},{32,40},... | collective-permute-start | bytes 331784 | tf_op jit(solution)/shard_map/ppermute | solution.py:354
  97.5 5.8 %collective-permute-start.18 = (bf16[432,128]{1,0:T(8,128)(2,1)S(1)}, bf16[432,128]{1,0:T(8,128)(2,1)S(1)}, u32[]{:S(2)}, u32[]{:S(2)}) collective-permute-start(bf16[432,128]{1,0:T(8,128)(2,1)S(1)} %fusion.7), channel_id=1, source_target_pairs={{0,16},{4,20},{8,24},{12,28},{16,0},{20,4},{24,8},{28,12},{32,48},... | collective-permute-start | bytes 331784 | tf_op jit(solution)/shard_map/ppermute | solution.py:354
  99.9 6.0 %collective-permute-start.19 = (bf16[432,128]{1,0:T(8,128)(2,1)S(1)}, bf16[432,128]{1,0:T(8,128)(2,1)S(1)}, u32[]{:S(2)}, u32[]{:S(2)}) collective-permute-start(bf16[432,128]{1,0:T(8,128)(2,1)S(1)} %fusion.7), channel_id=1, source_target_pairs={{0,24},{4,28},{8,16},{12,20},{16,8},{20,12},{24,0},{28,4},{32,56},... | collective-permute-start | bytes 331784 | tf_op jit(solution)/shard_map/ppermute | solution.py:354
  106.1 11.8 %collective-permute-start.20 = (bf16[4,432,128]{2,1,0:T(8,128)(2,1)S(1)}, bf16[4,432,128]{2,1,0:T(8,128)(2,1)S(1)}, u32[]{:S(2)}, u32[]{:S(2)}) collective-permute-start(bf16[4,432,128]{2,1,0:T(8,128)(2,1)S(1)} %get-tuple-element.69), channel_id=1, source_target_pairs={{0,4},{4,0},{8,12},{12,8},{16,20},{20,16},{24,28},{28,24},{32,36},... | collective-permute-start | bytes 1327112 | tf_op jit(solution)/shard_map/ppermute | solution.py:354
  108.4 7.9 %collective-permute-start.16 = (bf16[1024,128]{1,0:T(8,128)(2,1)S(1)}, bf16[1024,128]{1,0:T(8,128)(2,1)S(1)}, u32[]{:S(2)}, u32[]{:S(2)}) collective-permute-start(bf16[1024,128]{1,0:T(8,128)(2,1)S(1)} %get-tuple-element.64.act_ref), channel_id=1, source_target_pairs={{0,1},{1,0},{2,3},{3,2},{4,5},{5,4},{6,7},{7,6},{8,9},{9,8},{10,11... | collective-permute-start | bytes 786440 | tf_op jit(solution)/shard_map/ppermute | solution.py:350

commit v2 on v1

--- a/solution.py
+++ b/solution.py
@@ -70,6 +70,10 @@
     return jnp.broadcast_to(kept, (column.shape[0], count)).astype(jnp.int16)
 
 
+def column_of(row):
+    return jnp.broadcast_to(row.astype(F32), (8, row.shape[1])).T[:, :1].astype(jnp.int32)
+
+
 def corner_mask(position, axis, shape):
     lane = lax.broadcasted_iota(jnp.int32, shape, axis)
     return (lane // TZ) == position
@@ -81,7 +85,7 @@
 
 def face_match(number, offset, column, sm_ref):
     start, length = SPANS[number]
-    return match(column, sm_ref[offset, :, start : start + length])
+    return match(column, sm_ref[offset : offset + 1, start : start + length])
 
 
 def corner_row(place, sm_ref):
@@ -89,15 +93,15 @@
     for number in CORNERS:
         start, length = SPANS[number]
         offset = toward(*DIRECTIONS[number])[place]
-        pieces.append(sm_ref[offset, :, start : start + length])
+        pieces.append(sm_ref[offset : offset + 1, start : start + length])
     return jnp.concatenate(pieces, 1)
 
 
-def corner_column(rc_ref, count):
+def corner_column(rc, count):
     pieces = []
     for number in CORNERS:
         start, length = SPANS[7 - number]
-        pieces.append(rc_ref[start : start + length, :])
+        pieces.append(rc[start : start + length, :])
     return spread(jnp.concatenate(pieces, 0), count)
 
 
@@ -139,15 +143,16 @@
     return lists
 
 
-def start_kernel(side_ref, x_ref, rr_ref, rc_ref, sm_ref, w_ref, xa_ref, xb_ref, ya_ref, yb_ref, face_g_ref, corner_g_ref):
+def start_kernel(side_ref, x_ref, rr_ref, sm_ref, w_ref, xa_ref, xb_ref, ya_ref, yb_ref, face_g_ref, corner_g_ref):
     lists = [None] * 8
+    rc = column_of(rr_ref[...])
     x_t = x_ref[...].astype(F32).T.astype(BF)
     selector = hot(rr_ref[...], ROWS)
     listed = dot(x_t, selector).astype(BF)
     for place, number in enumerate(FACES):
         start, length = SPANS[number]
         other, _ = SPANS[7 - number]
-        column = spread(rc_ref[other : other + length, :], length)
+        column = spread(rc[other : other + length, :], length)
         source = listed[:, other : other + length]
         picked = toward(*DIRECTIONS[number])
         gathered = []
@@ -159,7 +164,7 @@
         weight = jnp.concatenate([w_ref[offset] for offset in picked], 0)
         total = dot(weight, gathered, ((0,), (0,)))
         lists[number] = total.T.astype(BF)
-    column = corner_column(rc_ref, 4 * TZ)
+    column = corner_column(rc, 4 * TZ)
     source = jnp.concatenate(
         [listed[:, SPANS[7 - n][0] : SPANS[7 - n][0] + TZ] for n in CORNERS], 1
     )
@@ -182,12 +187,6 @@
     pack_sides(lists, 1, (side_ref[0], side_ref[1]), xa_ref, xb_ref, ya_ref, yb_ref)
 
 
-def pair_of(step):
-    first = jnp.where(2 * step >= 13, 2 * step + 1, 2 * step)
-    second = jnp.where(2 * step + 1 >= 13, 2 * step + 2, 2 * step + 1)
-    return first, second
-
-
 def forward_kernel(x_ref, lm_ref, w_ref, g_ref, pre_ref, x_t, total, *, width):
     step = pl.program_id(0)
 
@@ -196,16 +195,18 @@
         x_t[...] = x_ref[...].astype(F32).T.astype(BF)
         total[...] = dot(w_ref[13], x_t[...], ((0,), (0,)))
 
-    pair = pair_of(step)
-    weight = jnp.concatenate([w_ref[k] for k in pair], 0)
+    source = x_t[...]
+    weight = jnp.concatenate([w_ref[14 * step + i] for i in range(13)], 0)
     for begin in range(0, ROWS, width):
         cols = slice(begin, begin + width)
-        gathered = [dot(x_t[...], hot(lm_ref[k, :, cols], ROWS)).astype(BF) for k in pair]
+        gathered = [
+            dot(source, hot(lm_ref[pl.ds(14 * step + i, 1), cols], ROWS)).astype(BF) for i in range(13)
+        ]
         gathered = jnp.concatenate(gathered, 0)
         g_ref[:, cols] = gathered
         total[:, cols] += dot(weight, gathered, ((0,), (0,)))
 
-    @pl.when(step == 12)
+    @pl.when(step == 1)
     def _():
         pre_ref[...] = total[...].T
 
@@ -239,14 +240,15 @@
     dw_ref[pl.ds(14 * step, 13)] = total.reshape(13, C, C)
 
 
-def return_kernel(side_ref, ixa_ref, ixb_ref, iya_ref, iyb_ref, rc_ref, sm_ref, w_ref, face_g_ref, corner_g_ref, dw_in_ref, dw_ref, placed_ref, total):
+def return_kernel(side_ref, ixa_ref, ixb_ref, iya_ref, iyb_ref, rr_ref, sm_ref, w_ref, face_g_ref, corner_g_ref, dw_in_ref, dw_ref, placed_ref, total):
     total[...] = dw_in_ref[...]
+    rc = column_of(rr_ref[...])
     sides = (side_ref[0], side_ref[1])
     returned = unpack_sides(-1, sides, ixa_ref[...], ixb_ref[...], iya_ref[...], iyb_ref[...])
     for place, number in enumerate(FACES):
         start, length = SPANS[number]
         other, _ = SPANS[7 - number]
-        column = spread(rc_ref[other : other + length, :], length)
+        column = spread(rc[other : other + length, :], length)
         back = returned[number]
         picked = toward(*DIRECTIONS[number])
         pieces = []
@@ -259,7 +261,7 @@
         kernel_part = dot(face_g_ref[place], back)
         for index, offset in enumerate(picked):
             total[offset] += kernel_part[index * C : (index + 1) * C, :]
-    column = corner_column(rc_ref, 4 * TZ)
+    column = corner_column(rc, 4 * TZ)
     back = jnp.concatenate([returned[n] for n in CORNERS], 0)
     kernel_part = dot(corner_g_ref[...], back)
     pieces = []
@@ -280,31 +282,38 @@
     dw_ref[...] = total[...].astype(BF)
 
 
-def backward_kernel(grad_ref, own_ref, lm_ref, w_ref, out_ref, grad_t, total):
-    step = pl.program_id(0)
-
-    @pl.when(step == 0)
-    def _():
-        grad_t[...] = grad_ref[...].astype(F32).T.astype(BF)
-        total[...] = dot(w_ref[13], own_ref[...].astype(F32).T.astype(BF))
-
-    pair = pair_of(step)
-    weight = jnp.concatenate([w_ref[k] for k in pair], 1)
-    gathered = [dot(grad_t[...], hot(lm_ref[26 - k], ROWS)).astype(BF) for k in pair]
-    total[...] += dot(weight, jnp.concatenate(gathered, 0))
-
-    @pl.when(step == 12)
-    def _():
-        out_ref[...] = total[...].T
-
-
-def final_kernel(local_ref, placed_ref, rr_ref, act_ref, pair_ref, mixed_ref, out_ref):
+def backward_kernel(grad_ref, lm_ref, w_ref, out_ref, *, begin):
+    size = out_ref.shape[0]
+    source = grad_ref[...].astype(F32).T.astype(BF)
+    gathered = []
+    for k in range(27):
+        if k == 13:
+            gathered.append(source[:, begin : begin + size])
+        else:
+            gathered.append(dot(source, hot(lm_ref[26 - k : 27 - k, begin : begin + size], ROWS)).astype(BF))
+    weight = jnp.concatenate([w_ref[k] for k in range(27)], 1)
+    out_ref[...] = dot(weight, jnp.concatenate(gathered, 0)).T
+
+
+def final_kernel(*refs):
+    placed_ref, rr_ref, act_ref, pair_ref, mixed_ref, out_ref = refs[-6:]
     placed = placed_ref[...]
     high = placed.astype(BF)
     low = (placed - high.astype(F32)).astype(BF)
     both = dot(hot(rr_ref[...], ROWS), jnp.concatenate([high, low], 1))
-    out_ref[...] = (local_ref[...] + both[:, :C] + both[:, C:]).astype(BF)
+    both = both[:, :C] + both[:, C:]
+    size = ROWS // len(refs[:-6])
+    for index, ref in enumerate(refs[:-6]):
+        rows = slice(index * size, (index + 1) * size)
+        out_ref[rows, :] = (ref[...] + both[rows]).astype(BF)
     mixed_ref[...] = (act_ref[...].astype(F32) + pair_ref[...].astype(F32)).astype(BF)
+
+
+def assemble_kernel(bits_ref, own_ref, one_ref, two_ref, four_ref, out_ref):
+    place = bits_ref[0] * 4 + bits_ref[1] * 2 + bits_ref[2]
+    blocks = [own_ref[...], one_ref[...]] + [two_ref[i] for i in range(2)] + [four_ref[i] for i in range(4)]
+    for distance, block in enumerate(blocks):
+        out_ref[place ^ distance] = block.astype(F32)
 
 
 PARAMS = pltpu.CompilerParams(vmem_limit_bytes=48 * 2**20)
@@ -377,10 +386,9 @@
     x = features[0]
     w = weights[0]
     cot = cotangent[0]
-    lm = local_map.T.reshape(27, 1, ROWS)
-    sm = send_map.T.reshape(27, 1, HALO)
+    lm = local_map.T
+    sm = send_map.T
     rr = recv_map.reshape(1, HALO)
-    rc = recv_map.reshape(HALO, 1)
     me = lax.axis_index("space")
     sides = jnp.stack([me % 2, me // TILES_X % 2]).astype(jnp.int32)
     smem = pl.BlockSpec(memory_space=pltpu.SMEM)
@@ -388,20 +396,20 @@
     out_lists = [shape((CAP + 2 * TZ, C), BF)] * 2 + [shape((CAP, C), BF)] * 2
     xa, xb, ya, yb, face_g, corner_g = pl.pallas_call(
         start_kernel,
-        in_specs=[smem] + [vmem] * 5,
+        in_specs=[smem] + [vmem] * 4,
         out_shape=out_lists + [shape((4, 9 * C, CAP), BF), shape((12 * C, 4 * TZ), BF)],
         compiler_params=PARAMS,
         cost_estimate=cost(2e9, 4e6),
         name="start",
-    )(sides, x, rr, rc, sm, w)
+    )(sides, x, rr, sm, w)
     cot_pair = swapped(cot)
     in_x = exchange_x(xa, xb)
     in_y = exchange_y(ya, yb, *in_x, sides)
     gathered, pre = pl.pallas_call(
         functools.partial(forward_kernel, width=512),
-        grid=(13,),
-        in_specs=[whole((ROWS, C)), whole((27, 1, ROWS)), whole((27, C, C))],
-        out_specs=[pl.BlockSpec((2 * C, ROWS), lambda j: (j, 0)), whole((ROWS, C))],
+        grid=(2,),
+        in_specs=[whole((ROWS, C)), whole((27, ROWS)), whole((27, C, C))],
+        out_specs=[pl.BlockSpec((13 * C, ROWS), lambda j: (j, 0)), whole((ROWS, C))],
         out_shape=[shape((26 * C, ROWS), BF), shape((ROWS, C), F32)],
         scratch_shapes=[pltpu.VMEM((C, ROWS), BF), pltpu.VMEM((C, ROWS), F32)],
         compiler_params=PARAMS,
@@ -429,23 +437,20 @@
         name="weight",
     )(gathered, grad, x)
 
-    size = ROWS // 4
+    parts = 4
+    size = ROWS // parts
 
     def backward(index, grad):
         return pl.pallas_call(
-            backward_kernel,
-            grid=(13,),
-            in_specs=[whole((ROWS, C)), pl.BlockSpec((size, C), lambda j: (index, 0)),
-                      pl.BlockSpec((27, 1, size), lambda j: (0, 0, index)), whole((27, C, C))],
-            out_specs=whole((size, C)),
+            functools.partial(backward_kernel, begin=index * size),
             out_shape=shape((size, C), F32),
-            scratch_shapes=[pltpu.VMEM((C, ROWS), BF), pltpu.VMEM((C, size), F32)],
             compiler_params=PARAMS,
-            cost_estimate=cost(5e9, 2e6),
+            cost_estimate=cost(3e9, 2e6),
             name="backward",
-        )(grad, grad, lm, w)
-
-    locals_ = [backward(0, tie(grad, dw_local))]
+        )(grad, lm, w)
+
+    act_pair = swapped(act)
+    act_pair, dw_local = lax.optimization_barrier((act_pair, dw_local))
     dw, placed = pl.pallas_call(
         return_kernel,
         in_specs=[smem] + [vmem] * 10,
@@ -454,35 +459,40 @@
         compiler_params=PARAMS,
         cost_estimate=cost(3e9, 4e6),
         name="returning",
-    )(sides, *in_x, *in_y, rc, sm, w, face_g, corner_g, tie(dw_local, locals_[0]))
-    act_pair = swapped(tie(act, dw))
-
-    core, x_at, z_at = me % 2, me // 2 % 4, me // 8
-    halves = dw.reshape(2, -1, C)
-    got = xor_send(pick(halves, 1 - core), 1)
-    locals_.append(backward(1, tie(grad, dw)))
-    half = add_up([pick(halves, core), tie(got, locals_[1])])
-    quarters = half.reshape(4, -1, C)
-    got = [xor_send(pick(quarters, x_at ^ bits), bits * 2) for bits in (1, 2, 3)]
-    locals_.append(backward(2, tie(grad, half)))
-    quarter = add_up([pick(quarters, x_at)] + [tie(v, locals_[2]) for v in got])
-    got = [xor_send(quarter, bits * 8) for bits in (1, 2, 3)]
-    locals_.append(backward(3, tie(grad, quarter)))
-    stacked = jnp.stack([quarter] + [tie(v, locals_[3]) for v in got])
-    quarter = add_up([pick(stacked, z_at ^ index) for index in range(4)])
-    got = jnp.stack([quarter] + [xor_send(quarter, bits * 2) for bits in (1, 2, 3)])
-    local = tie(jnp.concatenate(locals_, 0), quarter)
+    )(sides, *in_x, *in_y, rr, sm, w, face_g, corner_g, dw_local)
+
+    bits = [me % 2, me // 2 % 2, me // 4 % 2]
+    blocks = dw.reshape(2, 2, 2, -1, C)
+    locals_ = []
+    for stage, place in enumerate((1, 2, 4)):
+        kept, sent = pick(blocks, bits[stage]), pick(blocks, 1 - bits[stage])
+        got = xor_send(sent, place)
+        locals_.append(backward(stage, tie(grad, sent)))
+        blocks = add_up([kept, tie(got, locals_[-1])])
+    got = xor_send(blocks, 8)
+    locals_.append(backward(3, tie(grad, blocks)))
+    blocks = add_up([blocks, tie(got, locals_[-1])])
+    got = xor_send(blocks, 16)
     mixed, input_grad = pl.pallas_call(
         final_kernel,
         out_shape=[shape((ROWS, C), BF), shape((ROWS, C), BF)],
         compiler_params=PARAMS,
         cost_estimate=cost(1e9, 3e6),
         name="final",
-    )(local, placed, rr, act, act_pair)
-    half = jnp.stack([pick(got, x_at ^ index) for index in range(4)])
-    got = jnp.stack([half, xor_send(half, 1)])
-    both = jnp.stack([pick(got, core), pick(got, 1 - core)])
-    weight_grad = both.reshape(dw.shape).astype(F32)
+    )(*locals_, tie(placed, blocks), rr, act, act_pair)
+    own = add_up([blocks, tie(got, input_grad)])
+    one = xor_send(own, 4)
+    two = xor_send(jnp.stack([own, one]), 2)
+    four = xor_send(jnp.concatenate([jnp.stack([own, one]), two], 0), 1)
+    weight_grad = pl.pallas_call(
+        assemble_kernel,
+        in_specs=[smem] + [vmem] * 4,
+        out_shape=shape((8,) + own.shape, F32),
+        compiler_params=PARAMS,
+        cost_estimate=cost(1e6, 3e6),
+        name="assemble",
+    )(jnp.stack(bits).astype(jnp.int32), own, one, two, four)
+    weight_grad = weight_grad.reshape(dw.shape)
     return (mixed[None], input_grad[None], weight_grad[None])
 
 

time: 120 us -> 106 us (0.88)
  Pallas kernels: 59.8 us -> 41.4 us
  waiting for transfers between devices: 17.5 us -> 25.4 us
  starting transfers between devices: 31.2 us -> 29.3 us
  other arithmetic: 3.14 us -> 1.56 us
    pallas_call x6 -> x7, Pallas kernels: 46.1 us -> 27.4 us  [the longest x1 10.8 us: on_device(): pl.pallas_call(functools.partial(forward_kernel, width=512), grid=(2,), i...]
    ppermute x11 -> x8, waiting for transfers between devices: 5.95 us -> 18.9 us  [xor_send(): lax.ppermute(value, 'space', [(i, i ^ bits) for i in range(lax.axis_size(...]
    ppermute x2, waiting for transfers between devices: 6.51 us -> 0.01 us  [swapped(): lax.ppermute(array, 'segment', [(i, i ^ 1) for i in range(lax.axis_size('...]
    reshape x3 -> x0, local copies, waits for them, and re-layouts: 1.98 us -> none  [the longest x1 1 us: on_device(): sm = send_map.T.reshape(27, 1, HALO)]
    ppermute x4, waiting for transfers between devices: 0.01 us -> 1.76 us  [exchange_y(): lax.ppermute(v, 'space', pairing('y', n))]
    ppermute x4, starting transfers between devices: 9.81 us -> 8.07 us  [exchange_y(): lax.ppermute(v, 'space', pairing('y', n))]
    convert_element_type x1 -> x0, other arithmetic: 1.41 us -> none  [on_device(): weight_grad = both.reshape(dw.shape).astype(F32)]
    ppermute x11 -> x8, starting transfers between devices: 15 us -> 13.7 us  [xor_send(): lax.ppermute(value, 'space', [(i, i ^ bits) for i in range(lax.axis_size(...]
  transfers between devices with their start and end apart: 21 -> 18, of which waited for: 6 -> 10; matrix products, arithmetic and copies ran while one was open for 1% -> 0% of each run, Pallas kernels for 40% -> 25%
where the time goes in v2:
time: 106 us; the launch traced here: 105 us
  Pallas kernels  41.4 us (39%)
  starting transfers between devices  29.3 us (28%)
  waiting for transfers between devices  25.4 us (24%)
  local copies, waits for them, and re-layouts  6.82 us (6%)
  other arithmetic  1.56 us (1%)
    ppermute x8, waiting for transfers between devices, xor_send(): lax.ppermute(value, 'space', [(i, i ^ bits) for i in range(lax.axis_size(...  18.9 us
    ppermute x8, starting transfers between devices, xor_send(): lax.ppermute(value, 'space', [(i, i ^ bits) for i in range(lax.axis_size(...  13.7 us
    pallas_call x1, Pallas kernels, on_device(): pl.pallas_call(functools.partial(forward_kernel, width=512), grid=(2,), i...  10.8 us
    pallas_call x4, Pallas kernels, backward(): pl.pallas_call(functools.partial(backward_kernel, begin=index * size), ou...  9.78 us
    ppermute x4, starting transfers between devices, exchange_y(): lax.ppermute(v, 'space', pairing('y', n))  8.07 us
    pallas_call x1, Pallas kernels, on_device(): pl.pallas_call(return_kernel, in_specs=[smem] + [vmem] * 10, out_shape=[s...  5.35 us
    unnamed x22, local copies, waits for them, and re-layouts  5.27 us
    pallas_call x1, Pallas kernels, on_device(): pl.pallas_call(start_kernel, in_specs=[smem] + [vmem] * 4, out_shape=out_...  4.98 us
  transfers between devices with their start and end apart: 18, of which 10 were waited for; matrix products, arithmetic and copies ran while one was open for 0% of the time, Pallas kernels for 25%

profile of v2, /device:TPU:1, one launch (start us, length us, event | category | flops | bytes accessed | tf_op | source)
XLA Modules:
  0.0 105.3 jit_solution(9712339674217762473)
XLA Ops:
  0.7 0.7 reshape.18.rr_ref.refs_5_
  1.4 0.1 pad_add_fusion.side_ref
  1.4 1.2 %copy-done = bf16[1,27,128,128]{3,2,1,0:T(8,128)(2,1)S(1)} copy-done((bf16[1,27,128,128]{3,2,1,0:T(8,128)(2,1)S(1)}, bf16[1,27,128,128]{3,2,1,0:T(8,128)(2,1)}, u32[]{:S(2)}) %copy-start) | copy-done | bytes 884760
  2.6 0.9 copy-done.3
  3.6 0.9 copy-done.5
  4.5 5.0 %start.1 = (bf16[320,128]{1,0:T(8,128)(2,1)S(1)}, bf16[320,128]{1,0:T(8,128)(2,1)S(1)}, bf16[256,128]{1,0:T(8,128)(2,1)S(1)}, bf16[256,128]{1,0:T(8,128)(2,1)S(1...) custom-call(s32[2]{0:T(128)S(1)} %pad_add_fusion.side_ref, bf16[1024,128]{1,0:T(8,128)(2,1)S(1)} %bitcast.44, ...), custom_call_target="tpu_custom_call" | custom-call | flops 2000000000 | bytes 4000000 | tf_op jit(solution)/shard_map/start/pallas_call | solution.py:397
  9.5 0.0 copy-start.8
  9.5 1.5 %copy-done.8 = bf16[4,1152,256]{2,1,0:T(8,128)(2,1)} copy-done((bf16[4,1152,256]{2,1,0:T(8,128)(2,1)}, bf16[4,1152,256]{2,1,0:T(8,128)(2,1)S(1)}, u32[]{:S(2)}) %copy-start.8) | copy-done | bytes 2359320
  11.0 0.7 copy-done.9
  11.7 1.4 %collective-permute-start = (bf16[320,128]{1,0:T(8,128)(2,1)S(1)}, bf16[320,128]{1,0:T(8,128)(2,1)S(1)}, u32[]{:S(2)}, u32[]{:S(2)}) collective-permute-start(bf16[320,128]{1,0:T(8,128)(2,1)S(1)} %get-tuple-element.34), channel_id=1, source_target_pairs={{0,4},{4,0},{8,12},{12,8},{16,20},{20,16},{24,28},{28,24},{32,36},... | collective-permute-start | bytes 245768 | tf_op jit(solution)/shard_map/ppermute | solution.py:346
  13.1 1.2 %collective-permute-start.1 = (bf16[320,128]{1,0:T(8,128)(2,1)S(1)}, bf16[320,128]{1,0:T(8,128)(2,1)S(1)}, u32[]{:S(2)}, u32[]{:S(2)}) collective-permute-start(bf16[320,128]{1,0:T(8,128)(2,1)S(1)} %get-tuple-element.35), channel_id=1, source_target_pairs={{0,12},{4,8},{8,4},{12,0},{16,28},{20,24},{24,20},{28,16},{32,44},... | collective-permute-start | bytes 245768 | tf_op jit(solution)/shard_map/ppermute | solution.py:346
  14.3 0.0 copy-done.2
  14.3 1.3 %collective-permute-start.4 = (bf16[1024,128]{1,0:T(8,128)(2,1)S(1)}, bf16[1024,128]{1,0:T(8,128)(2,1)S(1)}, u32[]{:S(2)}, u32[]{:S(2)}) collective-permute-start(bf16[1024,128]{1,0:T(8,128)(2,1)S(1)} %bitcast.42), channel_id=1, source_target_pairs={{0,1},{1,0},{2,3},{3,2},{4,5},{5,4},{6,7},{7,6},{8,9},{9,8},{10,11... | collective-permute-start | bytes 786440 | tf_op jit(solution)/shard_map/ppermute | solution.py:359
  15.6 0.0 collective-permute-done.ixa_ref
  15.6 1.6 %collective-permute-done.1.ixb_ref = bf16[320,128]{1,0:T(8,128)(2,1)S(1)} collective-permute-done((bf16[320,128]{1,0:T(8,128)(2,1)S(1)}, bf16[320,128]{1,0:T(8,128)(2,1)S(1)}, u32[]{:S(2)}, u32[]{:S(2)}) %collective-permute-start.1) | collective-permute-done | bytes 81952 | tf_op jit(solution)/shard_map/ppermute | solution.py:346
  17.2 2.9 %collective-permute-start.2 = (bf16[320,128]{1,0:T(8,128)(2,1)S(1)}, bf16[320,128]{1,0:T(8,128)(2,1)S(1)}, u32[]{:S(2)}, u32[]{:S(2)}) collective-permute-start(bf16[320,128]{1,0:T(8,128)(2,1)S(1)} %pad_maximum_fusion.2), channel_id=1, source_target_pairs={{0,16},{4,20},{8,24},{12,28},{16,0},{20,4},{24,8},{28,12},{32,48},... | collective-permute-start | bytes 245768 | tf_op jit(solution)/shard_map/ppermute | solution.py:355
  20.1 3.7 %collective-permute-start.3 = (bf16[320,128]{1,0:T(8,128)(2,1)S(1)}, bf16[320,128]{1,0:T(8,128)(2,1)S(1)}, u32[]{:S(2)}, u32[]{:S(2)}) collective-permute-start(bf16[320,128]{1,0:T(8,128)(2,1)S(1)} %pad_maximum_fusion.3), channel_id=1, source_target_pairs={{0,112},{4,116},{8,120},{12,124},{16,32},{20,36},{24,40},{28,44},{... | collective-permute-start | bytes 245768 | tf_op jit(solution)/shard_map/ppermute | solution.py:355
  23.8 0.0 copy-done.7
  23.8 10.8 %forward.1 = (bf16[3328,1024]{1,0:T(8,128)(2,1)}, f32[1024,128]{1,0:T(8,128)S(1)}) custom-call(bf16[1024,128]{1,0:T(8,128)(2,1)S(1)} %bitcast.45, s32[27,1024]{1,0:T(8,128)S(1)} %bitcast.49, bf16[27,128,128]{2,1,0:T(8,128)(2,1)S(1)} %bitcast.36), custom_call_target="tpu_custom_call" | custom-call | flops 15000000512 | bytes 9000000 | tf_op jit(solution)/shard_map/forward/pallas_call | solution.py:408
  34.6 0.0 collective-permute-done.2.iya_ref
  34.6 0.0 collective-permute-done.3.iyb_ref
  34.6 0.0 collective-permute-done.4.pair_ref
  34.6 2.5 %activate.1 = (bf16[1024,128]{1,0:T(8,128)(2,1)S(1)}, bf16[1024,128]{1,0:T(8,128)(2,1)S(1)}, bf16[320,128]{1,0:T(8,128)(2,1)S(1)}, bf16[320,128]{1,0:T(8,128)(2,...) custom-call(s32[2]{0:T(128)S(1)} %pad_add_fusion.side_ref, ...), custom_call_target="tpu_custom_call" | custom-call | flops 1500000000 | bytes 3000000 | tf_op jit(solution)/shard_map/activate/pallas_call | solution.py:419
  37.2 0.7 collective-permute-start.5
  37.9 1.3 %collective-permute-start.9 = (bf16[1024,128]{1,0:T(8,128)(2,1)S(1)}, bf16[1024,128]{1,0:T(8,128)(2,1)S(1)}, u32[]{:S(2)}, u32[]{:S(2)}) collective-permute-start(bf16[1024,128]{1,0:T(8,128)(2,1)S(1)} %get-tuple-element.45.refs_6_), channel_id=1, source_target_pairs={{0,1},{1,0},{2,3},{3,2},{4,5},{5,4},{6,7},{7,6},{8,9},{9,8},{10,11... | collective-permute-start | bytes 786440 | tf_op jit(solution)/shard_map/ppermute | solution.py:359
  39.2 1.6 %collective-permute-start.6 = (bf16[320,128]{1,0:T(8,128)(2,1)S(1)}, bf16[320,128]{1,0:T(8,128)(2,1)S(1)}, u32[]{:S(2)}, u32[]{:S(2)}) collective-permute-start(bf16[320,128]{1,0:T(8,128)(2,1)S(1)} %get-tuple-element.40), channel_id=1, source_target_pairs={{0,12},{4,8},{8,4},{12,0},{16,28},{20,24},{24,20},{28,16},{32,44},... | collective-permute-start | bytes 245768 | tf_op jit(solution)/shard_map/ppermute | solution.py:346
  40.7 0.0 collective-permute-done.5.ixa_ref
  40.7 3.1 %collective-permute-done.6.ixb_ref = bf16[320,128]{1,0:T(8,128)(2,1)S(1)} collective-permute-done((bf16[320,128]{1,0:T(8,128)(2,1)S(1)}, bf16[320,128]{1,0:T(8,128)(2,1)S(1)}, u32[]{:S(2)}, u32[]{:S(2)}) %collective-permute-start.6) | collective-permute-done | bytes 81952 | tf_op jit(solution)/shard_map/ppermute | solution.py:346
  43.9 1.5 %collective-permute-start.8 = (bf16[320,128]{1,0:T(8,128)(2,1)S(1)}, bf16[320,128]{1,0:T(8,128)(2,1)S(1)}, u32[]{:S(2)}, u32[]{:S(2)}) collective-permute-start(bf16[320,128]{1,0:T(8,128)(2,1)S(1)} %pad_maximum_fusion.5), channel_id=1, source_target_pairs={{0,112},{4,116},{8,120},{12,124},{16,32},{20,36},{24,40},{28,44},{... | collective-permute-start | bytes 245768 | tf_op jit(solution)/shard_map/ppermute | solution.py:355
  45.4 0.0 collective-permute-start.7
  45.4 0.0 copy-start.6
  45.4 0.0 copy-start.10
  45.4 4.4 %weight.1.dw_in_ref = f32[27,128,128]{2,1,0:T(8,128)S(1)} custom-call(bf16[3328,1024]{1,0:T(8,128)(2,1)} %get-tuple-element.46.g_ref, bf16[1024,128]{1,0:T(8,128)(2,1)S(1)} %get-tuple-element.55.grad_ref, bf16[1024,128]{1,0:T(8,128)(2,1)S(1)} %bitcast.46), custom_call_target="tpu_custom_call" | custom-call | flops 4000000000 | bytes 9000000 | tf_op jit(solution)/shard_map/weight/pallas_call | solution.py:429
  49.8 0.0 collective-permute-done.9.refs_7_
  49.8 1.8 %collective-permute-done.8.iyb_ref = bf16[320,128]{1,0:T(8,128)(2,1)S(1)} collective-permute-done((bf16[320,128]{1,0:T(8,128)(2,1)S(1)}, bf16[320,128]{1,0:T(8,128)(2,1)S(1)}, u32[]{:S(2)}, u32[]{:S(2)}) %collective-permute-start.8) | collective-permute-done | bytes 81952 | tf_op jit(solution)/shard_map/ppermute | solution.py:355
  51.6 0.0 collective-permute-done.7.iya_ref
  51.6 0.0 copy-done.6
  51.6 5.3 %returning.1 = (bf16[27,128,128]{2,1,0:T(8,128)(2,1)S(1)}, f32[1152,128]{1,0:T(8,128)S(1)}) custom-call(s32[2]{0:T(128)S(1)} %pad_add_fusion.side_ref, bf16[320,128]{1,0:T(8,128)(2,1)S(1)} %collective-permute-done.5.ixa_ref, bf16[320,128]{1,0:T(8,128)(2,1)S(1)} %collective-permute-done.6.ixb_ref, bf16[320,128]{1,0:T(8,128)(2,1)S(1)} %collective-permute-done.7.iya_ref, ...), custom_call_target="tpu_custom_call" | custom-call | flops 3000000000 | bytes 4000000 | tf_op jit(solution)/shard_map/returning/pallas_call | solution.py:454
  57.0 0.8 dynamic-slice_bitcast_fusion
  57.8 1.1 %collective-permute-start.10 = (bf16[2,2,432,128]{3,2,1,0:T(8,128)(2,1)}, bf16[2,2,432,128]{3,2,1,0:T(8,128)(2,1)}, u32[]{:S(2)}, u32[]{:S(2)}) collective-permute-start(bf16[2,2,432,128]{3,2,1,0:T(8,128)(2,1)} %dynamic-slice_bitcast_fusion), channel_id=1, source_target_pairs={{0,4},{4,0},{8,12},{12,8},{16,20},{20,16},{24,28},{28,24},{32,36},... | collective-permute-start | bytes 1327112 | tf_op jit(solution)/shard_map/ppermute | solution.py:363
  58.8 2.4 %backward.4.refs_0_ = f32[256,128]{1,0:T(8,128)S(1)} custom-call(bf16[1024,128]{1,0:T(8,128)(2,1)S(1)} %get-tuple-element.55.grad_ref, s32[27,1024]{1,0:T(8,128)S(1)} %bitcast.50, bf16[27,128,128]{2,1,0:T(8,128)(2,1)S(1)} %bitcast.38), custom_call_target="tpu_custom_call" | custom-call | flops 3000000000 | bytes 2000000 | tf_op jit(solution)/shard_map/backward/pallas_call | solution.py:444
  61.3 0.0 collective-permute-done.10
  61.3 1.1 %fusion = bf16[2,2,432,128]{3,2,1,0:T(8,128)(2,1)S(1)} fusion(bf16[2,2,432,128]{3,2,1,0:T(8,128)(2,1)} %collective-permute-done.10, bf16[2,2,2,432,128]{4,3,2,1,0:T(8,128)(2,1)S(1)} %bitcast.34, s32[]{:T(128)S(6)} %select_n.100), kind=kLoop, calls=%fused_computation.1 | loop fusion | flops 884736 | bytes 1327108 | tf_op jit(solution)/shard_map/convert_element_type | solution.py:370
  62.5 1.8 %collective-permute-start.11 = (bf16[2,432,128]{2,1,0:T(8,128)(2,1)S(1)}, bf16[2,432,128]{2,1,0:T(8,128)(2,1)S(1)}, u32[]{:S(2)}, u32[]{:S(2)}) collective-permute-start(bf16[2,432,128]{2,1,0:T(8,128)(2,1)S(1)} %dynamic-slice_bitcast_fusion.1), channel_id=1, source_target_pairs={{0,8},{4,12},{8,0},{12,4},{16,24},{20,28},{24,16},{28,20},{32,40},... | collective-permute-start | bytes 663560 | tf_op jit(solution)/shard_map/ppermute | solution.py:363
  64.2 2.4 %backward.5.refs_1_ = f32[256,128]{1,0:T(8,128)S(1)} custom-call(bf16[1024,128]{1,0:T(8,128)(2,1)S(1)} %get-tuple-element.55.grad_ref, s32[27,1024]{1,0:T(8,128)S(1)} %bitcast.51, bf16[27,128,128]{2,1,0:T(8,128)(2,1)S(1)} %bitcast.39), custom_call_target="tpu_custom_call" | custom-call | flops 3000000000 | bytes 2000000 | tf_op jit(solution)/shard_map/backward/pallas_call | solution.py:444
  66.7 3.3 %collective-permute-done.11 = bf16[2,432,128]{2,1,0:T(8,128)(2,1)S(1)} collective-permute-done((bf16[2,432,128]{2,1,0:T(8,128)(2,1)S(1)}, bf16[2,432,128]{2,1,0:T(8,128)(2,1)S(1)}, u32[]{:S(2)}, u32[]{:S(2)}) %collective-permute-start.11) | collective-permute-done | bytes 221216 | tf_op jit(solution)/shard_map/ppermute | solution.py:363
  70.0 0.1 fusion.1
  70.0 0.8 collective-permute-start.12
  70.8 2.4 %backward.6.refs_2_ = f32[256,128]{1,0:T(8,128)S(1)} custom-call(bf16[1024,128]{1,0:T(8,128)(2,1)S(1)} %get-tuple-element.55.grad_ref, s32[27,1024]{1,0:T(8,128)S(1)} %bitcast.52, bf16[27,128,128]{2,1,0:T(8,128)(2,1)S(1)} %bitcast.40), custom_call_target="tpu_custom_call" | custom-call | flops 3000000000 | bytes 2000000 | tf_op jit(solution)/shard_map/backward/pallas_call | solution.py:444
  73.2 2.6 %collective-permute-done.12 = bf16[432,128]{1,0:T(8,128)(2,1)S(1)} collective-permute-done((bf16[432,128]{1,0:T(8,128)(2,1)S(1)}, bf16[432,128]{1,0:T(8,128)(2,1)S(1)}, u32[]{:S(2)}, u32[]{:S(2)}) %collective-permute-start.12) | collective-permute-done | bytes 110624 | tf_op jit(solution)/shard_map/ppermute | solution.py:363
  75.8 0.1 collective-permute-start.13
  75.9 2.5 %backward.7.refs_3_ = f32[256,128]{1,0:T(8,128)S(1)} custom-call(bf16[1024,128]{1,0:T(8,128)(2,1)S(1)} %get-tuple-element.55.grad_ref, s32[27,1024]{1,0:T(8,128)S(1)} %bitcast.53, bf16[27,128,128]{2,1,0:T(8,128)(2,1)S(1)} %bitcast.41), custom_call_target="tpu_custom_call" | custom-call | flops 3000000000 | bytes 2000000 | tf_op jit(solution)/shard_map/backward/pallas_call | solution.py:444
  78.4 1.1 %collective-permute-done.13 = bf16[432,128]{1,0:T(8,128)(2,1)S(1)} collective-permute-done((bf16[432,128]{1,0:T(8,128)(2,1)S(1)}, bf16[432,128]{1,0:T(8,128)(2,1)S(1)}, u32[]{:S(2)}, u32[]{:S(2)}) %collective-permute-start.13) | collective-permute-done | bytes 110624 | tf_op jit(solution)/shard_map/ppermute | solution.py:363
  79.6 1.3 %collective-permute-start.14 = (bf16[432,128]{1,0:T(8,128)(2,1)S(1)}, bf16[432,128]{1,0:T(8,128)(2,1)S(1)}, u32[]{:S(2)}, u32[]{:S(2)}) collective-permute-start(bf16[432,128]{1,0:T(8,128)(2,1)S(1)} %add_convert_fusion.1), channel_id=1, source_target_pairs={{0,64},{4,68},{8,72},{12,76},{16,80},{20,84},{24,88},{28,92},{32,9... | collective-permute-start | bytes 331784 | tf_op jit(solution)/shard_map/ppermute | solution.py:363
  80.8 1.7 %final.1 = (bf16[1024,128]{1,0:T(8,128)(2,1)}, bf16[1024,128]{1,0:T(8,128)(2,1)}) custom-call(f32[256,128]{1,0:T(8,128)S(1)} %backward.4.refs_0_, f32[256,128]{1,0:T(8,128)S(1)} %backward.5.refs_1_, f32[256,128]{1,0:T(8,128)S(1)} %backward.6.refs_2_, f32[256,128]{1,0:T(8,128)S(1)} %backward.7.refs_3_, f32[1152,128]{1,0:T(8,128)S(1)} %get-tuple-element.58.refs_4_, ...), custom_call_target="tpu_custom_call" | custom-call | flops 1000000000 | bytes 3000000 | tf_op jit(solution)/shard_map/final/pallas_call | solution.py:476
  82.5 2.2 %collective-permute-done.14 = bf16[432,128]{1,0:T(8,128)(2,1)S(1)} collective-permute-done((bf16[432,128]{1,0:T(8,128)(2,1)S(1)}, bf16[432,128]{1,0:T(8,128)(2,1)S(1)}, u32[]{:S(2)}, u32[]{:S(2)}) %collective-permute-start.14) | collective-permute-done | bytes 110624 | tf_op jit(solution)/shard_map/ppermute | solution.py:363
  84.8 1.1 %collective-permute-start.15 = (bf16[432,128]{1,0:T(8,128)(2,1)S(1)}, bf16[432,128]{1,0:T(8,128)(2,1)S(1)}, u32[]{:S(2)}, u32[]{:S(2)}) collective-permute-start(bf16[432,128]{1,0:T(8,128)(2,1)S(1)} %add_convert_fusion.own_ref), channel_id=1, source_target_pairs={{0,16},{4,20},{8,24},{12,28},{16,0},{20,4},{24,8},{28,12},{32,48},... | collective-permute-start | bytes 331784 | tf_op jit(solution)/shard_map/ppermute | solution.py:363
  85.9 4.1 %collective-permute-done.15.one_ref = bf16[432,128]{1,0:T(8,128)(2,1)S(1)} collective-permute-done((bf16[432,128]{1,0:T(8,128)(2,1)S(1)}, bf16[432,128]{1,0:T(8,128)(2,1)S(1)}, u32[]{:S(2)}, u32[]{:S(2)}) %collective-permute-start.15) | collective-permute-done | bytes 110624 | tf_op jit(solution)/shard_map/ppermute | solution.py:363
  90.0 1.0 collective-permute-start.16
  91.0 4.2 %collective-permute-done.16.two_ref = bf16[2,432,128]{2,1,0:T(8,128)(2,1)S(1)} collective-permute-done((bf16[2,432,128]{2,1,0:T(8,128)(2,1)S(1)}, bf16[2,432,128]{2,1,0:T(8,128)(2,1)S(1)}, u32[]{:S(2)}, u32[]{:S(2)}) %collective-permute-start.16) | collective-permute-done | bytes 221216 | tf_op jit(solution)/shard_map/ppermute | solution.py:363
  95.3 6.7 %collective-permute-start.17 = (bf16[4,432,128]{2,1,0:T(8,128)(2,1)S(1)}, bf16[4,432,128]{2,1,0:T(8,128)(2,1)S(1)}, u32[]{:S(2)}, u32[]{:S(2)}) collective-permute-start(bf16[4,432,128]{2,1,0:T(8,128)(2,1)S(1)} %pad_maximum_fusion), channel_id=1, source_target_pairs={{0,4},{4,0},{8,12},{12,8},{16,20},{20,16},{24,28},{28,24},{32,36},... | collective-permute-start | bytes 1327112 | tf_op jit(solution)/shard_map/ppermute | solution.py:363
  102.0 0.1 pad_add_fusion.1.bits_ref
  102.1 1.3 %collective-permute-done.17.four_ref = bf16[4,432,128]{2,1,0:T(8,128)(2,1)S(1)} collective-permute-done((bf16[4,432,128]{2,1,0:T(8,128)(2,1)S(1)}, bf16[4,432,128]{2,1,0:T(8,128)(2,1)S(1)}, u32[]{:S(2)}, u32[]{:S(2)}) %collective-permute-start.17) | collective-permute-done | bytes 442400 | tf_op jit(solution)/shard_map/ppermute | solution.py:363
  103.4 1.9 %assemble.1 = f32[8,432,128]{2,1,0:T(8,128)} custom-call(s32[3]{0:T(128)S(1)} %pad_add_fusion.1.bits_ref, bf16[432,128]{1,0:T(8,128)(2,1)S(1)} %add_convert_fusion.own_ref, bf16[432,128]{1,0:T(8,128)(2,1)S(1)} %collective-permute-done.15.one_ref, bf16[2,432,128]{2,1,0:T(8,128)(2,1)S(1)} %collective-permute-done.16.two_ref, ...), custom_call_target="tpu_custom_call" | custom-call | flops 1000000 | bytes 3000000 | tf_op jit(solution)/shard_map/assemble/pallas_call | solution.py:487
  (26 shorter events, 0.3 us)
Async XLA Ops:
  1.4 1.2 %copy-start = (bf16[1,27,128,128]{3,2,1,0:T(8,128)(2,1)S(1)}, bf16[1,27,128,128]{3,2,1,0:T(8,128)(2,1)}, u32[]{:S(2)}) copy-start(bf16[1,27,128,128]{3,2,1,0:T(8,128)(2,1)} %param.7) | copy-start | bytes 2654212
  2.6 0.9 copy-start.3
  3.6 0.9 copy-start.5
  4.5 9.8 %copy-start.2 = (bf16[1,1024,128]{2,1,0:T(8,128)(2,1)S(1)}, bf16[1,1024,128]{2,1,0:T(8,128)(2,1)}, u32[]{:S(2)}) copy-start(bf16[1,1024,128]{2,1,0:T(8,128)(2,1)} %param.8) | copy-start | bytes 786436
  4.5 19.3 %copy-start.1 = (bf16[1,27,128,128]{3,2,1,0:T(8,128)(2,1)S(1)}, bf16[1,27,128,128]{3,2,1,0:T(8,128)(2,1)}, u32[]{:S(2)}) copy-start(bf16[1,27,128,128]{3,2,1,0:T(8,128)(2,1)} %param.7) | copy-start | bytes 2654212
  4.5 19.3 %copy-start.4 = (bf16[1,1024,128]{2,1,0:T(8,128)(2,1)S(1)}, bf16[1,1024,128]{2,1,0:T(8,128)(2,1)}, u32[]{:S(2)}) copy-start(bf16[1,1024,128]{2,1,0:T(8,128)(2,1)} %param.6) | copy-start | bytes 786436
  4.5 19.3 %copy-start.7 = (s32[1024,27]{0,1:T(8,128)S(1)}, s32[1024,27]{0,1:T(8,128)}, u32[]{:S(2)}) copy-start(s32[1024,27]{0,1:T(8,128)} %param.9) | copy-start | bytes 331780
  9.5 1.5 %copy-start.8 = (bf16[4,1152,256]{2,1,0:T(8,128)(2,1)}, bf16[4,1152,256]{2,1,0:T(8,128)(2,1)S(1)}, u32[]{:S(2)}) copy-start(bf16[4,1152,256]{2,1,0:T(8,128)(2,1)S(1)} %get-tuple-element.43.face_g_ref) | copy-start | bytes 7077892
  11.0 0.7 copy-start.9
  11.7 3.9 %collective-permute-start = (bf16[320,128]{1,0:T(8,128)(2,1)S(1)}, bf16[320,128]{1,0:T(8,128)(2,1)S(1)}, u32[]{:S(2)}, u32[]{:S(2)}) collective-permute-start(bf16[320,128]{1,0:T(8,128)(2,1)S(1)} %get-tuple-element.34), channel_id=1, source_target_pairs={{0,4},{4,0},{8,12},{12,8},{16,20},{20,16},{24,28},{28,24},{32,36},... | collective-permute-start | bytes 245768 | tf_op jit(solution)/shard_map/ppermute | solution.py:346
  13.1 4.1 %collective-permute-start.1 = (bf16[320,128]{1,0:T(8,128)(2,1)S(1)}, bf16[320,128]{1,0:T(8,128)(2,1)S(1)}, u32[]{:S(2)}, u32[]{:S(2)}) collective-permute-start(bf16[320,128]{1,0:T(8,128)(2,1)S(1)} %get-tuple-element.35), channel_id=1, source_target_pairs={{0,12},{4,8},{8,4},{12,0},{16,28},{20,24},{24,20},{28,16},{32,44},... | collective-permute-start | bytes 245768 | tf_op jit(solution)/shard_map/ppermute | solution.py:346
  14.3 20.3 %collective-permute-start.4 = (bf16[1024,128]{1,0:T(8,128)(2,1)S(1)}, bf16[1024,128]{1,0:T(8,128)(2,1)S(1)}, u32[]{:S(2)}, u32[]{:S(2)}) collective-permute-start(bf16[1024,128]{1,0:T(8,128)(2,1)S(1)} %bitcast.42), channel_id=1, source_target_pairs={{0,1},{1,0},{2,3},{3,2},{4,5},{5,4},{6,7},{7,6},{8,9},{9,8},{10,11... | collective-permute-start | bytes 786440 | tf_op jit(solution)/shard_map/ppermute | solution.py:359
  17.2 17.4 %collective-permute-start.2 = (bf16[320,128]{1,0:T(8,128)(2,1)S(1)}, bf16[320,128]{1,0:T(8,128)(2,1)S(1)}, u32[]{:S(2)}, u32[]{:S(2)}) collective-permute-start(bf16[320,128]{1,0:T(8,128)(2,1)S(1)} %pad_maximum_fusion.2), channel_id=1, source_target_pairs={{0,16},{4,20},{8,24},{12,28},{16,0},{20,4},{24,8},{28,12},{32,48},... | collective-permute-start | bytes 245768 | tf_op jit(solution)/shard_map/ppermute | solution.py:355
  20.1 14.5 %collective-permute-start.3 = (bf16[320,128]{1,0:T(8,128)(2,1)S(1)}, bf16[320,128]{1,0:T(8,128)(2,1)S(1)}, u32[]{:S(2)}, u32[]{:S(2)}) collective-permute-start(bf16[320,128]{1,0:T(8,128)(2,1)S(1)} %pad_maximum_fusion.3), channel_id=1, source_target_pairs={{0,112},{4,116},{8,120},{12,124},{16,32},{20,36},{24,40},{28,44},{... | collective-permute-start | bytes 245768 | tf_op jit(solution)/shard_map/ppermute | solution.py:355
  37.2 3.6 %collective-permute-start.5 = (bf16[320,128]{1,0:T(8,128)(2,1)S(1)}, bf16[320,128]{1,0:T(8,128)(2,1)S(1)}, u32[]{:S(2)}, u32[]{:S(2)}) collective-permute-start(bf16[320,128]{1,0:T(8,128)(2,1)S(1)} %get-tuple-element.39), channel_id=1, source_target_pairs={{0,4},{4,0},{8,12},{12,8},{16,20},{20,16},{24,28},{28,24},{32,36},... | collective-permute-start | bytes 245768 | tf_op jit(solution)/shard_map/ppermute | solution.py:346
  37.9 12.0 %collective-permute-start.9 = (bf16[1024,128]{1,0:T(8,128)(2,1)S(1)}, bf16[1024,128]{1,0:T(8,128)(2,1)S(1)}, u32[]{:S(2)}, u32[]{:S(2)}) collective-permute-start(bf16[1024,128]{1,0:T(8,128)(2,1)S(1)} %get-tuple-element.45.refs_6_), channel_id=1, source_target_pairs={{0,1},{1,0},{2,3},{3,2},{4,5},{5,4},{6,7},{7,6},{8,9},{9,8},{10,11... | collective-permute-start | bytes 786440 | tf_op jit(solution)/shard_map/ppermute | solution.py:359
  39.2 4.7 %collective-permute-start.6 = (bf16[320,128]{1,0:T(8,128)(2,1)S(1)}, bf16[320,128]{1,0:T(8,128)(2,1)S(1)}, u32[]{:S(2)}, u32[]{:S(2)}) collective-permute-start(bf16[320,128]{1,0:T(8,128)(2,1)S(1)} %get-tuple-element.40), channel_id=1, source_target_pairs={{0,12},{4,8},{8,4},{12,0},{16,28},{20,24},{24,20},{28,16},{32,44},... | collective-permute-start | bytes 245768 | tf_op jit(solution)/shard_map/ppermute | solution.py:346
  43.9 7.7 %collective-permute-start.8 = (bf16[320,128]{1,0:T(8,128)(2,1)S(1)}, bf16[320,128]{1,0:T(8,128)(2,1)S(1)}, u32[]{:S(2)}, u32[]{:S(2)}) collective-permute-start(bf16[320,128]{1,0:T(8,128)(2,1)S(1)} %pad_maximum_fusion.5), channel_id=1, source_target_pairs={{0,112},{4,116},{8,120},{12,124},{16,32},{20,36},{24,40},{28,44},{... | collective-permute-start | bytes 245768 | tf_op jit(solution)/shard_map/ppermute | solution.py:355
  45.4 6.2 %collective-permute-start.7 = (bf16[320,128]{1,0:T(8,128)(2,1)S(1)}, bf16[320,128]{1,0:T(8,128)(2,1)S(1)}, u32[]{:S(2)}, u32[]{:S(2)}) collective-permute-start(bf16[320,128]{1,0:T(8,128)(2,1)S(1)} %pad_maximum_fusion.4), channel_id=1, source_target_pairs={{0,16},{4,20},{8,24},{12,28},{16,0},{20,4},{24,8},{28,12},{32,48},... | collective-permute-start | bytes 245768 | tf_op jit(solution)/shard_map/ppermute | solution.py:355
  45.4 6.2 %copy-start.6 = (s32[1152,27]{0,1:T(8,128)S(1)}, s32[1152,27]{0,1:T(8,128)}, u32[]{:S(2)}) copy-start(s32[1152,27]{0,1:T(8,128)} %param.10) | copy-start | bytes 373252
  45.4 6.2 %copy-start.10 = (bf16[1536,128]{1,0:T(8,128)(2,1)S(1)}, bf16[1536,128]{1,0:T(8,128)(2,1)}, u32[]{:S(2)}) copy-start(bf16[1536,128]{1,0:T(8,128)(2,1)} %copy-done.9) | copy-start | bytes 1179652
  57.8 3.5 %collective-permute-start.10 = (bf16[2,2,432,128]{3,2,1,0:T(8,128)(2,1)}, bf16[2,2,432,128]{3,2,1,0:T(8,128)(2,1)}, u32[]{:S(2)}, u32[]{:S(2)}) collective-permute-start(bf16[2,2,432,128]{3,2,1,0:T(8,128)(2,1)} %dynamic-slice_bitcast_fusion), channel_id=1, source_target_pairs={{0,4},{4,0},{8,12},{12,8},{16,20},{20,16},{24,28},{28,24},{32,36},... | collective-permute-start | bytes 1327112 | tf_op jit(solution)/shard_map/ppermute | solution.py:363
  62.5 7.5 %collective-permute-start.11 = (bf16[2,432,128]{2,1,0:T(8,128)(2,1)S(1)}, bf16[2,432,128]{2,1,0:T(8,128)(2,1)S(1)}, u32[]{:S(2)}, u32[]{:S(2)}) collective-permute-start(bf16[2,432,128]{2,1,0:T(8,128)(2,1)S(1)} %dynamic-slice_bitcast_fusion.1), channel_id=1, source_target_pairs={{0,8},{4,12},{8,0},{12,4},{16,24},{20,28},{24,16},{28,20},{32,40},... | collective-permute-start | bytes 663560 | tf_op jit(solution)/shard_map/ppermute | solution.py:363
  70.0 5.8 %collective-permute-start.12 = (bf16[432,128]{1,0:T(8,128)(2,1)S(1)}, bf16[432,128]{1,0:T(8,128)(2,1)S(1)}, u32[]{:S(2)}, u32[]{:S(2)}) collective-permute-start(bf16[432,128]{1,0:T(8,128)(2,1)S(1)} %dynamic-slice_bitcast_fusion.2), channel_id=1, source_target_pairs={{0,16},{4,20},{8,24},{12,28},{16,0},{20,4},{24,8},{28,12},{32,48},... | collective-permute-start | bytes 331784 | tf_op jit(solution)/shard_map/ppermute | solution.py:363
  75.8 3.7 %collective-permute-start.13 = (bf16[432,128]{1,0:T(8,128)(2,1)S(1)}, bf16[432,128]{1,0:T(8,128)(2,1)S(1)}, u32[]{:S(2)}, u32[]{:S(2)}) collective-permute-start(bf16[432,128]{1,0:T(8,128)(2,1)S(1)} %fusion.2), channel_id=1, source_target_pairs={{0,32},{4,36},{8,40},{12,44},{16,48},{20,52},{24,56},{28,60},{32,0... | collective-permute-start | bytes 331784 | tf_op jit(solution)/shard_map/ppermute | solution.py:363
  79.6 5.2 %collective-permute-start.14 = (bf16[432,128]{1,0:T(8,128)(2,1)S(1)}, bf16[432,128]{1,0:T(8,128)(2,1)S(1)}, u32[]{:S(2)}, u32[]{:S(2)}) collective-permute-start(bf16[432,128]{1,0:T(8,128)(2,1)S(1)} %add_convert_fusion.1), channel_id=1, source_target_pairs={{0,64},{4,68},{8,72},{12,76},{16,80},{20,84},{24,88},{28,92},{32,9... | collective-permute-start | bytes 331784 | tf_op jit(solution)/shard_map/ppermute | solution.py:363
  84.8 5.2 %collective-permute-start.15 = (bf16[432,128]{1,0:T(8,128)(2,1)S(1)}, bf16[432,128]{1,0:T(8,128)(2,1)S(1)}, u32[]{:S(2)}, u32[]{:S(2)}) collective-permute-start(bf16[432,128]{1,0:T(8,128)(2,1)S(1)} %add_convert_fusion.own_ref), channel_id=1, source_target_pairs={{0,16},{4,20},{8,24},{12,28},{16,0},{20,4},{24,8},{28,12},{32,48},... | collective-permute-start | bytes 331784 | tf_op jit(solution)/shard_map/ppermute | solution.py:363
  90.0 5.3 %collective-permute-start.16 = (bf16[2,432,128]{2,1,0:T(8,128)(2,1)S(1)}, bf16[2,432,128]{2,1,0:T(8,128)(2,1)S(1)}, u32[]{:S(2)}, u32[]{:S(2)}) collective-permute-start(bf16[2,432,128]{2,1,0:T(8,128)(2,1)S(1)} %pad_maximum_fusion.1), channel_id=1, source_target_pairs={{0,8},{4,12},{8,0},{12,4},{16,24},{20,28},{24,16},{28,20},{32,40},... | collective-permute-start | bytes 663560 | tf_op jit(solution)/shard_map/ppermute | solution.py:363
  95.3 8.1 %collective-permute-start.17 = (bf16[4,432,128]{2,1,0:T(8,128)(2,1)S(1)}, bf16[4,432,128]{2,1,0:T(8,128)(2,1)S(1)}, u32[]{:S(2)}, u32[]{:S(2)}) collective-permute-start(bf16[4,432,128]{2,1,0:T(8,128)(2,1)S(1)} %pad_maximum_fusion), channel_id=1, source_target_pairs={{0,4},{4,0},{8,12},{12,8},{16,20},{20,16},{24,28},{28,24},{32,36},... | collective-permute-start | bytes 1327112 | tf_op jit(solution)/shard_map/ppermute | solution.py:363

commit v3 on v2

v3 whole, which is shorter than its diff:
```python
import functools

import jax
import jax.numpy as jnp
from jax import lax
from jax.experimental import pallas as pl
from jax.experimental.pallas import tpu as pltpu
from jax.sharding import PartitionSpec as P

TZ = 32
TILES_X = 4
CAP = 256
ROWS = 1024
C = 128
HALO = 1152

DIRECTIONS = ((-1, -1), (-1, 0), (-1, 1), (0, -1), (0, 1), (1, -1), (1, 0), (1, 1))
BF = jnp.bfloat16
F32 = jnp.float32


def spans():
    result = []
    start = 0
    for step_x, step_y in DIRECTIONS:
        length = TZ if step_x != 0 and step_y != 0 else CAP
        result.append((start, length))
        start = start + length
    return result


SPANS = spans()
FACES = [n for n, (a, b) in enumerate(DIRECTIONS) if a == 0 or b == 0]
CORNERS = [n for n, (a, b) in enumerate(DIRECTIONS) if a != 0 and b != 0]


def toward(step_x, step_y):
    picked = []
    for offset in range(27):
        along_x = offset // 9 - 1
        along_y = offset // 3 % 3 - 1
        if (step_x == 0 or along_x == -step_x) and (step_y == 0 or along_y == -step_y):
            picked.append(offset)
    return picked


def dot(a, b, dims=((1,), (0,))):
    return lax.dot_general(a, b, (dims, ((), ())), preferred_element_type=F32)


def hot(row, rows):
    pos = lax.broadcasted_iota(jnp.int32, (256, 128), 0).astype(jnp.int16)
    count = row.shape[1]
    blocks = []
    for base in range(0, rows, 256):
        rel = (row - base).astype(jnp.int16)
        parts = [
            jnp.where(rel[:, t : t + 128] == pos, BF(1), BF(0)) for t in range(0, count, 128)
        ]
        blocks.append(jnp.concatenate(parts, 1))
    return jnp.concatenate(blocks, 0)


def spread(column, count):
    kept = jnp.where(column == ROWS, -1, column)
    return jnp.broadcast_to(kept, (column.shape[0], count)).astype(jnp.int16)


def places_from_one(rows):
    return (lax.broadcasted_iota(jnp.int32, (rows, 128), 0) + 1).astype(BF)


def positions(column, row):
    rows, count = column.shape
    numbers = places_from_one(rows)
    numbers = jnp.concatenate([numbers] * (count // 128), 1)
    found = jnp.where(column == row.astype(jnp.int16), numbers, BF(0))
    while rows > 16:
        rows //= 2
        found = jnp.maximum(found[:rows], found[rows:])
    return jnp.max(found.astype(F32), axis=0, keepdims=True)


def match(row, rows):
    numbers = places_from_one(rows)
    row = row.astype(BF)
    parts = [jnp.where(row[:, t : t + 128] == numbers, BF(1), BF(0)) for t in range(0, row.shape[1], 128)]
    return jnp.concatenate(parts, 1)


def face_rows(block):
    block = block.astype(F32)
    return [jnp.concatenate([block[k : k + 1], block[16 + k : 17 + k]], 1) for k in range(9)]


def column_of(row):
    return jnp.broadcast_to(row.astype(F32), (8, row.shape[1])).T[:, :1].astype(jnp.int32)


def inside(place, axis, dims):
    return (lax.broadcasted_iota(jnp.int32, dims, axis) // TZ) == place


def number_of(step_x, step_y):
    return DIRECTIONS.index((step_x, step_y))


def pack_sides(lists, orient, sides, xa_ref, xb_ref, ya_ref, yb_ref):
    x_odd, y_odd = sides[0] == 1, sides[1] == 1

    def x_side(side):
        picked = [(orient * side, 0), (orient * side, -orient), (orient * side, orient)]
        return jnp.concatenate([lists[number_of(*d)] for d in picked], 0)

    plus, minus = x_side(1), x_side(-1)
    xa_ref[...] = jnp.where(x_odd, minus, plus)
    xb_ref[...] = jnp.where(x_odd, plus, minus)
    plus, minus = lists[number_of(0, orient)], lists[number_of(0, -orient)]
    ya_ref[...] = jnp.where(y_odd, minus, plus)
    yb_ref[...] = jnp.where(y_odd, plus, minus)


def unpack_sides(orient, sides, face, edge, xa, xb, ya, yb):
    x_odd, y_odd = sides[0] == 1, sides[1] == 1

    def of_side(side, odd, a, b):
        return jnp.where(odd, b, a) if side == 1 else jnp.where(odd, a, b)

    lists = []
    for step_x, step_y in DIRECTIONS:
        if step_y == 0:
            lists.append(of_side(-orient * step_x, x_odd, xa[:face], xb[:face]))
        elif step_x == 0:
            lists.append(of_side(-orient * step_y, y_odd, ya[:face], yb[:face]))
        else:
            first = of_side(-orient * step_y, y_odd, ya[face : face + edge], yb[face : face + edge])
            second = of_side(-orient * step_y, y_odd, ya[face + edge :], yb[face + edge :])
            lists.append(of_side(-orient * step_x, x_odd, first, second))
    return lists


def start_kernel(side_ref, x_ref, rr_ref, sm_ref, xa_ref, xb_ref, ya_ref, yb_ref, face_p_ref, edge_p_ref):
    lists = [None] * 8
    row = rr_ref[...]
    column = column_of(row)
    listed = dot(x_ref[...].astype(F32).T.astype(BF), hot(row, ROWS)).T.astype(BF)
    for place, number in enumerate(FACES):
        start, length = SPANS[number]
        other, _ = SPANS[7 - number]
        wide = spread(column[other : other + length], length)
        found = [
            positions(wide, sm_ref[offset : offset + 1, start : start + length])
            for offset in toward(*DIRECTIONS[number])
        ]
        found = jnp.concatenate(found + [jnp.zeros((7, length), F32)], 0)
        found = jnp.concatenate([found[:, :128], found[:, 128:]], 0).astype(BF)
        face_p_ref[place] = found
        lists[number] = jnp.concatenate([listed[other : other + length], found], 0)
    wide = spread(
        jnp.concatenate([column[SPANS[7 - n][0] : SPANS[7 - n][0] + TZ] for n in CORNERS], 0), 4 * TZ
    )
    found = []
    for step in range(3):
        pieces = []
        for number in CORNERS:
            start, length = SPANS[number]
            offset = toward(*DIRECTIONS[number])[step]
            pieces.append(sm_ref[offset : offset + 1, start : start + length])
        found.append(positions(wide, jnp.concatenate(pieces, 1)))
    found = jnp.concatenate(found + [jnp.zeros((13, 4 * TZ), F32)], 0).astype(BF)
    edge_p_ref[...] = found
    for number in CORNERS:
        other, length = SPANS[7 - number]
        lists[number] = jnp.concatenate([listed[other : other + length], found], 0)
    pack_sides(lists, 1, (side_ref[0], side_ref[1]), xa_ref, xb_ref, ya_ref, yb_ref)


def forward_kernel(x_ref, lm_ref, w_ref, g_ref, pre_ref, x_t, total, *, width):
    step = pl.program_id(0)

    @pl.when(step == 0)
    def _():
        x_t[...] = x_ref[...].astype(F32).T.astype(BF)
        total[...] = dot(w_ref[13], x_t[...], ((0,), (0,)))

    source = x_t[...]
    weight = jnp.concatenate([w_ref[14 * step + i] for i in range(13)], 0)
    for begin in range(0, ROWS, width):
        cols = slice(begin, begin + width)
        gathered = [
            dot(source, hot(lm_ref[pl.ds(14 * step + i, 1), cols], ROWS)).astype(BF) for i in range(13)
        ]
        gathered = jnp.concatenate(gathered, 0)
        g_ref[:, cols] = gathered
        total[:, cols] += dot(weight, gathered, ((0,), (0,)))

    @pl.when(step == 1)
    def _():
        pre_ref[...] = total[...].T


def high_low(values):
    high = values.astype(BF)
    return jnp.concatenate([high, (values - high.astype(F32)).astype(BF)], 1)


def activate_kernel(
    side_ref, pre_ref, ixa_ref, ixb_ref, iya_ref, iyb_ref, rr_ref, cot_ref, pair_ref, w_ref,
    act_ref, grad_ref, xa_ref, xb_ref, ya_ref, yb_ref, dw_ref,
):
    sides = (side_ref[0], side_ref[1])
    arrived = unpack_sides(
        1, sides, CAP + 32, TZ + 16, ixa_ref[...], ixb_ref[...], iya_ref[...], iyb_ref[...]
    )
    sums = [None] * 8
    sources = []
    for number in FACES:
        picked = toward(*DIRECTIONS[number])
        source = arrived[number][:CAP].astype(F32).T.astype(BF)
        sources.append(source)
        gathered = [dot(source, match(row, CAP)).astype(BF) for row in face_rows(arrived[number][CAP:])]
        weight = jnp.concatenate([w_ref[offset] for offset in picked], 0)
        sums[number] = dot(weight, jnp.concatenate(gathered, 0), ((0,), (0,))).T
    edge_source = jnp.concatenate([arrived[n][:TZ] for n in CORNERS], 0).astype(F32).T.astype(BF)
    edge_found = jnp.zeros((16, 4 * TZ), F32)
    for place, number in enumerate(CORNERS):
        rows = arrived[number][TZ:].astype(F32)
        edge_found = jnp.where(inside(place, 1, rows.shape), rows, edge_found)
    gathered = [dot(edge_source, match(edge_found[k : k + 1], 4 * TZ)).astype(BF) for k in range(3)]
    masked = []
    weights = []
    for place, number in enumerate(CORNERS):
        for step in range(3):
            masked.append(jnp.where(inside(place, 1, (C, 4 * TZ)), gathered[step], BF(0)))
            weights.append(w_ref[toward(*DIRECTIONS[number])[step]])
    total = dot(jnp.concatenate(weights, 0), jnp.concatenate(masked, 0), ((0,), (0,))).T
    for place, number in enumerate(CORNERS):
        sums[number] = total[place * TZ : (place + 1) * TZ]

    selector = hot(rr_ref[...], ROWS)
    both = dot(selector, high_low(jnp.concatenate(sums, 0)))
    pre = pre_ref[...] + both[:, :C] + both[:, C:]
    gate = 1.0 / (1.0 + jnp.exp(-pre))
    act_ref[...] = (pre * gate).astype(BF)
    upstream = cot_ref[...].astype(F32) + pair_ref[...].astype(F32)
    grad = upstream * gate * (1.0 + pre * (1.0 - gate))
    grad_ref[...] = grad.astype(BF)
    listed = dot(grad.T.astype(BF), selector).T.astype(BF)
    lists = [listed[start : start + length] for start, length in SPANS]
    pack_sides(lists, -1, sides, xa_ref, xb_ref, ya_ref, yb_ref)

    dw_ref[...] = jnp.zeros_like(dw_ref)
    for source, number in zip(sources, FACES):
        pieces = [
            dot(match(row, CAP), lists[number]).astype(BF) for row in face_rows(arrived[number][CAP:])
        ]
        part = dot(source, jnp.concatenate(pieces, 1))
        for index, offset in enumerate(toward(*DIRECTIONS[number])):
            dw_ref[offset] += part[:, index * C : (index + 1) * C]
    back = jnp.concatenate([lists[n] for n in CORNERS], 0)
    spots = [dot(match(edge_found[k : k + 1], 4 * TZ), back).astype(BF) for k in range(3)]
    pieces = [
        jnp.where(inside(place, 0, (4 * TZ, C)), spots[step], BF(0)) for place in range(4) for step in range(3)
    ]
    part = dot(edge_source, jnp.concatenate(pieces, 1))
    for place, number in enumerate(CORNERS):
        for step in range(3):
            index = 3 * place + step
            dw_ref[toward(*DIRECTIONS[number])[step]] += part[:, index * C : (index + 1) * C]


def weight_kernel(g_ref, grad_ref, x_ref, halo_ref, dw_ref):
    step = pl.program_id(0)

    @pl.when(step == 0)
    def _():
        dw_ref[13] = halo_ref[13] + dot(x_ref[...], grad_ref[...], ((0,), (0,)))

    total = dot(g_ref[...], grad_ref[...])
    dw_ref[pl.ds(14 * step, 13)] = halo_ref[pl.ds(14 * step, 13)] + total.reshape(13, C, C)


def return_kernel(side_ref, ixa_ref, ixb_ref, iya_ref, iyb_ref, face_p_ref, edge_p_ref, w_ref, placed_ref):
    sides = (side_ref[0], side_ref[1])
    returned = unpack_sides(-1, sides, CAP, TZ, ixa_ref[...], ixb_ref[...], iya_ref[...], iyb_ref[...])
    for place, number in enumerate(FACES):
        other, length = SPANS[7 - number]
        pieces = [dot(match(row, CAP), returned[number]).astype(BF) for row in face_rows(face_p_ref[place])]
        weight = jnp.concatenate([w_ref[offset] for offset in toward(*DIRECTIONS[number])], 1)
        placed_ref[other : other + length, :] = dot(jnp.concatenate(pieces, 1), weight, ((1,), (1,)))
    back = jnp.concatenate([returned[n] for n in CORNERS], 0)
    found = edge_p_ref[...].astype(F32)
    spots = [dot(match(found[k : k + 1], 4 * TZ), back).astype(BF) for k in range(3)]
    pieces = []
    weights = []
    for place, number in enumerate(CORNERS):
        for step in range(3):
            pieces.append(jnp.where(inside(place, 0, (4 * TZ, C)), spots[step], BF(0)))
            weights.append(w_ref[toward(*DIRECTIONS[number])[step]])
    result = dot(jnp.concatenate(pieces, 1), jnp.concatenate(weights, 1), ((1,), (1,)))
    for place, number in enumerate(CORNERS):
        other, length = SPANS[7 - number]
        placed_ref[other : other + length, :] = result[place * TZ : (place + 1) * TZ, :]


def backward_kernel(grad_ref, lm_ref, w_ref, out_ref, *, begin):
    size = out_ref.shape[0]
    source = grad_ref[...].astype(F32).T.astype(BF)
    gathered = []
    for k in range(27):
        if k == 13:
            gathered.append(source[:, begin : begin + size])
        else:
            gathered.append(dot(source, hot(lm_ref[26 - k : 27 - k, begin : begin + size], ROWS)).astype(BF))
    weight = jnp.concatenate([w_ref[k] for k in range(27)], 1)
    out_ref[...] = dot(weight, jnp.concatenate(gathered, 0)).T


def final_kernel(*refs):
    placed_ref, rr_ref, act_ref, pair_ref, mixed_ref, out_ref = refs[-6:]
    both = dot(hot(rr_ref[...], ROWS), high_low(placed_ref[...]))
    both = both[:, :C] + both[:, C:]
    size = ROWS // len(refs[:-6])
    for index, ref in enumerate(refs[:-6]):
        rows = slice(index * size, (index + 1) * size)
        out_ref[rows, :] = (ref[...] + both[rows]).astype(BF)
    mixed_ref[...] = (act_ref[...].astype(F32) + pair_ref[...].astype(F32)).astype(BF)


def assemble_kernel(bits_ref, own_ref, one_ref, two_ref, four_ref, out_ref):
    place = bits_ref[0] * 4 + bits_ref[1] * 2 + bits_ref[2]
    blocks = [own_ref[...], one_ref[...]] + [two_ref[i] for i in range(2)] + [four_ref[i] for i in range(4)]
    for distance, block in enumerate(blocks):
        out_ref[place ^ distance] = block.astype(F32)


PARAMS = pltpu.CompilerParams(vmem_limit_bytes=48 * 2**20)


def shape(dims, dtype):
    return jax.ShapeDtypeStruct(dims, dtype)


def whole(dims):
    return pl.BlockSpec(dims, lambda *ids: (0,) * len(dims))


def pairing(axis, which):
    pairs = []
    for tile in range(lax.axis_size("space")):
        at_x, at_y = tile % TILES_X, tile // TILES_X
        tiles_y = lax.axis_size("space") // TILES_X
        if axis == "x":
            move = 1 if (at_x + which) % 2 == 0 else -1
            at_x = (at_x + move) % TILES_X
        else:
            move = 1 if (at_y + which) % 2 == 0 else -1
            at_y = (at_y + move) % tiles_y
        pairs.append((tile, at_y * TILES_X + at_x))
    return pairs


def exchange_x(xa, xb):
    return [lax.ppermute(v, "space", pairing("x", n)) for n, v in enumerate((xa, xb))]


def exchange_y(ya, yb, xa, xb, sides, face, edge):
    sent = []
    for which, own in enumerate((ya, yb)):
        down = sides[1] != which
        corners = [jnp.where(down, v[face : face + edge], v[face + edge :]) for v in (xa, xb)]
        sent.append(jnp.concatenate([own] + corners, 0))
    return [lax.ppermute(v, "space", pairing("y", n)) for n, v in enumerate(sent)]


def swapped(array):
    return lax.ppermute(array, "segment", [(i, i ^ 1) for i in range(lax.axis_size("segment"))])


def xor_send(value, bits):
    return lax.ppermute(value, "space", [(i, i ^ bits) for i in range(lax.axis_size("space"))])


def pick(array, index):
    return lax.dynamic_index_in_dim(array, index, 0, False)


def cost(flops, data):
    return pl.CostEstimate(flops=int(flops), bytes_accessed=int(data), transcendentals=0)


def tie(value, other):
    return lax.optimization_barrier((value, other))[0]


def on_device(features, weights, cotangent, local_map, send_map, recv_map):
    x = features[0]
    w = weights[0]
    cot = cotangent[0]
    lm = local_map.T
    sm = send_map.T
    rr = recv_map.reshape(1, HALO)
    me = lax.axis_index("space")
    sides = jnp.stack([me % 2, me // TILES_X % 2]).astype(jnp.int32)
    smem = pl.BlockSpec(memory_space=pltpu.SMEM)
    vmem = pl.BlockSpec(memory_space=pltpu.VMEM)
    def lists_shape(face, edge):
        return [shape((face + 2 * edge, C), BF)] * 2 + [shape((face, C), BF)] * 2

    xa, xb, ya, yb, face_p, edge_p = pl.pallas_call(
        start_kernel,
        in_specs=[smem] + [vmem] * 3,
        out_shape=lists_shape(CAP + 32, TZ + 16) + [shape((4, 32, C), BF), shape((16, C), BF)],
        compiler_params=PARAMS,
        cost_estimate=cost(2e9, 4e6),
        name="start",
    )(sides, x, rr, sm)
    cot_pair = swapped(cot)
    in_x = exchange_x(xa, xb)
    in_y = exchange_y(ya, yb, *in_x, sides, CAP + 32, TZ + 16)
    gathered, pre = pl.pallas_call(
        functools.partial(forward_kernel, width=512),
        grid=(2,),
        in_specs=[whole((ROWS, C)), whole((27, ROWS)), whole((27, C, C))],
        out_specs=[pl.BlockSpec((13 * C, ROWS), lambda j: (j, 0)), whole((ROWS, C))],
        out_shape=[shape((26 * C, ROWS), BF), shape((ROWS, C), F32)],
        scratch_shapes=[pltpu.VMEM((C, ROWS), BF), pltpu.VMEM((C, ROWS), F32)],
        compiler_params=PARAMS,
        cost_estimate=cost(15e9, 9e6),
        name="forward",
    )(x, lm, w)
    act, grad, xa, xb, ya, yb, dw_halo = pl.pallas_call(
        activate_kernel,
        in_specs=[smem] + [vmem] * 9,
        out_shape=[shape((ROWS, C), BF)] * 2 + lists_shape(CAP, TZ) + [shape((27, C, C), F32)],
        compiler_params=PARAMS,
        cost_estimate=cost(4e9, 3e6),
        name="activate",
    )(sides, pre, *in_x, *in_y, rr, cot, cot_pair, w)
    dw = pl.pallas_call(
        weight_kernel,
        grid=(2,),
        in_specs=[pl.BlockSpec((13 * C, ROWS), lambda j: (j, 0)), whole((ROWS, C)), whole((ROWS, C)), whole((27, C, C))],
        out_specs=whole((27, C, C)),
        out_shape=shape((27, C, C), F32),
        compiler_params=PARAMS,
        cost_estimate=cost(4e9, 9e6),
        name="weight",
    )(gathered, grad, x, dw_halo)

    size = ROWS // 4

    def backward(index, grad):
        return pl.pallas_call(
            functools.partial(backward_kernel, begin=index * size),
            out_shape=shape((size, C), F32),
            compiler_params=PARAMS,
            cost_estimate=cost(3e9, 2e6),
            name="backward",
        )(grad, lm, w)

    bits = [me % 2, me // 2 % 2, me // 8 % 2]
    blocks = dw.reshape(2, 2, 2, -1, C)

    def halve(blocks, stage):
        sent = pick(blocks, 1 - bits[stage]).astype(BF)
        return pick(blocks, bits[stage]), sent

    kept, sent = halve(blocks, 0)
    got = xor_send(sent, 1)
    in_x = exchange_x(tie(xa, sent), tie(xb, sent))
    locals_ = [backward(0, tie(grad, sent))]
    blocks = kept + tie(got, locals_[0]).astype(F32)

    kept, sent = halve(blocks, 1)
    got = xor_send(sent, 2)
    in_y = exchange_y(tie(ya, sent), tie(yb, sent), *in_x, sides, CAP, TZ)
    locals_.append(backward(1, tie(grad, sent)))
    blocks = kept + tie(got, locals_[1]).astype(F32)

    kept, sent = halve(blocks, 2)
    got = xor_send(sent, 8)
    placed = pl.pallas_call(
        return_kernel,
        in_specs=[smem] + [vmem] * 7,
        out_shape=shape((HALO, C), F32),
        compiler_params=PARAMS,
        cost_estimate=cost(3e9, 4e6),
        name="returning",
    )(sides, *in_x, *in_y, face_p, edge_p, tie(w, sent))
    own = (kept + tie(got, placed).astype(F32)).astype(BF)

    got = xor_send(own, 4)
    locals_.append(backward(2, tie(grad, own)))
    own = (own.astype(F32) + tie(got, locals_[2]).astype(F32)).astype(BF)
    got = xor_send(own, 16)
    act_pair = swapped(tie(act, own))
    locals_.append(backward(3, tie(grad, own)))
    own = (own.astype(F32) + tie(got, locals_[3]).astype(F32)).astype(BF)
    one = xor_send(own, 8)
    mixed, input_grad = pl.pallas_call(
        final_kernel,
        out_shape=[shape((ROWS, C), BF), shape((ROWS, C), BF)],
        compiler_params=PARAMS,
        cost_estimate=cost(1e9, 3e6),
        name="final",
    )(*locals_, tie(placed, own), rr, act, act_pair)
    one = tie(one, input_grad)
    two = xor_send(jnp.stack([own, one]), 2)
    four = xor_send(jnp.concatenate([jnp.stack([own, one]), two], 0), 1)
    weight_grad = pl.pallas_call(
        assemble_kernel,
        in_specs=[smem] + [vmem] * 4,
        out_shape=shape((8,) + own.shape, F32),
        compiler_params=PARAMS,
        cost_estimate=cost(1e6, 3e6),
        name="assemble",
    )(jnp.stack(bits).astype(jnp.int32), own, one, two, four)
    return (mixed[None], input_grad[None], weight_grad.reshape(dw.shape)[None])


def solution(mesh):
    in_specs = (
        P("segment", "space", None),
        P("segment", None, None, None),
        P("segment", "space", None),
        P("space", None),
        P("space", None),
        P("space"),
    )
    out_specs = (
        P("segment", "space", None),
        P("segment", "space", None),
        P("segment", None, None, None),
    )
    return jax.shard_map(
        on_device, mesh=mesh, in_specs=in_specs, out_specs=out_specs, check_vma=False
    )
```

time: 106 us -> 89.2 us (0.84)
  waiting for transfers between devices: 25.4 us -> 16.8 us
  local copies, waits for them, and re-layouts: 6.82 us -> 2.7 us
  starting transfers between devices: 29.3 us -> 27.6 us
  other arithmetic: 1.56 us -> 0.49 us
    ppermute x8, waiting for transfers between devices: 18.9 us -> 9.73 us  [xor_send(): lax.ppermute(value, 'space', [(i, i ^ bits) for i in range(lax.axis_size(...]
    unnamed x22 -> x12, local copies, waits for them, and re-layouts: 5.27 us -> 1.87 us
    ppermute x4, waiting for transfers between devices: 4.72 us -> 2.99 us  [exchange_x(): lax.ppermute(v, 'space', pairing('x', n))]
    ppermute x8, starting transfers between devices: 13.7 us -> 12.4 us  [xor_send(): lax.ppermute(value, 'space', [(i, i ^ bits) for i in range(lax.axis_size(...]
    ppermute x2, waiting for transfers between devices: 0.01 us -> 1.33 us  [swapped(): lax.ppermute(array, 'segment', [(i, i ^ 1) for i in range(lax.axis_size('...]
    convert_element_type x5 -> x3, other arithmetic: 1.3 us -> 0.1 us  [the longest x1 0.03 us: on_device(): own = (own.astype(F32) + tie(got, locals_[3]).astype(F32)).astype(BF)]
  transfers between devices with their start and end apart: 18 -> 18, of which waited for: 10 -> 11; matrix products, arithmetic and copies ran while one was open for 0% -> 0% of each run, Pallas kernels for 25% -> 28%
where the time goes in v3:
time: 89.2 us; the launch traced here: 89 us
  Pallas kernels  40.6 us (46%)
  starting transfers between devices  27.6 us (31%)
  waiting for transfers between devices  16.8 us (19%)
  local copies, waits for them, and re-layouts  2.7 us (3%)
    ppermute x8, starting transfers between devices, xor_send(): lax.ppermute(value, 'space', [(i, i ^ bits) for i in range(lax.axis_size(...  12.4 us
    pallas_call x1, Pallas kernels, on_device(): pl.pallas_call(functools.partial(forward_kernel, width=512), grid=(2,), i...  10.8 us
    pallas_call x4, Pallas kernels, backward(): pl.pallas_call(functools.partial(backward_kernel, begin=index * size), ou...  9.79 us
    ppermute x8, waiting for transfers between devices, xor_send(): lax.ppermute(value, 'space', [(i, i ^ bits) for i in range(lax.axis_size(...  9.73 us
    ppermute x4, starting transfers between devices, exchange_y(): lax.ppermute(v, 'space', pairing('y', n))  8.21 us
    pallas_call x1, Pallas kernels, on_device(): pl.pallas_call(activate_kernel, in_specs=[smem] + [vmem] * 9, out_shape=[...  6.77 us
    ppermute x4, starting transfers between devices, exchange_x(): lax.ppermute(v, 'space', pairing('x', n))  4.47 us
    pallas_call x1, Pallas kernels, on_device(): pl.pallas_call(weight_kernel, grid=(2,), in_specs=[pl.BlockSpec((13 * C,...  4.4 us
  transfers between devices with their start and end apart: 18, of which 11 were waited for; matrix products, arithmetic and copies ran while one was open for 0% of the time, Pallas kernels for 28%

profile of v3, /device:TPU:1, one launch (start us, length us, event | category | flops | bytes accessed | tf_op | source)
XLA Modules:
  0.0 89.0 jit_solution(10295397267251837207)
XLA Ops:
  0.7 0.7 reshape.15.rr_ref.refs_5_
  1.4 0.1 pad_add_fusion.side_ref
  1.4 0.0 copy-start.2
  1.4 0.9 %copy-done.2 = bf16[1,1024,128]{2,1,0:T(8,128)(2,1)S(1)} copy-done((bf16[1,1024,128]{2,1,0:T(8,128)(2,1)S(1)}, bf16[1,1024,128]{2,1,0:T(8,128)(2,1)}, u32[]{:S(2)}) %copy-start.2) | copy-done | bytes 262168
  2.4 0.0 copy-start.4
  2.4 0.9 %copy-done.4 = s32[1152,27]{0,1:T(8,128)S(1)} copy-done((s32[1152,27]{0,1:T(8,128)S(1)}, s32[1152,27]{0,1:T(8,128)}, u32[]{:S(2)}) %copy-start.4) | copy-done | bytes 124440
  3.3 0.0 copy-start.1
  3.3 0.0 copy-start
  3.3 0.0 copy-start.3
  3.3 0.0 copy-start.5
  3.3 2.3 %start.1 = (bf16[384,128]{1,0:T(8,128)(2,1)S(1)}, bf16[384,128]{1,0:T(8,128)(2,1)S(1)}, bf16[288,128]{1,0:T(8,128)(2,1)S(1)}, bf16[288,128]{1,0:T(8,128)(2,1)S(1...) custom-call(s32[2]{0:T(128)S(1)} %pad_add_fusion.side_ref, bf16[1024,128]{1,0:T(8,128)(2,1)S(1)} %bitcast.44, ...), custom_call_target="tpu_custom_call" | custom-call | flops 2000000000 | bytes 4000000 | tf_op jit(solution)/shard_map/start/pallas_call | solution.py:410
  5.6 1.5 %collective-permute-start = (bf16[384,128]{1,0:T(8,128)(2,1)S(1)}, bf16[384,128]{1,0:T(8,128)(2,1)S(1)}, u32[]{:S(2)}, u32[]{:S(2)}) collective-permute-start(bf16[384,128]{1,0:T(8,128)(2,1)S(1)} %get-tuple-element.38), channel_id=1, source_target_pairs={{0,4},{4,0},{8,12},{12,8},{16,20},{20,16},{24,28},{28,24},{32,36},... | collective-permute-start | bytes 294920 | tf_op jit(solution)/shard_map/ppermute | solution.py:364
  7.1 1.3 %collective-permute-start.1 = (bf16[384,128]{1,0:T(8,128)(2,1)S(1)}, bf16[384,128]{1,0:T(8,128)(2,1)S(1)}, u32[]{:S(2)}, u32[]{:S(2)}) collective-permute-start(bf16[384,128]{1,0:T(8,128)(2,1)S(1)} %get-tuple-element.39), channel_id=1, source_target_pairs={{0,12},{4,8},{8,4},{12,0},{16,28},{20,24},{24,20},{28,16},{32,44},... | collective-permute-start | bytes 294920 | tf_op jit(solution)/shard_map/ppermute | solution.py:364
  8.4 0.0 copy-done.1
  8.4 1.3 %collective-permute-start.4 = (bf16[1024,128]{1,0:T(8,128)(2,1)S(1)}, bf16[1024,128]{1,0:T(8,128)(2,1)S(1)}, u32[]{:S(2)}, u32[]{:S(2)}) collective-permute-start(bf16[1024,128]{1,0:T(8,128)(2,1)S(1)} %bitcast.42), channel_id=1, source_target_pairs={{0,1},{1,0},{2,3},{3,2},{4,5},{5,4},{6,7},{7,6},{8,9},{9,8},{10,11... | collective-permute-start | bytes 786440 | tf_op jit(solution)/shard_map/ppermute | solution.py:377
  9.7 0.0 collective-permute-done.ixa_ref
  9.7 1.9 %collective-permute-done.1.ixb_ref = bf16[384,128]{1,0:T(8,128)(2,1)S(1)} collective-permute-done((bf16[384,128]{1,0:T(8,128)(2,1)S(1)}, bf16[384,128]{1,0:T(8,128)(2,1)S(1)}, u32[]{:S(2)}, u32[]{:S(2)}) %collective-permute-start.1) | collective-permute-done | bytes 98336 | tf_op jit(solution)/shard_map/ppermute | solution.py:364
  11.6 3.2 %collective-permute-start.2 = (bf16[384,128]{1,0:T(8,128)(2,1)S(1)}, bf16[384,128]{1,0:T(8,128)(2,1)S(1)}, u32[]{:S(2)}, u32[]{:S(2)}) collective-permute-start(bf16[384,128]{1,0:T(8,128)(2,1)S(1)} %pad_maximum_fusion.2), channel_id=1, source_target_pairs={{0,16},{4,20},{8,24},{12,28},{16,0},{20,4},{24,8},{28,12},{32,48},... | collective-permute-start | bytes 294920 | tf_op jit(solution)/shard_map/ppermute | solution.py:373
  14.9 3.8 %collective-permute-start.3 = (bf16[384,128]{1,0:T(8,128)(2,1)S(1)}, bf16[384,128]{1,0:T(8,128)(2,1)S(1)}, u32[]{:S(2)}, u32[]{:S(2)}) collective-permute-start(bf16[384,128]{1,0:T(8,128)(2,1)S(1)} %pad_maximum_fusion.3), channel_id=1, source_target_pairs={{0,112},{4,116},{8,120},{12,124},{16,32},{20,36},{24,40},{28,44},{... | collective-permute-start | bytes 294920 | tf_op jit(solution)/shard_map/ppermute | solution.py:373
  18.6 0.0 copy-done
  18.6 0.0 copy-done.3
  18.6 0.0 copy-done.5
  18.6 10.8 %forward.1 = (bf16[3328,1024]{1,0:T(8,128)(2,1)}, f32[1024,128]{1,0:T(8,128)S(1)}) custom-call(bf16[1024,128]{1,0:T(8,128)(2,1)S(1)} %bitcast.45, s32[27,1024]{1,0:T(8,128)S(1)} %bitcast.48, bf16[27,128,128]{2,1,0:T(8,128)(2,1)S(1)} %bitcast.35), custom_call_target="tpu_custom_call" | custom-call | flops 15000000512 | bytes 9000000 | tf_op jit(solution)/shard_map/forward/pallas_call | solution.py:421
  29.4 0.0 collective-permute-done.2.iya_ref
  29.4 0.0 collective-permute-done.3.iyb_ref
  29.4 0.0 collective-permute-done.4.pair_ref
  29.4 6.8 %activate.1 = (bf16[1024,128]{1,0:T(8,128)(2,1)S(1)}, bf16[1024,128]{1,0:T(8,128)(2,1)S(1)}, bf16[320,128]{1,0:T(8,128)(2,1)S(1)}, bf16[320,128]{1,0:T(8,128)(2,...) custom-call(s32[2]{0:T(128)S(1)} %pad_add_fusion.side_ref, ...), custom_call_target="tpu_custom_call" | custom-call | flops 4000000000 | bytes 3000000 | tf_op jit(solution)/shard_map/activate/pallas_call | solution.py:432
  36.2 4.4 %weight.1 = f32[27,128,128]{2,1,0:T(8,128)S(1)} custom-call(bf16[3328,1024]{1,0:T(8,128)(2,1)} %get-tuple-element.43.g_ref, bf16[1024,128]{1,0:T(8,128)(2,1)S(1)} %get-tuple-element.63.grad_ref, bf16[1024,128]{1,0:T(8,128)(2,1)S(1)} %bitcast.46, f32[27,128,128]{2,1,0:T(8,128)S(1)} %get-tuple-element.44.halo_ref), custom_call_target="tpu_custom_call" | custom-call | flops 4000000000 | bytes 9000000 | tf_op jit(solution)/shard_map/weight/pallas_call | solution.py:440
  40.6 0.1 fusion
  40.7 0.7 collective-permute-start.5
  41.4 1.4 %collective-permute-start.9 = (bf16[320,128]{1,0:T(8,128)(2,1)S(1)}, bf16[320,128]{1,0:T(8,128)(2,1)S(1)}, u32[]{:S(2)}, u32[]{:S(2)}) collective-permute-start(bf16[320,128]{1,0:T(8,128)(2,1)S(1)} %get-tuple-element.52), channel_id=1, source_target_pairs={{0,12},{4,8},{8,4},{12,0},{16,28},{20,24},{24,20},{28,16},{32,44},... | collective-permute-start | bytes 245768 | tf_op jit(solution)/shard_map/ppermute | solution.py:364
  42.8 2.4 %backward.4.refs_0_ = f32[256,128]{1,0:T(8,128)S(1)} custom-call(bf16[1024,128]{1,0:T(8,128)(2,1)S(1)} %get-tuple-element.63.grad_ref, s32[27,1024]{1,0:T(8,128)S(1)} %bitcast.49, bf16[27,128,128]{2,1,0:T(8,128)(2,1)S(1)} %bitcast.37), custom_call_target="tpu_custom_call" | custom-call | flops 3000000000 | bytes 2000000 | tf_op jit(solution)/shard_map/backward/pallas_call | solution.py:454
  45.2 0.3 collective-permute-start.8
  45.5 0.2 collective-permute-done.9.ixb_ref
  45.7 0.9 collective-permute-done.8.ixa_ref
  46.6 0.0 collective-permute-done.5
  46.6 0.1 bitcast_add_fusion
  46.8 0.5 collective-permute-start.6
  47.2 1.2 %collective-permute-start.11 = (bf16[320,128]{1,0:T(8,128)(2,1)S(1)}, bf16[320,128]{1,0:T(8,128)(2,1)S(1)}, u32[]{:S(2)}, u32[]{:S(2)}) collective-permute-start(bf16[320,128]{1,0:T(8,128)(2,1)S(1)} %pad_maximum_fusion.5), channel_id=1, source_target_pairs={{0,112},{4,116},{8,120},{12,124},{16,32},{20,36},{24,40},{28,44},{... | collective-permute-start | bytes 245768 | tf_op jit(solution)/shard_map/ppermute | solution.py:373
  48.5 0.0 collective-permute-start.10
  48.5 2.4 %backward.5.refs_1_ = f32[256,128]{1,0:T(8,128)S(1)} custom-call(bf16[1024,128]{1,0:T(8,128)(2,1)S(1)} %get-tuple-element.63.grad_ref, s32[27,1024]{1,0:T(8,128)S(1)} %bitcast.50, bf16[27,128,128]{2,1,0:T(8,128)(2,1)S(1)} %bitcast.38), custom_call_target="tpu_custom_call" | custom-call | flops 3000000000 | bytes 2000000 | tf_op jit(solution)/shard_map/backward/pallas_call | solution.py:454
  50.9 2.7 %collective-permute-done.6 = bf16[2,432,128]{2,1,0:T(8,128)(2,1)S(1)} collective-permute-done((bf16[2,432,128]{2,1,0:T(8,128)(2,1)S(1)}, bf16[2,432,128]{2,1,0:T(8,128)(2,1)S(1)}, u32[]{:S(2)}, u32[]{:S(2)}) %collective-permute-start.6) | collective-permute-done | bytes 221216 | tf_op jit(solution)/shard_map/ppermute | solution.py:381
  53.7 0.1 collective-permute-start.7
  53.8 1.7 %collective-permute-done.11.iyb_ref = bf16[320,128]{1,0:T(8,128)(2,1)S(1)} collective-permute-done((bf16[320,128]{1,0:T(8,128)(2,1)S(1)}, bf16[320,128]{1,0:T(8,128)(2,1)S(1)}, u32[]{:S(2)}, u32[]{:S(2)}) %collective-permute-start.11) | collective-permute-done | bytes 81952 | tf_op jit(solution)/shard_map/ppermute | solution.py:373
  55.5 1.0 %collective-permute-done.10.iya_ref = bf16[320,128]{1,0:T(8,128)(2,1)S(1)} collective-permute-done((bf16[320,128]{1,0:T(8,128)(2,1)S(1)}, bf16[320,128]{1,0:T(8,128)(2,1)S(1)}, u32[]{:S(2)}, u32[]{:S(2)}) %collective-permute-start.10) | collective-permute-done | bytes 81952 | tf_op jit(solution)/shard_map/ppermute | solution.py:373
  56.6 3.0 %returning.1.refs_4_ = f32[1152,128]{1,0:T(8,128)S(1)} custom-call(s32[2]{0:T(128)S(1)} %pad_add_fusion.side_ref, bf16[320,128]{1,0:T(8,128)(2,1)S(1)} %collective-permute-done.8.ixa_ref, bf16[320,128]{1,0:T(8,128)(2,1)S(1)} %collective-permute-done.9.ixb_ref, bf16[320,128]{1,0:T(8,128)(2,1)S(1)} %collective-permute-done.10.iya_ref, ...), custom_call_target="tpu_custom_call" | custom-call | flops 3000000000 | bytes 4000000 | tf_op jit(solution)/shard_map/returning/pallas_call | solution.py:483
  59.5 0.0 collective-permute-done.7
  59.6 2.4 %collective-permute-start.12 = (bf16[432,128]{1,0:T(8,128)(2,1)S(1)}, bf16[432,128]{1,0:T(8,128)(2,1)S(1)}, u32[]{:S(2)}, u32[]{:S(2)}) collective-permute-start(bf16[432,128]{1,0:T(8,128)(2,1)S(1)} %fusion.2), channel_id=1, source_target_pairs={{0,16},{4,20},{8,24},{12,28},{16,0},{20,4},{24,8},{28,12},{32,48},... | collective-permute-start | bytes 331784 | tf_op jit(solution)/shard_map/ppermute | solution.py:381
  62.0 2.4 %backward.6.refs_2_ = f32[256,128]{1,0:T(8,128)S(1)} custom-call(bf16[1024,128]{1,0:T(8,128)(2,1)S(1)} %get-tuple-element.63.grad_ref, s32[27,1024]{1,0:T(8,128)S(1)} %bitcast.51, bf16[27,128,128]{2,1,0:T(8,128)(2,1)S(1)} %bitcast.40), custom_call_target="tpu_custom_call" | custom-call | flops 3000000000 | bytes 2000000 | tf_op jit(solution)/shard_map/backward/pallas_call | solution.py:454
  64.4 0.4 collective-permute-done.12
  64.8 3.4 %collective-permute-start.13 = (bf16[432,128]{1,0:T(8,128)(2,1)S(1)}, bf16[432,128]{1,0:T(8,128)(2,1)S(1)}, u32[]{:S(2)}, u32[]{:S(2)}) collective-permute-start(bf16[432,128]{1,0:T(8,128)(2,1)S(1)} %add_convert_fusion.1), channel_id=1, source_target_pairs={{0,64},{4,68},{8,72},{12,76},{16,80},{20,84},{24,88},{28,92},{32,9... | collective-permute-start | bytes 331784 | tf_op jit(solution)/shard_map/ppermute | solution.py:381
  68.2 1.3 %collective-permute-start.14 = (bf16[1024,128]{1,0:T(8,128)(2,1)S(1)}, bf16[1024,128]{1,0:T(8,128)(2,1)S(1)}, u32[]{:S(2)}, u32[]{:S(2)}) collective-permute-start(bf16[1024,128]{1,0:T(8,128)(2,1)S(1)} %get-tuple-element.67.refs_6_), channel_id=1, source_target_pairs={{0,1},{1,0},{2,3},{3,2},{4,5},{5,4},{6,7},{7,6},{8,9},{9,8},{10,11... | collective-permute-start | bytes 786440 | tf_op jit(solution)/shard_map/ppermute | solution.py:377
  69.5 2.5 %backward.7.refs_3_ = f32[256,128]{1,0:T(8,128)S(1)} custom-call(bf16[1024,128]{1,0:T(8,128)(2,1)S(1)} %get-tuple-element.63.grad_ref, s32[27,1024]{1,0:T(8,128)S(1)} %bitcast.52, bf16[27,128,128]{2,1,0:T(8,128)(2,1)S(1)} %bitcast.41), custom_call_target="tpu_custom_call" | custom-call | flops 3000000000 | bytes 2000000 | tf_op jit(solution)/shard_map/backward/pallas_call | solution.py:454
  72.0 0.0 collective-permute-done.13
  72.0 0.1 collective-permute-start.15
  72.1 1.3 %collective-permute-done.14.refs_7_ = bf16[1024,128]{1,0:T(8,128)(2,1)S(1)} collective-permute-done((bf16[1024,128]{1,0:T(8,128)(2,1)S(1)}, bf16[1024,128]{1,0:T(8,128)(2,1)S(1)}, u32[]{:S(2)}, u32[]{:S(2)}) %collective-permute-start.14) | collective-permute-done | bytes 262176 | tf_op jit(solution)/shard_map/ppermute | solution.py:377
  73.4 1.7 %final.1 = (bf16[1024,128]{1,0:T(8,128)(2,1)}, bf16[1024,128]{1,0:T(8,128)(2,1)}) custom-call(f32[256,128]{1,0:T(8,128)S(1)} %backward.4.refs_0_, f32[256,128]{1,0:T(8,128)S(1)} %backward.5.refs_1_, f32[256,128]{1,0:T(8,128)S(1)} %backward.6.refs_2_, f32[256,128]{1,0:T(8,128)S(1)} %backward.7.refs_3_, f32[1152,128]{1,0:T(8,128)S(1)} %returning.1.refs_4_, ...), custom_call_target="tpu_custom_call" | custom-call | flops 1000000000 | bytes 3000000 | tf_op jit(solution)/shard_map/final/pallas_call | solution.py:501
  75.1 0.9 collective-permute-done.15.one_ref
  76.0 0.4 collective-permute-start.16
  76.4 4.4 %collective-permute-done.16.two_ref = bf16[2,432,128]{2,1,0:T(8,128)(2,1)S(1)} collective-permute-done((bf16[2,432,128]{2,1,0:T(8,128)(2,1)S(1)}, bf16[2,432,128]{2,1,0:T(8,128)(2,1)S(1)}, u32[]{:S(2)}, u32[]{:S(2)}) %collective-permute-start.16) | collective-permute-done | bytes 221216 | tf_op jit(solution)/shard_map/ppermute | solution.py:381
  80.9 4.8 %collective-permute-start.17 = (bf16[4,432,128]{2,1,0:T(8,128)(2,1)S(1)}, bf16[4,432,128]{2,1,0:T(8,128)(2,1)S(1)}, u32[]{:S(2)}, u32[]{:S(2)}) collective-permute-start(bf16[4,432,128]{2,1,0:T(8,128)(2,1)S(1)} %pad_maximum_fusion), channel_id=1, source_target_pairs={{0,4},{4,0},{8,12},{12,8},{16,20},{20,16},{24,28},{28,24},{32,36},... | collective-permute-start | bytes 1327112 | tf_op jit(solution)/shard_map/ppermute | solution.py:381
  85.8 0.1 pad_add_fusion.1.bits_ref
  85.8 1.3 %collective-permute-done.17.four_ref = bf16[4,432,128]{2,1,0:T(8,128)(2,1)S(1)} collective-permute-done((bf16[4,432,128]{2,1,0:T(8,128)(2,1)S(1)}, bf16[4,432,128]{2,1,0:T(8,128)(2,1)S(1)}, u32[]{:S(2)}, u32[]{:S(2)}) %collective-permute-start.17) | collective-permute-done | bytes 442400 | tf_op jit(solution)/shard_map/ppermute | solution.py:381
  87.2 1.9 %assemble.1 = f32[8,432,128]{2,1,0:T(8,128)} custom-call(s32[3]{0:T(128)S(1)} %pad_add_fusion.1.bits_ref, bf16[432,128]{1,0:T(8,128)(2,1)S(1)} %add_convert_fusion.own_ref, bf16[432,128]{1,0:T(8,128)(2,1)S(1)} %collective-permute-done.15.one_ref, bf16[2,432,128]{2,1,0:T(8,128)(2,1)S(1)} %collective-permute-done.16.two_ref, ...), custom_call_target="tpu_custom_call" | custom-call | flops 1000000 | bytes 3000000 | tf_op jit(solution)/shard_map/assemble/pallas_call | solution.py:511
  (16 shorter events, 0.3 us)
Async XLA Ops:
  1.4 0.9 %copy-start.2 = (bf16[1,1024,128]{2,1,0:T(8,128)(2,1)S(1)}, bf16[1,1024,128]{2,1,0:T(8,128)(2,1)}, u32[]{:S(2)}) copy-start(bf16[1,1024,128]{2,1,0:T(8,128)(2,1)} %param.6) | copy-start | bytes 786436
  2.4 0.9 %copy-start.4 = (s32[1152,27]{0,1:T(8,128)S(1)}, s32[1152,27]{0,1:T(8,128)}, u32[]{:S(2)}) copy-start(s32[1152,27]{0,1:T(8,128)} %param.10) | copy-start | bytes 373252
  3.3 5.1 %copy-start.1 = (bf16[1,1024,128]{2,1,0:T(8,128)(2,1)S(1)}, bf16[1,1024,128]{2,1,0:T(8,128)(2,1)}, u32[]{:S(2)}) copy-start(bf16[1,1024,128]{2,1,0:T(8,128)(2,1)} %param.8) | copy-start | bytes 786436
  3.3 15.3 %copy-start = (bf16[1,27,128,128]{3,2,1,0:T(8,128)(2,1)S(1)}, bf16[1,27,128,128]{3,2,1,0:T(8,128)(2,1)}, u32[]{:S(2)}) copy-start(bf16[1,27,128,128]{3,2,1,0:T(8,128)(2,1)} %param.7) | copy-start | bytes 2654212
  3.3 15.3 %copy-start.3 = (bf16[1,1024,128]{2,1,0:T(8,128)(2,1)S(1)}, bf16[1,1024,128]{2,1,0:T(8,128)(2,1)}, u32[]{:S(2)}) copy-start(bf16[1,1024,128]{2,1,0:T(8,128)(2,1)} %param.6) | copy-start | bytes 786436
  3.3 15.3 %copy-start.5 = (s32[1024,27]{0,1:T(8,128)S(1)}, s32[1024,27]{0,1:T(8,128)}, u32[]{:S(2)}) copy-start(s32[1024,27]{0,1:T(8,128)} %param.9) | copy-start | bytes 331780
  5.6 4.1 %collective-permute-start = (bf16[384,128]{1,0:T(8,128)(2,1)S(1)}, bf16[384,128]{1,0:T(8,128)(2,1)S(1)}, u32[]{:S(2)}, u32[]{:S(2)}) collective-permute-start(bf16[384,128]{1,0:T(8,128)(2,1)S(1)} %get-tuple-element.38), channel_id=1, source_target_pairs={{0,4},{4,0},{8,12},{12,8},{16,20},{20,16},{24,28},{28,24},{32,36},... | collective-permute-start | bytes 294920 | tf_op jit(solution)/shard_map/ppermute | solution.py:364
  7.1 4.5 %collective-permute-start.1 = (bf16[384,128]{1,0:T(8,128)(2,1)S(1)}, bf16[384,128]{1,0:T(8,128)(2,1)S(1)}, u32[]{:S(2)}, u32[]{:S(2)}) collective-permute-start(bf16[384,128]{1,0:T(8,128)(2,1)S(1)} %get-tuple-element.39), channel_id=1, source_target_pairs={{0,12},{4,8},{8,4},{12,0},{16,28},{20,24},{24,20},{28,16},{32,44},... | collective-permute-start | bytes 294920 | tf_op jit(solution)/shard_map/ppermute | solution.py:364
  8.4 21.0 %collective-permute-start.4 = (bf16[1024,128]{1,0:T(8,128)(2,1)S(1)}, bf16[1024,128]{1,0:T(8,128)(2,1)S(1)}, u32[]{:S(2)}, u32[]{:S(2)}) collective-permute-start(bf16[1024,128]{1,0:T(8,128)(2,1)S(1)} %bitcast.42), channel_id=1, source_target_pairs={{0,1},{1,0},{2,3},{3,2},{4,5},{5,4},{6,7},{7,6},{8,9},{9,8},{10,11... | collective-permute-start | bytes 786440 | tf_op jit(solution)/shard_map/ppermute | solution.py:377
  11.6 17.8 %collective-permute-start.2 = (bf16[384,128]{1,0:T(8,128)(2,1)S(1)}, bf16[384,128]{1,0:T(8,128)(2,1)S(1)}, u32[]{:S(2)}, u32[]{:S(2)}) collective-permute-start(bf16[384,128]{1,0:T(8,128)(2,1)S(1)} %pad_maximum_fusion.2), channel_id=1, source_target_pairs={{0,16},{4,20},{8,24},{12,28},{16,0},{20,4},{24,8},{28,12},{32,48},... | collective-permute-start | bytes 294920 | tf_op jit(solution)/shard_map/ppermute | solution.py:373
  14.9 14.6 %collective-permute-start.3 = (bf16[384,128]{1,0:T(8,128)(2,1)S(1)}, bf16[384,128]{1,0:T(8,128)(2,1)S(1)}, u32[]{:S(2)}, u32[]{:S(2)}) collective-permute-start(bf16[384,128]{1,0:T(8,128)(2,1)S(1)} %pad_maximum_fusion.3), channel_id=1, source_target_pairs={{0,112},{4,116},{8,120},{12,124},{16,32},{20,36},{24,40},{28,44},{... | collective-permute-start | bytes 294920 | tf_op jit(solution)/shard_map/ppermute | solution.py:373
  40.7 5.9 %collective-permute-start.5 = (bf16[2,2,432,128]{3,2,1,0:T(8,128)(2,1)S(1)}, bf16[2,2,432,128]{3,2,1,0:T(8,128)(2,1)S(1)}, u32[]{:S(2)}, u32[]{:S(2)}) collective-permute-start(bf16[2,2,432,128]{3,2,1,0:T(8,128)(2,1)S(1)} %fusion), channel_id=1, source_target_pairs={{0,4},{4,0},{8,12},{12,8},{16,20},{20,16},{24,28},{28,24},{32,36},... | collective-permute-start | bytes 1327112 | tf_op jit(solution)/shard_map/ppermute | solution.py:381
  41.4 4.4 %collective-permute-start.9 = (bf16[320,128]{1,0:T(8,128)(2,1)S(1)}, bf16[320,128]{1,0:T(8,128)(2,1)S(1)}, u32[]{:S(2)}, u32[]{:S(2)}) collective-permute-start(bf16[320,128]{1,0:T(8,128)(2,1)S(1)} %get-tuple-element.52), channel_id=1, source_target_pairs={{0,12},{4,8},{8,4},{12,0},{16,28},{20,24},{24,20},{28,16},{32,44},... | collective-permute-start | bytes 245768 | tf_op jit(solution)/shard_map/ppermute | solution.py:364
  45.2 1.4 %collective-permute-start.8 = (bf16[320,128]{1,0:T(8,128)(2,1)S(1)}, bf16[320,128]{1,0:T(8,128)(2,1)S(1)}, u32[]{:S(2)}, u32[]{:S(2)}) collective-permute-start(bf16[320,128]{1,0:T(8,128)(2,1)S(1)} %get-tuple-element.50), channel_id=1, source_target_pairs={{0,4},{4,0},{8,12},{12,8},{16,20},{20,16},{24,28},{28,24},{32,36},... | collective-permute-start | bytes 245768 | tf_op jit(solution)/shard_map/ppermute | solution.py:364
  46.8 6.9 %collective-permute-start.6 = (bf16[2,432,128]{2,1,0:T(8,128)(2,1)S(1)}, bf16[2,432,128]{2,1,0:T(8,128)(2,1)S(1)}, u32[]{:S(2)}, u32[]{:S(2)}) collective-permute-start(bf16[2,432,128]{2,1,0:T(8,128)(2,1)S(1)} %fusion.1), channel_id=1, source_target_pairs={{0,8},{4,12},{8,0},{12,4},{16,24},{20,28},{24,16},{28,20},{32,40},... | collective-permute-start | bytes 663560 | tf_op jit(solution)/shard_map/ppermute | solution.py:381
  47.2 8.3 %collective-permute-start.11 = (bf16[320,128]{1,0:T(8,128)(2,1)S(1)}, bf16[320,128]{1,0:T(8,128)(2,1)S(1)}, u32[]{:S(2)}, u32[]{:S(2)}) collective-permute-start(bf16[320,128]{1,0:T(8,128)(2,1)S(1)} %pad_maximum_fusion.5), channel_id=1, source_target_pairs={{0,112},{4,116},{8,120},{12,124},{16,32},{20,36},{24,40},{28,44},{... | collective-permute-start | bytes 245768 | tf_op jit(solution)/shard_map/ppermute | solution.py:373
  48.5 8.1 %collective-permute-start.10 = (bf16[320,128]{1,0:T(8,128)(2,1)S(1)}, bf16[320,128]{1,0:T(8,128)(2,1)S(1)}, u32[]{:S(2)}, u32[]{:S(2)}) collective-permute-start(bf16[320,128]{1,0:T(8,128)(2,1)S(1)} %pad_maximum_fusion.4), channel_id=1, source_target_pairs={{0,16},{4,20},{8,24},{12,28},{16,0},{20,4},{24,8},{28,12},{32,48},... | collective-permute-start | bytes 245768 | tf_op jit(solution)/shard_map/ppermute | solution.py:373
  53.7 5.8 %collective-permute-start.7 = (bf16[432,128]{1,0:T(8,128)(2,1)S(1)}, bf16[432,128]{1,0:T(8,128)(2,1)S(1)}, u32[]{:S(2)}, u32[]{:S(2)}) collective-permute-start(bf16[432,128]{1,0:T(8,128)(2,1)S(1)} %fusion.3), channel_id=1, source_target_pairs={{0,32},{4,36},{8,40},{12,44},{16,48},{20,52},{24,56},{28,60},{32,0... | collective-permute-start | bytes 331784 | tf_op jit(solution)/shard_map/ppermute | solution.py:381
  59.6 5.2 %collective-permute-start.12 = (bf16[432,128]{1,0:T(8,128)(2,1)S(1)}, bf16[432,128]{1,0:T(8,128)(2,1)S(1)}, u32[]{:S(2)}, u32[]{:S(2)}) collective-permute-start(bf16[432,128]{1,0:T(8,128)(2,1)S(1)} %fusion.2), channel_id=1, source_target_pairs={{0,16},{4,20},{8,24},{12,28},{16,0},{20,4},{24,8},{28,12},{32,48},... | collective-permute-start | bytes 331784 | tf_op jit(solution)/shard_map/ppermute | solution.py:381
  64.8 7.2 %collective-permute-start.13 = (bf16[432,128]{1,0:T(8,128)(2,1)S(1)}, bf16[432,128]{1,0:T(8,128)(2,1)S(1)}, u32[]{:S(2)}, u32[]{:S(2)}) collective-permute-start(bf16[432,128]{1,0:T(8,128)(2,1)S(1)} %add_convert_fusion.1), channel_id=1, source_target_pairs={{0,64},{4,68},{8,72},{12,76},{16,80},{20,84},{24,88},{28,92},{32,9... | collective-permute-start | bytes 331784 | tf_op jit(solution)/shard_map/ppermute | solution.py:381
  68.2 5.2 %collective-permute-start.14 = (bf16[1024,128]{1,0:T(8,128)(2,1)S(1)}, bf16[1024,128]{1,0:T(8,128)(2,1)S(1)}, u32[]{:S(2)}, u32[]{:S(2)}) collective-permute-start(bf16[1024,128]{1,0:T(8,128)(2,1)S(1)} %get-tuple-element.67.refs_6_), channel_id=1, source_target_pairs={{0,1},{1,0},{2,3},{3,2},{4,5},{5,4},{6,7},{7,6},{8,9},{9,8},{10,11... | collective-permute-start | bytes 786440 | tf_op jit(solution)/shard_map/ppermute | solution.py:377
  72.0 4.0 %collective-permute-start.15 = (bf16[432,128]{1,0:T(8,128)(2,1)S(1)}, bf16[432,128]{1,0:T(8,128)(2,1)S(1)}, u32[]{:S(2)}, u32[]{:S(2)}) collective-permute-start(bf16[432,128]{1,0:T(8,128)(2,1)S(1)} %add_convert_fusion.own_ref), channel_id=1, source_target_pairs={{0,32},{4,36},{8,40},{12,44},{16,48},{20,52},{24,56},{28,60},{32,0... | collective-permute-start | bytes 331784 | tf_op jit(solution)/shard_map/ppermute | solution.py:381
  76.0 4.9 %collective-permute-start.16 = (bf16[2,432,128]{2,1,0:T(8,128)(2,1)S(1)}, bf16[2,432,128]{2,1,0:T(8,128)(2,1)S(1)}, u32[]{:S(2)}, u32[]{:S(2)}) collective-permute-start(bf16[2,432,128]{2,1,0:T(8,128)(2,1)S(1)} %pad_maximum_fusion.1), channel_id=1, source_target_pairs={{0,8},{4,12},{8,0},{12,4},{16,24},{20,28},{24,16},{28,20},{32,40},... | collective-permute-start | bytes 663560 | tf_op jit(solution)/shard_map/ppermute | solution.py:381
  80.9 6.2 %collective-permute-start.17 = (bf16[4,432,128]{2,1,0:T(8,128)(2,1)S(1)}, bf16[4,432,128]{2,1,0:T(8,128)(2,1)S(1)}, u32[]{:S(2)}, u32[]{:S(2)}) collective-permute-start(bf16[4,432,128]{2,1,0:T(8,128)(2,1)S(1)} %pad_maximum_fusion), channel_id=1, source_target_pairs={{0,4},{4,0},{8,12},{12,8},{16,20},{20,16},{24,28},{28,24},{32,36},... | collective-permute-start | bytes 1327112 | tf_op jit(solution)/shard_map/ppermute | solution.py:381

commit v4 on v3

--- a/solution.py
+++ b/solution.py
@@ -463,23 +463,28 @@
     blocks = dw.reshape(2, 2, 2, -1, C)
 
     def halve(blocks, stage):
-        sent = pick(blocks, 1 - bits[stage]).astype(BF)
-        return pick(blocks, bits[stage]), sent
-
+        return pick(blocks, bits[stage]), pick(blocks, 1 - bits[stage]).astype(BF)
+
+    def plus(one, two):
+        return one.astype(F32) + two.astype(F32)
+
+    locals_ = []
     kept, sent = halve(blocks, 0)
     got = xor_send(sent, 1)
+    kept, sent = halve(plus(kept, got), 1)
+    got = xor_send(sent, 2)
     in_x = exchange_x(tie(xa, sent), tie(xb, sent))
-    locals_ = [backward(0, tie(grad, sent))]
-    blocks = kept + tie(got, locals_[0]).astype(F32)
-
-    kept, sent = halve(blocks, 1)
-    got = xor_send(sent, 2)
-    in_y = exchange_y(tie(ya, sent), tie(yb, sent), *in_x, sides, CAP, TZ)
+    locals_.append(backward(0, tie(grad, sent)))
+    kept, sent = halve(plus(kept, tie(got, locals_[0])), 2)
+    got = xor_send(sent, 8)
     locals_.append(backward(1, tie(grad, sent)))
-    blocks = kept + tie(got, locals_[1]).astype(F32)
-
-    kept, sent = halve(blocks, 2)
-    got = xor_send(sent, 8)
+    own = plus(kept, tie(got, locals_[1])).astype(BF)
+    got = xor_send(own, 4)
+    in_y = exchange_y(tie(ya, own), tie(yb, own), *in_x, sides, CAP, TZ)
+    locals_.append(backward(2, tie(grad, own)))
+    own = plus(own, tie(got, locals_[2])).astype(BF)
+    got = xor_send(own, 16)
+    act_pair = swapped(tie(act, own))
     placed = pl.pallas_call(
         return_kernel,
         in_specs=[smem] + [vmem] * 7,
@@ -487,26 +492,20 @@
         compiler_params=PARAMS,
         cost_estimate=cost(3e9, 4e6),
         name="returning",
-    )(sides, *in_x, *in_y, face_p, edge_p, tie(w, sent))
-    own = (kept + tie(got, placed).astype(F32)).astype(BF)
-
-    got = xor_send(own, 4)
-    locals_.append(backward(2, tie(grad, own)))
-    own = (own.astype(F32) + tie(got, locals_[2]).astype(F32)).astype(BF)
-    got = xor_send(own, 16)
-    act_pair = swapped(tie(act, own))
+    )(sides, *in_x, *in_y, face_p, edge_p, tie(w, own))
+    own = plus(own, tie(got, placed)).astype(BF)
+    one = xor_send(own, 8)
     locals_.append(backward(3, tie(grad, own)))
-    own = (own.astype(F32) + tie(got, locals_[3]).astype(F32)).astype(BF)
-    one = xor_send(own, 8)
+    one = tie(one, locals_[3])
+    two = xor_send(jnp.stack([own, one]), 2)
     mixed, input_grad = pl.pallas_call(
         final_kernel,
         out_shape=[shape((ROWS, C), BF), shape((ROWS, C), BF)],
         compiler_params=PARAMS,
         cost_estimate=cost(1e9, 3e6),
         name="final",
-    )(*locals_, tie(placed, own), rr, act, act_pair)
-    one = tie(one, input_grad)
-    two = xor_send(jnp.stack([own, one]), 2)
+    )(*locals_, tie(placed, one), rr, act, act_pair)
+    two = tie(two, input_grad)
     four = xor_send(jnp.concatenate([jnp.stack([own, one]), two], 0), 1)
     weight_grad = pl.pallas_call(
         assemble_kernel,

time: 89.2 us -> 90.1 us (1.010)
  waiting for transfers between devices: 16.8 us -> 15.4 us
  local copies, waits for them, and re-layouts: 2.7 us -> 4.09 us
  other arithmetic: 0.49 us -> 1.5 us
    ppermute x4, waiting for transfers between devices: 2.99 us -> 6.27 us  [exchange_x(): lax.ppermute(v, 'space', pairing('x', n))]
    ppermute x4, starting transfers between devices: 8.21 us -> 11.1 us  [exchange_y(): lax.ppermute(v, 'space', pairing('y', n))]
    ppermute x4, waiting for transfers between devices: 2.72 us -> 0.01 us  [exchange_y(): lax.ppermute(v, 'space', pairing('y', n))]
    ppermute x8, starting transfers between devices: 12.4 us -> 10.2 us  [xor_send(): lax.ppermute(value, 'space', [(i, i ^ bits) for i in range(lax.axis_size(...]
    ppermute x2, waiting for transfers between devices: 1.33 us -> 0.01 us  [swapped(): lax.ppermute(array, 'segment', [(i, i ^ 1) for i in range(lax.axis_size('...]
    ppermute x4, starting transfers between devices: 4.47 us -> 3.41 us  [exchange_x(): lax.ppermute(v, 'space', pairing('x', n))]
    add x2, other arithmetic: 0.12 us -> 1.14 us  [plus(): return one.astype(F32) + two.astype(F32)]
    unnamed x12 -> x24, local copies, waits for them, and re-layouts: 1.87 us -> 2.5 us
  transfers between devices with their start and end apart: 18 -> 18, of which waited for: 11 -> 7; matrix products, arithmetic and copies ran while one was open for 0% -> 0% of each run, Pallas kernels for 28% -> 28%
where the time goes in v4:
time: 90.1 us; the launch traced here: 89.9 us
  Pallas kernels  40.7 us (45%)
  starting transfers between devices  27.3 us (30%)
  waiting for transfers between devices  15.4 us (17%)
  local copies, waits for them, and re-layouts  4.09 us (5%)
  other arithmetic  1.5 us (2%)
  between operations  0.91 us (1%)
    ppermute x4, starting transfers between devices, exchange_y(): lax.ppermute(v, 'space', pairing('y', n))  11.1 us
    pallas_call x1, Pallas kernels, on_device(): pl.pallas_call(functools.partial(forward_kernel, width=512), grid=(2,), i...  10.8 us
    ppermute x8, starting transfers between devices, xor_send(): lax.ppermute(value, 'space', [(i, i ^ bits) for i in range(lax.axis_size(...  10.2 us
    pallas_call x4, Pallas kernels, backward(): pl.pallas_call(functools.partial(backward_kernel, begin=index * size), ou...  9.79 us
    ppermute x8, waiting for transfers between devices, xor_send(): lax.ppermute(value, 'space', [(i, i ^ bits) for i in range(lax.axis_size(...  9.09 us
    pallas_call x1, Pallas kernels, on_device(): pl.pallas_call(activate_kernel, in_specs=[smem] + [vmem] * 9, out_shape=[...  6.77 us
    ppermute x4, waiting for transfers between devices, exchange_x(): lax.ppermute(v, 'space', pairing('x', n))  6.27 us
    pallas_call x1, Pallas kernels, on_device(): pl.pallas_call(weight_kernel, grid=(2,), in_specs=[pl.BlockSpec((13 * C,...  4.51 us
  transfers between devices with their start and end apart: 18, of which 7 were waited for; matrix products, arithmetic and copies ran while one was open for 0% of the time, Pallas kernels for 28%

profile of v4, /device:TPU:1, one launch (start us, length us, event | category | flops | bytes accessed | tf_op | source)
XLA Modules:
  0.0 89.9 jit_solution(17261753919441769655)
XLA Ops:
  0.7 0.7 reshape.15.rr_ref.refs_5_
  1.4 0.1 pad_add_fusion.side_ref
  1.4 0.9 %copy-done.2 = bf16[1,1024,128]{2,1,0:T(8,128)(2,1)S(1)} copy-done((bf16[1,1024,128]{2,1,0:T(8,128)(2,1)S(1)}, bf16[1,1024,128]{2,1,0:T(8,128)(2,1)}, u32[]{:S(2)}) %copy-start.2) | copy-done | bytes 262168
  2.4 0.9 %copy-done.4 = s32[1152,27]{0,1:T(8,128)S(1)} copy-done((s32[1152,27]{0,1:T(8,128)S(1)}, s32[1152,27]{0,1:T(8,128)}, u32[]{:S(2)}) %copy-start.4) | copy-done | bytes 124440
  3.3 2.3 %start.1 = (bf16[384,128]{1,0:T(8,128)(2,1)S(1)}, bf16[384,128]{1,0:T(8,128)(2,1)S(1)}, bf16[288,128]{1,0:T(8,128)(2,1)S(1)}, bf16[288,128]{1,0:T(8,128)(2,1)S(1...) custom-call(s32[2]{0:T(128)S(1)} %pad_add_fusion.side_ref, bf16[1024,128]{1,0:T(8,128)(2,1)S(1)} %bitcast.44, ...), custom_call_target="tpu_custom_call" | custom-call | flops 2000000000 | bytes 4000000 | tf_op jit(solution)/shard_map/start/pallas_call | solution.py:410
  5.6 0.0 copy-start.10
  5.6 0.6 copy-done.10
  6.2 1.4 %collective-permute-start = (bf16[384,128]{1,0:T(8,128)(2,1)S(1)}, bf16[384,128]{1,0:T(8,128)(2,1)S(1)}, u32[]{:S(2)}, u32[]{:S(2)}) collective-permute-start(bf16[384,128]{1,0:T(8,128)(2,1)S(1)} %get-tuple-element.38), channel_id=1, source_target_pairs={{0,4},{4,0},{8,12},{12,8},{16,20},{20,16},{24,28},{28,24},{32,36},... | collective-permute-start | bytes 294920 | tf_op jit(solution)/shard_map/ppermute | solution.py:364
  7.7 1.2 %collective-permute-start.1 = (bf16[384,128]{1,0:T(8,128)(2,1)S(1)}, bf16[384,128]{1,0:T(8,128)(2,1)S(1)}, u32[]{:S(2)}, u32[]{:S(2)}) collective-permute-start(bf16[384,128]{1,0:T(8,128)(2,1)S(1)} %get-tuple-element.39), channel_id=1, source_target_pairs={{0,12},{4,8},{8,4},{12,0},{16,28},{20,24},{24,20},{28,16},{32,44},... | collective-permute-start | bytes 294920 | tf_op jit(solution)/shard_map/ppermute | solution.py:364
  8.8 0.0 copy-done.1
  8.8 1.3 %collective-permute-start.4 = (bf16[1024,128]{1,0:T(8,128)(2,1)S(1)}, bf16[1024,128]{1,0:T(8,128)(2,1)S(1)}, u32[]{:S(2)}, u32[]{:S(2)}) collective-permute-start(bf16[1024,128]{1,0:T(8,128)(2,1)S(1)} %bitcast.42), channel_id=1, source_target_pairs={{0,1},{1,0},{2,3},{3,2},{4,5},{5,4},{6,7},{7,6},{8,9},{9,8},{10,11... | collective-permute-start | bytes 786440 | tf_op jit(solution)/shard_map/ppermute | solution.py:377
  10.1 0.0 collective-permute-done.ixa_ref
  10.1 1.9 %collective-permute-done.1.ixb_ref = bf16[384,128]{1,0:T(8,128)(2,1)S(1)} collective-permute-done((bf16[384,128]{1,0:T(8,128)(2,1)S(1)}, bf16[384,128]{1,0:T(8,128)(2,1)S(1)}, u32[]{:S(2)}, u32[]{:S(2)}) %collective-permute-start.1) | collective-permute-done | bytes 98336 | tf_op jit(solution)/shard_map/ppermute | solution.py:364
  12.1 3.2 %collective-permute-start.2 = (bf16[384,128]{1,0:T(8,128)(2,1)S(1)}, bf16[384,128]{1,0:T(8,128)(2,1)S(1)}, u32[]{:S(2)}, u32[]{:S(2)}) collective-permute-start(bf16[384,128]{1,0:T(8,128)(2,1)S(1)} %pad_maximum_fusion.2), channel_id=1, source_target_pairs={{0,16},{4,20},{8,24},{12,28},{16,0},{20,4},{24,8},{28,12},{32,48},... | collective-permute-start | bytes 294920 | tf_op jit(solution)/shard_map/ppermute | solution.py:373
  15.3 3.8 %collective-permute-start.3 = (bf16[384,128]{1,0:T(8,128)(2,1)S(1)}, bf16[384,128]{1,0:T(8,128)(2,1)S(1)}, u32[]{:S(2)}, u32[]{:S(2)}) collective-permute-start(bf16[384,128]{1,0:T(8,128)(2,1)S(1)} %pad_maximum_fusion.3), channel_id=1, source_target_pairs={{0,112},{4,116},{8,120},{12,124},{16,32},{20,36},{24,40},{28,44},{... | collective-permute-start | bytes 294920 | tf_op jit(solution)/shard_map/ppermute | solution.py:373
  19.0 0.0 copy-done
  19.1 0.0 copy-done.3
  19.1 10.8 %forward.1 = (bf16[3328,1024]{1,0:T(8,128)(2,1)}, f32[1024,128]{1,0:T(8,128)S(1)}) custom-call(bf16[1024,128]{1,0:T(8,128)(2,1)S(1)} %bitcast.45, s32[27,1024]{1,0:T(8,128)S(1)} %bitcast.48, bf16[27,128,128]{2,1,0:T(8,128)(2,1)S(1)} %bitcast.35), custom_call_target="tpu_custom_call" | custom-call | flops 15000000512 | bytes 9000000 | tf_op jit(solution)/shard_map/forward/pallas_call | solution.py:421
  29.9 0.0 collective-permute-done.2.iya_ref
  29.9 0.0 collective-permute-done.3.iyb_ref
  29.9 0.0 collective-permute-done.4.pair_ref
  29.9 6.8 %activate.1 = (bf16[1024,128]{1,0:T(8,128)(2,1)S(1)}, bf16[1024,128]{1,0:T(8,128)(2,1)S(1)}, bf16[320,128]{1,0:T(8,128)(2,1)S(1)}, bf16[320,128]{1,0:T(8,128)(2,...) custom-call(s32[2]{0:T(128)S(1)} %pad_add_fusion.side_ref, ...), custom_call_target="tpu_custom_call" | custom-call | flops 4000000000 | bytes 3000000 | tf_op jit(solution)/shard_map/activate/pallas_call | solution.py:432
  36.6 0.0 copy-start.6
  36.6 0.0 copy-start.8
  36.7 4.5 %weight.1 = f32[27,128,128]{2,1,0:T(8,128)S(1)} custom-call(bf16[3328,1024]{1,0:T(8,128)(2,1)} %get-tuple-element.43.g_ref, bf16[1024,128]{1,0:T(8,128)(2,1)S(1)} %get-tuple-element.63.grad_ref, bf16[1024,128]{1,0:T(8,128)(2,1)S(1)} %bitcast.46, f32[27,128,128]{2,1,0:T(8,128)S(1)} %get-tuple-element.44.halo_ref), custom_call_target="tpu_custom_call" | custom-call | flops 4000000000 | bytes 9000000 | tf_op jit(solution)/shard_map/weight/pallas_call | solution.py:440
  41.2 0.0 copy-done.6
  41.2 0.0 copy-done.8
  41.2 0.0 copy-start.7
  41.2 0.8 fusion
  42.0 0.5 collective-permute-start.5
  42.5 1.8 %collective-permute-done.5 = bf16[2,2,432,128]{3,2,1,0:T(8,128)(2,1)} collective-permute-done((bf16[2,2,432,128]{3,2,1,0:T(8,128)(2,1)}, bf16[2,2,432,128]{3,2,1,0:T(8,128)(2,1)}, u32[]{:S(2)}, u32[]{:S(2)}) %collective-permute-start.5) | collective-permute-done | bytes 442400 | tf_op jit(solution)/shard_map/ppermute | solution.py:381
  44.3 1.1 %bitcast_add_fusion = f32[2,2,432,128]{3,2,1,0:T(8,128)S(1)} fusion(bf16[2,2,432,128]{3,2,1,0:T(8,128)(2,1)} %collective-permute-done.5, f32[2,2,2,432,128]{4,3,2,1,0:T(8,128)S(1)} %bitcast.32, s32[]{:T(128)S(6)} %select_n.105), kind=kLoop, calls=%fused_computation | loop fusion | flops 442368 | bytes 2211844 | tf_op jit(solution)/shard_map/add | solution.py:469
  45.4 1.4 %collective-permute-start.6 = (bf16[2,432,128]{2,1,0:T(8,128)(2,1)S(1)}, bf16[2,432,128]{2,1,0:T(8,128)(2,1)S(1)}, u32[]{:S(2)}, u32[]{:S(2)}) collective-permute-start(bf16[2,432,128]{2,1,0:T(8,128)(2,1)S(1)} %fusion.1), channel_id=1, source_target_pairs={{0,8},{4,12},{8,0},{12,4},{16,24},{20,28},{24,16},{28,20},{32,40},... | collective-permute-start | bytes 663560 | tf_op jit(solution)/shard_map/ppermute | solution.py:381
  46.8 0.7 collective-permute-start.11
  47.5 2.4 %backward.4.refs_0_ = f32[256,128]{1,0:T(8,128)S(1)} custom-call(bf16[1024,128]{1,0:T(8,128)(2,1)S(1)} %copy-done.9, s32[27,1024]{1,0:T(8,128)S(1)} %bitcast.49, bf16[27,128,128]{2,1,0:T(8,128)(2,1)S(1)} %bitcast.37), custom_call_target="tpu_custom_call" | custom-call | flops 3000000000 | bytes 2000000 | tf_op jit(solution)/shard_map/backward/pallas_call | solution.py:454
  50.0 0.1 collective-permute-start.10
  50.1 4.4 %collective-permute-done.11.ixb_ref = bf16[320,128]{1,0:T(8,128)(2,1)S(1)} collective-permute-done((bf16[320,128]{1,0:T(8,128)(2,1)S(1)}, bf16[320,128]{1,0:T(8,128)(2,1)S(1)}, u32[]{:S(2)}, u32[]{:S(2)}) %collective-permute-start.11) | collective-permute-done | bytes 81952 | tf_op jit(solution)/shard_map/ppermute | solution.py:364
  54.4 0.0 collective-permute-done.10.ixa_ref
  54.5 0.0 collective-permute-done.6
  54.6 0.1 collective-permute-start.7
  54.6 2.4 %backward.5.refs_1_ = f32[256,128]{1,0:T(8,128)S(1)} custom-call(bf16[1024,128]{1,0:T(8,128)(2,1)S(1)} %copy-done.9, s32[27,1024]{1,0:T(8,128)S(1)} %bitcast.50, bf16[27,128,128]{2,1,0:T(8,128)(2,1)S(1)} %bitcast.38), custom_call_target="tpu_custom_call" | custom-call | flops 3000000000 | bytes 2000000 | tf_op jit(solution)/shard_map/backward/pallas_call | solution.py:454
  57.1 2.3 %collective-permute-done.7 = bf16[432,128]{1,0:T(8,128)(2,1)S(1)} collective-permute-done((bf16[432,128]{1,0:T(8,128)(2,1)S(1)}, bf16[432,128]{1,0:T(8,128)(2,1)S(1)}, u32[]{:S(2)}, u32[]{:S(2)}) %collective-permute-start.7) | collective-permute-done | bytes 110624 | tf_op jit(solution)/shard_map/ppermute | solution.py:381
  59.4 1.1 %collective-permute-start.8 = (bf16[432,128]{1,0:T(8,128)(2,1)S(1)}, bf16[432,128]{1,0:T(8,128)(2,1)S(1)}, u32[]{:S(2)}, u32[]{:S(2)}) collective-permute-start(bf16[432,128]{1,0:T(8,128)(2,1)S(1)} %fusion.2), channel_id=1, source_target_pairs={{0,16},{4,20},{8,24},{12,28},{16,0},{20,4},{24,8},{28,12},{32,48},... | collective-permute-start | bytes 331784 | tf_op jit(solution)/shard_map/ppermute | solution.py:381
  60.5 1.9 %collective-permute-start.13 = (bf16[320,128]{1,0:T(8,128)(2,1)S(1)}, bf16[320,128]{1,0:T(8,128)(2,1)S(1)}, u32[]{:S(2)}, u32[]{:S(2)}) collective-permute-start(bf16[320,128]{1,0:T(8,128)(2,1)S(1)} %pad_maximum_fusion.5), channel_id=1, source_target_pairs={{0,112},{4,116},{8,120},{12,124},{16,32},{20,36},{24,40},{28,44},{... | collective-permute-start | bytes 245768 | tf_op jit(solution)/shard_map/ppermute | solution.py:373
  62.4 2.2 %collective-permute-start.12 = (bf16[320,128]{1,0:T(8,128)(2,1)S(1)}, bf16[320,128]{1,0:T(8,128)(2,1)S(1)}, u32[]{:S(2)}, u32[]{:S(2)}) collective-permute-start(bf16[320,128]{1,0:T(8,128)(2,1)S(1)} %pad_maximum_fusion.4), channel_id=1, source_target_pairs={{0,16},{4,20},{8,24},{12,28},{16,0},{20,4},{24,8},{28,12},{32,48},... | collective-permute-start | bytes 245768 | tf_op jit(solution)/shard_map/ppermute | solution.py:373
  64.6 2.4 %backward.6.refs_2_ = f32[256,128]{1,0:T(8,128)S(1)} custom-call(bf16[1024,128]{1,0:T(8,128)(2,1)S(1)} %copy-done.9, s32[27,1024]{1,0:T(8,128)S(1)} %bitcast.51, bf16[27,128,128]{2,1,0:T(8,128)(2,1)S(1)} %bitcast.39), custom_call_target="tpu_custom_call" | custom-call | flops 3000000000 | bytes 2000000 | tf_op jit(solution)/shard_map/backward/pallas_call | solution.py:454
  67.1 0.0 collective-permute-done.8
  67.1 2.0 %collective-permute-start.9 = (bf16[432,128]{1,0:T(8,128)(2,1)S(1)}, bf16[432,128]{1,0:T(8,128)(2,1)S(1)}, u32[]{:S(2)}, u32[]{:S(2)}) collective-permute-start(bf16[432,128]{1,0:T(8,128)(2,1)S(1)} %add_convert_fusion.1), channel_id=1, source_target_pairs={{0,64},{4,68},{8,72},{12,76},{16,80},{20,84},{24,88},{28,92},{32,9... | collective-permute-start | bytes 331784 | tf_op jit(solution)/shard_map/ppermute | solution.py:381
  69.1 1.3 %collective-permute-start.15 = (bf16[1024,128]{1,0:T(8,128)(2,1)S(1)}, bf16[1024,128]{1,0:T(8,128)(2,1)S(1)}, u32[]{:S(2)}, u32[]{:S(2)}) collective-permute-start(bf16[1024,128]{1,0:T(8,128)(2,1)S(1)} %get-tuple-element.67.refs_6_), channel_id=1, source_target_pairs={{0,1},{1,0},{2,3},{3,2},{4,5},{5,4},{6,7},{7,6},{8,9},{9,8},{10,11... | collective-permute-start | bytes 786440 | tf_op jit(solution)/shard_map/ppermute | solution.py:377
  70.4 0.0 collective-permute-done.13.iyb_ref
  70.4 0.0 collective-permute-done.12.iya_ref
  70.4 3.0 %returning.1.refs_4_ = f32[1152,128]{1,0:T(8,128)S(1)} custom-call(s32[2]{0:T(128)S(1)} %pad_add_fusion.side_ref, bf16[320,128]{1,0:T(8,128)(2,1)S(1)} %collective-permute-done.10.ixa_ref, bf16[320,128]{1,0:T(8,128)(2,1)S(1)} %collective-permute-done.11.ixb_ref, bf16[320,128]{1,0:T(8,128)(2,1)S(1)} %collective-permute-done.12.iya_ref, ...), custom_call_target="tpu_custom_call" | custom-call | flops 3000000000 | bytes 4000000 | tf_op jit(solution)/shard_map/returning/pallas_call | solution.py:488
  73.4 0.0 collective-permute-done.9
  73.4 0.6 collective-permute-start.14
  74.0 2.4 %backward.7.refs_3_ = f32[256,128]{1,0:T(8,128)S(1)} custom-call(bf16[1024,128]{1,0:T(8,128)(2,1)S(1)} %copy-done.9, s32[27,1024]{1,0:T(8,128)S(1)} %bitcast.52, bf16[27,128,128]{2,1,0:T(8,128)(2,1)S(1)} %bitcast.41), custom_call_target="tpu_custom_call" | custom-call | flops 3000000000 | bytes 2000000 | tf_op jit(solution)/shard_map/backward/pallas_call | solution.py:454
  76.5 0.9 %collective-permute-done.14.one_ref = bf16[432,128]{1,0:T(8,128)(2,1)S(1)} collective-permute-done((bf16[432,128]{1,0:T(8,128)(2,1)S(1)}, bf16[432,128]{1,0:T(8,128)(2,1)S(1)}, u32[]{:S(2)}, u32[]{:S(2)}) %collective-permute-start.14) | collective-permute-done | bytes 110624 | tf_op jit(solution)/shard_map/ppermute | solution.py:381
  77.4 0.4 collective-permute-start.16
  77.8 0.0 collective-permute-done.15.refs_7_
  77.8 1.7 %final.1 = (bf16[1024,128]{1,0:T(8,128)(2,1)}, bf16[1024,128]{1,0:T(8,128)(2,1)}) custom-call(f32[256,128]{1,0:T(8,128)S(1)} %backward.4.refs_0_, f32[256,128]{1,0:T(8,128)S(1)} %backward.5.refs_1_, f32[256,128]{1,0:T(8,128)S(1)} %backward.6.refs_2_, f32[256,128]{1,0:T(8,128)S(1)} %backward.7.refs_3_, f32[1152,128]{1,0:T(8,128)S(1)} %returning.1.refs_4_, ...), custom_call_target="tpu_custom_call" | custom-call | flops 1000000000 | bytes 3000000 | tf_op jit(solution)/shard_map/final/pallas_call | solution.py:501
  79.5 2.8 %collective-permute-done.16.two_ref = bf16[2,432,128]{2,1,0:T(8,128)(2,1)S(1)} collective-permute-done((bf16[2,432,128]{2,1,0:T(8,128)(2,1)S(1)}, bf16[2,432,128]{2,1,0:T(8,128)(2,1)S(1)}, u32[]{:S(2)}, u32[]{:S(2)}) %collective-permute-start.16) | collective-permute-done | bytes 221216 | tf_op jit(solution)/shard_map/ppermute | solution.py:381
  82.3 4.3 %collective-permute-start.17 = (bf16[4,432,128]{2,1,0:T(8,128)(2,1)S(1)}, bf16[4,432,128]{2,1,0:T(8,128)(2,1)S(1)}, u32[]{:S(2)}, u32[]{:S(2)}) collective-permute-start(bf16[4,432,128]{2,1,0:T(8,128)(2,1)S(1)} %pad_maximum_fusion), channel_id=1, source_target_pairs={{0,4},{4,0},{8,12},{12,8},{16,20},{20,16},{24,28},{28,24},{32,36},... | collective-permute-start | bytes 1327112 | tf_op jit(solution)/shard_map/ppermute | solution.py:381
  86.6 0.1 pad_add_fusion.1.bits_ref
  86.7 1.3 %collective-permute-done.17.four_ref = bf16[4,432,128]{2,1,0:T(8,128)(2,1)S(1)} collective-permute-done((bf16[4,432,128]{2,1,0:T(8,128)(2,1)S(1)}, bf16[4,432,128]{2,1,0:T(8,128)(2,1)S(1)}, u32[]{:S(2)}, u32[]{:S(2)}) %collective-permute-start.17) | collective-permute-done | bytes 442400 | tf_op jit(solution)/shard_map/ppermute | solution.py:381
  88.0 1.9 %assemble.1 = f32[8,432,128]{2,1,0:T(8,128)} custom-call(s32[3]{0:T(128)S(1)} %pad_add_fusion.1.bits_ref, bf16[432,128]{1,0:T(8,128)(2,1)S(1)} %add_convert_fusion.own_ref, bf16[432,128]{1,0:T(8,128)(2,1)S(1)} %collective-permute-done.14.one_ref, bf16[2,432,128]{2,1,0:T(8,128)(2,1)S(1)} %collective-permute-done.16.two_ref, ...), custom_call_target="tpu_custom_call" | custom-call | flops 1000000 | bytes 3000000 | tf_op jit(solution)/shard_map/assemble/pallas_call | solution.py:510
  (28 shorter events, 0.3 us)
Async XLA Ops:
  1.4 0.9 %copy-start.2 = (bf16[1,1024,128]{2,1,0:T(8,128)(2,1)S(1)}, bf16[1,1024,128]{2,1,0:T(8,128)(2,1)}, u32[]{:S(2)}) copy-start(bf16[1,1024,128]{2,1,0:T(8,128)(2,1)} %param.6) | copy-start | bytes 786436
  2.4 0.9 %copy-start.4 = (s32[1152,27]{0,1:T(8,128)S(1)}, s32[1152,27]{0,1:T(8,128)}, u32[]{:S(2)}) copy-start(s32[1152,27]{0,1:T(8,128)} %param.10) | copy-start | bytes 373252
  3.3 5.5 %copy-start.1 = (bf16[1,1024,128]{2,1,0:T(8,128)(2,1)S(1)}, bf16[1,1024,128]{2,1,0:T(8,128)(2,1)}, u32[]{:S(2)}) copy-start(bf16[1,1024,128]{2,1,0:T(8,128)(2,1)} %param.8) | copy-start | bytes 786436
  3.3 15.7 %copy-start = (bf16[1,27,128,128]{3,2,1,0:T(8,128)(2,1)S(1)}, bf16[1,27,128,128]{3,2,1,0:T(8,128)(2,1)}, u32[]{:S(2)}) copy-start(bf16[1,27,128,128]{3,2,1,0:T(8,128)(2,1)} %param.7) | copy-start | bytes 2654212
  3.3 15.7 %copy-start.3 = (bf16[1,1024,128]{2,1,0:T(8,128)(2,1)S(1)}, bf16[1,1024,128]{2,1,0:T(8,128)(2,1)}, u32[]{:S(2)}) copy-start(bf16[1,1024,128]{2,1,0:T(8,128)(2,1)} %param.6) | copy-start | bytes 786436
  3.3 15.7 %copy-start.5 = (s32[1024,27]{0,1:T(8,128)S(1)}, s32[1024,27]{0,1:T(8,128)}, u32[]{:S(2)}) copy-start(s32[1024,27]{0,1:T(8,128)} %param.9) | copy-start | bytes 331780
  5.6 0.6 copy-start.10
  6.2 3.9 %collective-permute-start = (bf16[384,128]{1,0:T(8,128)(2,1)S(1)}, bf16[384,128]{1,0:T(8,128)(2,1)S(1)}, u32[]{:S(2)}, u32[]{:S(2)}) collective-permute-start(bf16[384,128]{1,0:T(8,128)(2,1)S(1)} %get-tuple-element.38), channel_id=1, source_target_pairs={{0,4},{4,0},{8,12},{12,8},{16,20},{20,16},{24,28},{28,24},{32,36},... | collective-permute-start | bytes 294920 | tf_op jit(solution)/shard_map/ppermute | solution.py:364
  7.7 4.4 %collective-permute-start.1 = (bf16[384,128]{1,0:T(8,128)(2,1)S(1)}, bf16[384,128]{1,0:T(8,128)(2,1)S(1)}, u32[]{:S(2)}, u32[]{:S(2)}) collective-permute-start(bf16[384,128]{1,0:T(8,128)(2,1)S(1)} %get-tuple-element.39), channel_id=1, source_target_pairs={{0,12},{4,8},{8,4},{12,0},{16,28},{20,24},{24,20},{28,16},{32,44},... | collective-permute-start | bytes 294920 | tf_op jit(solution)/shard_map/ppermute | solution.py:364
  8.8 21.0 %collective-permute-start.4 = (bf16[1024,128]{1,0:T(8,128)(2,1)S(1)}, bf16[1024,128]{1,0:T(8,128)(2,1)S(1)}, u32[]{:S(2)}, u32[]{:S(2)}) collective-permute-start(bf16[1024,128]{1,0:T(8,128)(2,1)S(1)} %bitcast.42), channel_id=1, source_target_pairs={{0,1},{1,0},{2,3},{3,2},{4,5},{5,4},{6,7},{7,6},{8,9},{9,8},{10,11... | collective-permute-start | bytes 786440 | tf_op jit(solution)/shard_map/ppermute | solution.py:377
  12.1 17.8 %collective-permute-start.2 = (bf16[384,128]{1,0:T(8,128)(2,1)S(1)}, bf16[384,128]{1,0:T(8,128)(2,1)S(1)}, u32[]{:S(2)}, u32[]{:S(2)}) collective-permute-start(bf16[384,128]{1,0:T(8,128)(2,1)S(1)} %pad_maximum_fusion.2), channel_id=1, source_target_pairs={{0,16},{4,20},{8,24},{12,28},{16,0},{20,4},{24,8},{28,12},{32,48},... | collective-permute-start | bytes 294920 | tf_op jit(solution)/shard_map/ppermute | solution.py:373
  15.3 14.6 %collective-permute-start.3 = (bf16[384,128]{1,0:T(8,128)(2,1)S(1)}, bf16[384,128]{1,0:T(8,128)(2,1)S(1)}, u32[]{:S(2)}, u32[]{:S(2)}) collective-permute-start(bf16[384,128]{1,0:T(8,128)(2,1)S(1)} %pad_maximum_fusion.3), channel_id=1, source_target_pairs={{0,112},{4,116},{8,120},{12,124},{16,32},{20,36},{24,40},{28,44},{... | collective-permute-start | bytes 294920 | tf_op jit(solution)/shard_map/ppermute | solution.py:373
  36.6 4.5 %copy-start.6 = (bf16[320,128]{1,0:T(8,128)(2,1)}, bf16[320,128]{1,0:T(8,128)(2,1)S(1)}, u32[]{:S(2)}) copy-start(bf16[320,128]{1,0:T(8,128)(2,1)S(1)} %get-tuple-element.54) | copy-start | bytes 245764
  36.6 4.5 %copy-start.8 = (bf16[1024,128]{1,0:T(8,128)(2,1)}, bf16[1024,128]{1,0:T(8,128)(2,1)S(1)}, u32[]{:S(2)}) copy-start(bf16[1024,128]{1,0:T(8,128)(2,1)S(1)} %get-tuple-element.63.grad_ref) | copy-start | bytes 786436
  41.2 5.6 %copy-start.7 = (bf16[320,128]{1,0:T(8,128)(2,1)S(1)}, bf16[320,128]{1,0:T(8,128)(2,1)}, u32[]{:S(2)}) copy-start(bf16[320,128]{1,0:T(8,128)(2,1)} %copy-done.6) | copy-start | bytes 245764
  42.0 2.3 %collective-permute-start.5 = (bf16[2,2,432,128]{3,2,1,0:T(8,128)(2,1)}, bf16[2,2,432,128]{3,2,1,0:T(8,128)(2,1)}, u32[]{:S(2)}, u32[]{:S(2)}) collective-permute-start(bf16[2,2,432,128]{3,2,1,0:T(8,128)(2,1)} %fusion), channel_id=1, source_target_pairs={{0,4},{4,0},{8,12},{12,8},{16,20},{20,16},{24,28},{28,24},{32,36},... | collective-permute-start | bytes 1327112 | tf_op jit(solution)/shard_map/ppermute | solution.py:381
  42.5 5.0 %copy-start.9 = (bf16[1024,128]{1,0:T(8,128)(2,1)S(1)}, bf16[1024,128]{1,0:T(8,128)(2,1)}, u32[]{:S(2)}) copy-start(bf16[1024,128]{1,0:T(8,128)(2,1)} %copy-done.8) | copy-start | bytes 786436
  45.4 9.0 %collective-permute-start.6 = (bf16[2,432,128]{2,1,0:T(8,128)(2,1)S(1)}, bf16[2,432,128]{2,1,0:T(8,128)(2,1)S(1)}, u32[]{:S(2)}, u32[]{:S(2)}) collective-permute-start(bf16[2,432,128]{2,1,0:T(8,128)(2,1)S(1)} %fusion.1), channel_id=1, source_target_pairs={{0,8},{4,12},{8,0},{12,4},{16,24},{20,28},{24,16},{28,20},{32,40},... | collective-permute-start | bytes 663560 | tf_op jit(solution)/shard_map/ppermute | solution.py:381
  46.8 7.6 %collective-permute-start.11 = (bf16[320,128]{1,0:T(8,128)(2,1)S(1)}, bf16[320,128]{1,0:T(8,128)(2,1)S(1)}, u32[]{:S(2)}, u32[]{:S(2)}) collective-permute-start(bf16[320,128]{1,0:T(8,128)(2,1)S(1)} %copy-done.7), channel_id=1, source_target_pairs={{0,12},{4,8},{8,4},{12,0},{16,28},{20,24},{24,20},{28,16},{32,44},... | collective-permute-start | bytes 245768 | tf_op jit(solution)/shard_map/ppermute | solution.py:364
  50.0 4.5 %collective-permute-start.10 = (bf16[320,128]{1,0:T(8,128)(2,1)S(1)}, bf16[320,128]{1,0:T(8,128)(2,1)S(1)}, u32[]{:S(2)}, u32[]{:S(2)}) collective-permute-start(bf16[320,128]{1,0:T(8,128)(2,1)S(1)} %get-tuple-element.52), channel_id=1, source_target_pairs={{0,4},{4,0},{8,12},{12,8},{16,20},{20,16},{24,28},{28,24},{32,36},... | collective-permute-start | bytes 245768 | tf_op jit(solution)/shard_map/ppermute | solution.py:364
  54.6 4.8 %collective-permute-start.7 = (bf16[432,128]{1,0:T(8,128)(2,1)S(1)}, bf16[432,128]{1,0:T(8,128)(2,1)S(1)}, u32[]{:S(2)}, u32[]{:S(2)}) collective-permute-start(bf16[432,128]{1,0:T(8,128)(2,1)S(1)} %fusion.3), channel_id=1, source_target_pairs={{0,32},{4,36},{8,40},{12,44},{16,48},{20,52},{24,56},{28,60},{32,0... | collective-permute-start | bytes 331784 | tf_op jit(solution)/shard_map/ppermute | solution.py:381
  59.4 7.7 %collective-permute-start.8 = (bf16[432,128]{1,0:T(8,128)(2,1)S(1)}, bf16[432,128]{1,0:T(8,128)(2,1)S(1)}, u32[]{:S(2)}, u32[]{:S(2)}) collective-permute-start(bf16[432,128]{1,0:T(8,128)(2,1)S(1)} %fusion.2), channel_id=1, source_target_pairs={{0,16},{4,20},{8,24},{12,28},{16,0},{20,4},{24,8},{28,12},{32,48},... | collective-permute-start | bytes 331784 | tf_op jit(solution)/shard_map/ppermute | solution.py:381
  60.5 9.9 %collective-permute-start.13 = (bf16[320,128]{1,0:T(8,128)(2,1)S(1)}, bf16[320,128]{1,0:T(8,128)(2,1)S(1)}, u32[]{:S(2)}, u32[]{:S(2)}) collective-permute-start(bf16[320,128]{1,0:T(8,128)(2,1)S(1)} %pad_maximum_fusion.5), channel_id=1, source_target_pairs={{0,112},{4,116},{8,120},{12,124},{16,32},{20,36},{24,40},{28,44},{... | collective-permute-start | bytes 245768 | tf_op jit(solution)/shard_map/ppermute | solution.py:373
  62.4 8.0 %copy-start.11 = (bf16[4,32,128]{2,1,0:T(8,128)(2,1)S(1)}, bf16[4,32,128]{2,1,0:T(8,128)(2,1)}, u32[]{:S(2)}) copy-start(bf16[4,32,128]{2,1,0:T(8,128)(2,1)} %copy-done.10) | copy-start | bytes 98308
  62.4 8.0 %collective-permute-start.12 = (bf16[320,128]{1,0:T(8,128)(2,1)S(1)}, bf16[320,128]{1,0:T(8,128)(2,1)S(1)}, u32[]{:S(2)}, u32[]{:S(2)}) collective-permute-start(bf16[320,128]{1,0:T(8,128)(2,1)S(1)} %pad_maximum_fusion.4), channel_id=1, source_target_pairs={{0,16},{4,20},{8,24},{12,28},{16,0},{20,4},{24,8},{28,12},{32,48},... | collective-permute-start | bytes 245768 | tf_op jit(solution)/shard_map/ppermute | solution.py:373
  67.1 6.2 %collective-permute-start.9 = (bf16[432,128]{1,0:T(8,128)(2,1)S(1)}, bf16[432,128]{1,0:T(8,128)(2,1)S(1)}, u32[]{:S(2)}, u32[]{:S(2)}) collective-permute-start(bf16[432,128]{1,0:T(8,128)(2,1)S(1)} %add_convert_fusion.1), channel_id=1, source_target_pairs={{0,64},{4,68},{8,72},{12,76},{16,80},{20,84},{24,88},{28,92},{32,9... | collective-permute-start | bytes 331784 | tf_op jit(solution)/shard_map/ppermute | solution.py:381
  69.1 8.7 %collective-permute-start.15 = (bf16[1024,128]{1,0:T(8,128)(2,1)S(1)}, bf16[1024,128]{1,0:T(8,128)(2,1)S(1)}, u32[]{:S(2)}, u32[]{:S(2)}) collective-permute-start(bf16[1024,128]{1,0:T(8,128)(2,1)S(1)} %get-tuple-element.67.refs_6_), channel_id=1, source_target_pairs={{0,1},{1,0},{2,3},{3,2},{4,5},{5,4},{6,7},{7,6},{8,9},{9,8},{10,11... | collective-permute-start | bytes 786440 | tf_op jit(solution)/shard_map/ppermute | solution.py:377
  73.4 4.0 %collective-permute-start.14 = (bf16[432,128]{1,0:T(8,128)(2,1)S(1)}, bf16[432,128]{1,0:T(8,128)(2,1)S(1)}, u32[]{:S(2)}, u32[]{:S(2)}) collective-permute-start(bf16[432,128]{1,0:T(8,128)(2,1)S(1)} %add_convert_fusion.own_ref), channel_id=1, source_target_pairs={{0,32},{4,36},{8,40},{12,44},{16,48},{20,52},{24,56},{28,60},{32,0... | collective-permute-start | bytes 331784 | tf_op jit(solution)/shard_map/ppermute | solution.py:381
  77.4 4.9 %collective-permute-start.16 = (bf16[2,432,128]{2,1,0:T(8,128)(2,1)S(1)}, bf16[2,432,128]{2,1,0:T(8,128)(2,1)S(1)}, u32[]{:S(2)}, u32[]{:S(2)}) collective-permute-start(bf16[2,432,128]{2,1,0:T(8,128)(2,1)S(1)} %pad_maximum_fusion.1), channel_id=1, source_target_pairs={{0,8},{4,12},{8,0},{12,4},{16,24},{20,28},{24,16},{28,20},{32,40},... | collective-permute-start | bytes 663560 | tf_op jit(solution)/shard_map/ppermute | solution.py:381
  82.3 5.7 %collective-permute-start.17 = (bf16[4,432,128]{2,1,0:T(8,128)(2,1)S(1)}, bf16[4,432,128]{2,1,0:T(8,128)(2,1)S(1)}, u32[]{:S(2)}, u32[]{:S(2)}) collective-permute-start(bf16[4,432,128]{2,1,0:T(8,128)(2,1)S(1)} %pad_maximum_fusion), channel_id=1, source_target_pairs={{0,4},{4,0},{8,12},{12,8},{16,20},{20,16},{24,28},{28,24},{32,36},... | collective-permute-start | bytes 1327112 | tf_op jit(solution)/shard_map/ppermute | solution.py:381

commit v5 on v4

--- a/solution.py
+++ b/solution.py
@@ -269,15 +269,22 @@
             dw_ref[toward(*DIRECTIONS[number])[step]] += part[:, index * C : (index + 1) * C]
 
 
-def weight_kernel(g_ref, grad_ref, x_ref, halo_ref, dw_ref):
+def weight_kernel(side_ref, g_ref, grad_ref, x_ref, halo_ref, kept_ref, sent_ref, total):
     step = pl.program_id(0)
 
     @pl.when(step == 0)
     def _():
-        dw_ref[13] = halo_ref[13] + dot(x_ref[...], grad_ref[...], ((0,), (0,)))
-
-    total = dot(g_ref[...], grad_ref[...])
-    dw_ref[pl.ds(14 * step, 13)] = halo_ref[pl.ds(14 * step, 13)] + total.reshape(13, C, C)
+        middle = halo_ref[13] + dot(x_ref[...], grad_ref[...], ((0,), (0,)))
+        total[13 * C : 14 * C, :] = middle
+
+    part = dot(g_ref[...], grad_ref[...]) + halo_ref[pl.ds(14 * step, 13)].reshape(13 * C, C)
+    total[pl.ds(pl.multiple_of(14 * C * step, 8), 13 * C), :] = part
+
+    @pl.when(step == 1)
+    def _():
+        half = kept_ref.shape[0]
+        kept_ref[...] = total[pl.ds(pl.multiple_of(side_ref[2] * half, 8), half), :]
+        sent_ref[...] = total[pl.ds(pl.multiple_of((1 - side_ref[2]) * half, 8), half), :].astype(BF)
 
 
 def return_kernel(side_ref, ixa_ref, ixb_ref, iya_ref, iyb_ref, face_p_ref, edge_p_ref, w_ref, placed_ref):
@@ -401,7 +408,7 @@
     sm = send_map.T
     rr = recv_map.reshape(1, HALO)
     me = lax.axis_index("space")
-    sides = jnp.stack([me % 2, me // TILES_X % 2]).astype(jnp.int32)
+    sides = jnp.stack([me % 2, me // TILES_X % 2, me % 2]).astype(jnp.int32)
     smem = pl.BlockSpec(memory_space=pltpu.SMEM)
     vmem = pl.BlockSpec(memory_space=pltpu.VMEM)
     def lists_shape(face, edge):
@@ -437,16 +444,18 @@
         cost_estimate=cost(4e9, 3e6),
         name="activate",
     )(sides, pre, *in_x, *in_y, rr, cot, cot_pair, w)
-    dw = pl.pallas_call(
+    half = 27 * C // 2
+    kept, sent = pl.pallas_call(
         weight_kernel,
         grid=(2,),
-        in_specs=[pl.BlockSpec((13 * C, ROWS), lambda j: (j, 0)), whole((ROWS, C)), whole((ROWS, C)), whole((27, C, C))],
-        out_specs=whole((27, C, C)),
-        out_shape=shape((27, C, C), F32),
+        in_specs=[smem, pl.BlockSpec((13 * C, ROWS), lambda j: (j, 0)), whole((ROWS, C)), whole((ROWS, C)), whole((27, C, C))],
+        out_specs=[whole((half, C)), whole((half, C))],
+        out_shape=[shape((half, C), F32), shape((half, C), BF)],
+        scratch_shapes=[pltpu.VMEM((27 * C, C), F32)],
         compiler_params=PARAMS,
         cost_estimate=cost(4e9, 9e6),
         name="weight",
-    )(gathered, grad, x, dw_halo)
+    )(sides, gathered, grad, x, dw_halo)
 
     size = ROWS // 4
 
@@ -459,8 +468,7 @@
             name="backward",
         )(grad, lm, w)
 
-    bits = [me % 2, me // 2 % 2, me // 8 % 2]
-    blocks = dw.reshape(2, 2, 2, -1, C)
+    bits = [me % 2, (me // 2 + me // 4) % 2, (me // 8 + me // 16) % 2]
 
     def halve(blocks, stage):
         return pick(blocks, bits[stage]), pick(blocks, 1 - bits[stage]).astype(BF)
@@ -469,22 +477,24 @@
         return one.astype(F32) + two.astype(F32)
 
     locals_ = []
-    kept, sent = halve(blocks, 0)
     got = xor_send(sent, 1)
-    kept, sent = halve(plus(kept, got), 1)
+    kept, sent = halve(plus(kept, got).reshape(2, 2, -1, C), 1)
     got = xor_send(sent, 2)
+    locals_.append(backward(0, tie(grad, sent)))
+    locals_.append(backward(1, tie(grad, locals_[0])))
+    kept, sent = halve(plus(kept, tie(got, locals_[1])), 2)
+    got = xor_send(sent, 8)
     in_x = exchange_x(tie(xa, sent), tie(xb, sent))
-    locals_.append(backward(0, tie(grad, sent)))
-    kept, sent = halve(plus(kept, tie(got, locals_[0])), 2)
-    got = xor_send(sent, 8)
-    locals_.append(backward(1, tie(grad, sent)))
-    own = plus(kept, tie(got, locals_[1])).astype(BF)
-    got = xor_send(own, 4)
-    in_y = exchange_y(tie(ya, own), tie(yb, own), *in_x, sides, CAP, TZ)
+    own = plus(kept, got).astype(BF)
+    got = xor_send(own, 6)
+    act_pair = swapped(tie(act, own))
     locals_.append(backward(2, tie(grad, own)))
     own = plus(own, tie(got, locals_[2])).astype(BF)
-    got = xor_send(own, 16)
-    act_pair = swapped(tie(act, own))
+    got = xor_send(own, 24)
+    in_y = exchange_y(tie(ya, own), tie(yb, own), *[tie(v, own) for v in in_x], sides, CAP, TZ)
+    locals_.append(backward(3, tie(grad, own)))
+    own = plus(own, tie(got, locals_[3])).astype(BF)
+    one = xor_send(own, 8)
     placed = pl.pallas_call(
         return_kernel,
         in_specs=[smem] + [vmem] * 7,
@@ -493,10 +503,7 @@
         cost_estimate=cost(3e9, 4e6),
         name="returning",
     )(sides, *in_x, *in_y, face_p, edge_p, tie(w, own))
-    own = plus(own, tie(got, placed)).astype(BF)
-    one = xor_send(own, 8)
-    locals_.append(backward(3, tie(grad, own)))
-    one = tie(one, locals_[3])
+    one = tie(one, placed)
     two = xor_send(jnp.stack([own, one]), 2)
     mixed, input_grad = pl.pallas_call(
         final_kernel,
@@ -515,7 +522,7 @@
         cost_estimate=cost(1e6, 3e6),
         name="assemble",
     )(jnp.stack(bits).astype(jnp.int32), own, one, two, four)
-    return (mixed[None], input_grad[None], weight_grad.reshape(dw.shape)[None])
+    return (mixed[None], input_grad[None], weight_grad.reshape(w.shape)[None])
 
 
 def solution(mesh):

time: 90.1 us -> 90.3 us (level)
  starting transfers between devices: 27.3 us -> 30.1 us
  local copies, waits for them, and re-layouts: 4.09 us -> 2.64 us
  waiting for transfers between devices: 15.4 us -> 14.2 us
    ppermute x4, waiting for transfers between devices: 0.01 us -> 2.83 us  [exchange_y(): lax.ppermute(v, 'space', pairing('y', n))]
    ppermute x4, waiting for transfers between devices: 6.27 us -> 3.6 us  [exchange_x(): lax.ppermute(v, 'space', pairing('x', n))]
    ppermute x4, starting transfers between devices: 3.41 us -> 5.43 us  [exchange_x(): lax.ppermute(v, 'space', pairing('x', n))]
    ppermute x8, waiting for transfers between devices: 9.09 us -> 7.81 us  [xor_send(): lax.ppermute(value, 'space', [(i, i ^ bits) for i in range(lax.axis_size(...]
    ppermute x8, starting transfers between devices: 10.2 us -> 11.2 us  [xor_send(): lax.ppermute(value, 'space', [(i, i ^ bits) for i in range(lax.axis_size(...]
    ppermute x2, starting transfers between devices: 2.58 us -> 1.65 us  [swapped(): lax.ppermute(array, 'segment', [(i, i ^ 1) for i in range(lax.axis_size('...]
    unnamed x24 -> x12, local copies, waits for them, and re-layouts: 2.5 us -> 1.88 us
  transfers between devices with their start and end apart: 18 -> 18, of which waited for: 7 -> 8; matrix products, arithmetic and copies ran while one was open for 0% -> 0% of each run, Pallas kernels for 28% -> 28%
where the time goes in v5:
time: 90.3 us; the launch traced here: 90.1 us
  Pallas kernels  40.7 us (45%)
  starting transfers between devices  30.1 us (33%)
  waiting for transfers between devices  14.2 us (16%)
  local copies, waits for them, and re-layouts  2.64 us (3%)
  other arithmetic  1.49 us (2%)
    ppermute x4, starting transfers between devices, exchange_y(): lax.ppermute(v, 'space', pairing('y', n))  11.8 us
    ppermute x8, starting transfers between devices, xor_send(): lax.ppermute(value, 'space', [(i, i ^ bits) for i in range(lax.axis_size(...  11.2 us
    pallas_call x1, Pallas kernels, on_device(): pl.pallas_call(functools.partial(forward_kernel, width=512), grid=(2,), i...  10.8 us
    pallas_call x4, Pallas kernels, backward(): pl.pallas_call(functools.partial(backward_kernel, begin=index * size), ou...  9.79 us
    ppermute x8, waiting for transfers between devices, xor_send(): lax.ppermute(value, 'space', [(i, i ^ bits) for i in range(lax.axis_size(...  7.81 us
    pallas_call x1, Pallas kernels, on_device(): pl.pallas_call(activate_kernel, in_specs=[smem] + [vmem] * 9, out_shape=[...  6.77 us
    ppermute x4, starting transfers between devices, exchange_x(): lax.ppermute(v, 'space', pairing('x', n))  5.43 us
    pallas_call x1, Pallas kernels, on_device(): pl.pallas_call(weight_kernel, grid=(2,), in_specs=[smem, pl.BlockSpec((13...  4.54 us
  transfers between devices with their start and end apart: 18, of which 8 were waited for; matrix products, arithmetic and copies ran while one was open for 0% of the time, Pallas kernels for 28%

profile of v5, /device:TPU:1, one launch (start us, length us, event | category | flops | bytes accessed | tf_op | source)
XLA Modules:
  0.0 90.1 jit_solution(6726660543266682944)
XLA Ops:
  0.7 0.7 reshape.14.rr_ref.refs_5_
  1.4 0.1 pad_add_fusion.side_ref
  1.4 0.0 copy-start.2
  1.4 0.9 %copy-done.2 = bf16[1,1024,128]{2,1,0:T(8,128)(2,1)S(1)} copy-done((bf16[1,1024,128]{2,1,0:T(8,128)(2,1)S(1)}, bf16[1,1024,128]{2,1,0:T(8,128)(2,1)}, u32[]{:S(2)}) %copy-start.2) | copy-done | bytes 262168
  2.4 0.0 copy-start.4
  2.4 0.9 %copy-done.4 = s32[1152,27]{0,1:T(8,128)S(1)} copy-done((s32[1152,27]{0,1:T(8,128)S(1)}, s32[1152,27]{0,1:T(8,128)}, u32[]{:S(2)}) %copy-start.4) | copy-done | bytes 124440
  3.3 0.0 copy-start.1
  3.3 0.0 copy-start
  3.3 0.0 copy-start.3
  3.3 0.0 copy-start.5
  3.3 2.3 %start.1 = (bf16[384,128]{1,0:T(8,128)(2,1)S(1)}, bf16[384,128]{1,0:T(8,128)(2,1)S(1)}, bf16[288,128]{1,0:T(8,128)(2,1)S(1)}, bf16[288,128]{1,0:T(8,128)(2,1)S(1...) custom-call(s32[3]{0:T(128)S(1)} %pad_add_fusion.side_ref, bf16[1024,128]{1,0:T(8,128)(2,1)S(1)} %bitcast.38, ...), custom_call_target="tpu_custom_call" | custom-call | flops 2000000000 | bytes 4000000 | tf_op jit(solution)/shard_map/start/pallas_call | solution.py:417
  5.6 1.5 %collective-permute-start = (bf16[384,128]{1,0:T(8,128)(2,1)S(1)}, bf16[384,128]{1,0:T(8,128)(2,1)S(1)}, u32[]{:S(2)}, u32[]{:S(2)}) collective-permute-start(bf16[384,128]{1,0:T(8,128)(2,1)S(1)} %get-tuple-element.41), channel_id=1, source_target_pairs={{0,4},{4,0},{8,12},{12,8},{16,20},{20,16},{24,28},{28,24},{32,36},... | collective-permute-start | bytes 294920 | tf_op jit(solution)/shard_map/ppermute | solution.py:371
  7.1 0.0 copy-done.1
  7.1 1.4 %collective-permute-start.4 = (bf16[1024,128]{1,0:T(8,128)(2,1)S(1)}, bf16[1024,128]{1,0:T(8,128)(2,1)S(1)}, u32[]{:S(2)}, u32[]{:S(2)}) collective-permute-start(bf16[1024,128]{1,0:T(8,128)(2,1)S(1)} %bitcast.36), channel_id=1, source_target_pairs={{0,1},{1,0},{2,3},{3,2},{4,5},{5,4},{6,7},{7,6},{8,9},{9,8},{10,11... | collective-permute-start | bytes 786440 | tf_op jit(solution)/shard_map/ppermute | solution.py:384
  8.5 1.5 %collective-permute-start.1 = (bf16[384,128]{1,0:T(8,128)(2,1)S(1)}, bf16[384,128]{1,0:T(8,128)(2,1)S(1)}, u32[]{:S(2)}, u32[]{:S(2)}) collective-permute-start(bf16[384,128]{1,0:T(8,128)(2,1)S(1)} %get-tuple-element.42), channel_id=1, source_target_pairs={{0,12},{4,8},{8,4},{12,0},{16,28},{20,24},{24,20},{28,16},{32,44},... | collective-permute-start | bytes 294920 | tf_op jit(solution)/shard_map/ppermute | solution.py:371
  10.0 0.0 collective-permute-done.ixa_ref
  10.0 3.6 %collective-permute-done.1.ixb_ref = bf16[384,128]{1,0:T(8,128)(2,1)S(1)} collective-permute-done((bf16[384,128]{1,0:T(8,128)(2,1)S(1)}, bf16[384,128]{1,0:T(8,128)(2,1)S(1)}, u32[]{:S(2)}, u32[]{:S(2)}) %collective-permute-start.1) | collective-permute-done | bytes 98336 | tf_op jit(solution)/shard_map/ppermute | solution.py:371
  13.6 2.8 %collective-permute-start.2 = (bf16[384,128]{1,0:T(8,128)(2,1)S(1)}, bf16[384,128]{1,0:T(8,128)(2,1)S(1)}, u32[]{:S(2)}, u32[]{:S(2)}) collective-permute-start(bf16[384,128]{1,0:T(8,128)(2,1)S(1)} %pad_maximum_fusion.2), channel_id=1, source_target_pairs={{0,16},{4,20},{8,24},{12,28},{16,0},{20,4},{24,8},{28,12},{32,48},... | collective-permute-start | bytes 294920 | tf_op jit(solution)/shard_map/ppermute | solution.py:380
  16.4 4.0 %collective-permute-start.3 = (bf16[384,128]{1,0:T(8,128)(2,1)S(1)}, bf16[384,128]{1,0:T(8,128)(2,1)S(1)}, u32[]{:S(2)}, u32[]{:S(2)}) collective-permute-start(bf16[384,128]{1,0:T(8,128)(2,1)S(1)} %pad_maximum_fusion.3), channel_id=1, source_target_pairs={{0,112},{4,116},{8,120},{12,124},{16,32},{20,36},{24,40},{28,44},{... | collective-permute-start | bytes 294920 | tf_op jit(solution)/shard_map/ppermute | solution.py:380
  20.4 0.0 copy-done
  20.4 0.0 copy-done.3
  20.4 0.0 copy-done.5
  20.4 10.8 %forward.1 = (bf16[3328,1024]{1,0:T(8,128)(2,1)}, f32[1024,128]{1,0:T(8,128)S(1)}) custom-call(bf16[1024,128]{1,0:T(8,128)(2,1)S(1)} %bitcast.39, s32[27,1024]{1,0:T(8,128)S(1)} %bitcast.42, bf16[27,128,128]{2,1,0:T(8,128)(2,1)S(1)} %bitcast.29), custom_call_target="tpu_custom_call" | custom-call | flops 15000000512 | bytes 9000000 | tf_op jit(solution)/shard_map/forward/pallas_call | solution.py:428
  31.2 0.0 collective-permute-done.2.iya_ref
  31.2 0.0 collective-permute-done.3.iyb_ref
  31.2 0.0 collective-permute-done.4.pair_ref
  31.2 6.8 %activate.1 = (bf16[1024,128]{1,0:T(8,128)(2,1)S(1)}, bf16[1024,128]{1,0:T(8,128)(2,1)S(1)}, bf16[320,128]{1,0:T(8,128)(2,1)S(1)}, bf16[320,128]{1,0:T(8,128)(2,...) custom-call(s32[3]{0:T(128)S(1)} %pad_add_fusion.side_ref, ...), custom_call_target="tpu_custom_call" | custom-call | flops 4000000000 | bytes 3000000 | tf_op jit(solution)/shard_map/activate/pallas_call | solution.py:439
  38.0 4.5 %weight.1 = (f32[1728,128]{1,0:T(8,128)S(1)}, bf16[1728,128]{1,0:T(8,128)(2,1)S(1)}) custom-call(s32[3]{0:T(128)S(1)} %pad_add_fusion.side_ref, bf16[3328,1024]{1,0:T(8,128)(2,1)} %get-tuple-element.46.g_ref, bf16[1024,128]{1,0:T(8,128)(2,1)S(1)} %get-tuple-element.55.grad_ref, bf16[1024,128]{1,0:T(8,128)(2,1)S(1)} %bitcast.40, ...), custom_call_target="tpu_custom_call" | custom-call | flops 4000000000 | bytes 9000000 | tf_op jit(solution)/shard_map/weight/pallas_call | solution.py:448
  42.5 0.7 collective-permute-start.5
  43.2 1.6 %collective-permute-done.5 = bf16[1728,128]{1,0:T(8,128)(2,1)} collective-permute-done((bf16[1728,128]{1,0:T(8,128)(2,1)S(1)}, bf16[1728,128]{1,0:T(8,128)(2,1)}, u32[]{:S(2)}, u32[]{:S(2)}) %collective-permute-start.5) | collective-permute-done | bytes 442400 | tf_op jit(solution)/shard_map/ppermute | solution.py:388
  44.8 1.1 %convert_add_fusion = f32[1728,128]{1,0:T(8,128)S(1)} fusion(f32[1728,128]{1,0:T(8,128)S(1)} %get-tuple-element.48, bf16[1728,128]{1,0:T(8,128)(2,1)} %collective-permute-done.5), kind=kLoop, calls=%fused_computation | loop fusion | flops 442368 | bytes 2211840 | tf_op jit(solution)/shard_map/add | solution.py:477
  45.9 1.5 %collective-permute-start.6 = (bf16[2,432,128]{2,1,0:T(8,128)(2,1)S(1)}, bf16[2,432,128]{2,1,0:T(8,128)(2,1)S(1)}, u32[]{:S(2)}, u32[]{:S(2)}) collective-permute-start(bf16[2,432,128]{2,1,0:T(8,128)(2,1)S(1)} %fusion), channel_id=1, source_target_pairs={{0,8},{4,12},{8,0},{12,4},{16,24},{20,28},{24,16},{28,20},{32,40},... | collective-permute-start | bytes 663560 | tf_op jit(solution)/shard_map/ppermute | solution.py:388
  47.4 2.4 %backward.4.refs_0_ = f32[256,128]{1,0:T(8,128)S(1)} custom-call(bf16[1024,128]{1,0:T(8,128)(2,1)S(1)} %get-tuple-element.55.grad_ref, s32[27,1024]{1,0:T(8,128)S(1)} %bitcast.43, bf16[27,128,128]{2,1,0:T(8,128)(2,1)S(1)} %bitcast.31), custom_call_target="tpu_custom_call" | custom-call | flops 3000000000 | bytes 2000000 | tf_op jit(solution)/shard_map/backward/pallas_call | solution.py:463
  49.9 2.4 %backward.5.refs_1_ = f32[256,128]{1,0:T(8,128)S(1)} custom-call(bf16[1024,128]{1,0:T(8,128)(2,1)S(1)} %get-tuple-element.55.grad_ref, s32[27,1024]{1,0:T(8,128)S(1)} %bitcast.44, bf16[27,128,128]{2,1,0:T(8,128)(2,1)S(1)} %bitcast.32), custom_call_target="tpu_custom_call" | custom-call | flops 3000000000 | bytes 2000000 | tf_op jit(solution)/shard_map/backward/pallas_call | solution.py:463
  52.4 0.5 collective-permute-done.6
  52.9 0.1 collective-permute-start.7
  53.0 1.3 %collective-permute-start.9 = (bf16[320,128]{1,0:T(8,128)(2,1)S(1)}, bf16[320,128]{1,0:T(8,128)(2,1)S(1)}, u32[]{:S(2)}, u32[]{:S(2)}) collective-permute-start(bf16[320,128]{1,0:T(8,128)(2,1)S(1)} %get-tuple-element.57), channel_id=1, source_target_pairs={{0,4},{4,0},{8,12},{12,8},{16,20},{20,16},{24,28},{28,24},{32,36},... | collective-permute-start | bytes 245768 | tf_op jit(solution)/shard_map/ppermute | solution.py:371
  54.3 1.2 %collective-permute-start.10 = (bf16[320,128]{1,0:T(8,128)(2,1)S(1)}, bf16[320,128]{1,0:T(8,128)(2,1)S(1)}, u32[]{:S(2)}, u32[]{:S(2)}) collective-permute-start(bf16[320,128]{1,0:T(8,128)(2,1)S(1)} %get-tuple-element.59), channel_id=1, source_target_pairs={{0,12},{4,8},{8,4},{12,0},{16,28},{20,24},{24,20},{28,16},{32,44},... | collective-permute-start | bytes 245768 | tf_op jit(solution)/shard_map/ppermute | solution.py:371
  55.5 1.1 %collective-permute-done.7 = bf16[432,128]{1,0:T(8,128)(2,1)S(1)} collective-permute-done((bf16[432,128]{1,0:T(8,128)(2,1)S(1)}, bf16[432,128]{1,0:T(8,128)(2,1)S(1)}, u32[]{:S(2)}, u32[]{:S(2)}) %collective-permute-start.7) | collective-permute-done | bytes 110624 | tf_op jit(solution)/shard_map/ppermute | solution.py:388
  56.6 0.6 collective-permute-start.8
  57.3 2.4 %backward.6.refs_2_ = f32[256,128]{1,0:T(8,128)S(1)} custom-call(bf16[1024,128]{1,0:T(8,128)(2,1)S(1)} %get-tuple-element.55.grad_ref, s32[27,1024]{1,0:T(8,128)S(1)} %bitcast.45, bf16[27,128,128]{2,1,0:T(8,128)(2,1)S(1)} %bitcast.33), custom_call_target="tpu_custom_call" | custom-call | flops 3000000000 | bytes 2000000 | tf_op jit(solution)/shard_map/backward/pallas_call | solution.py:463
  59.7 0.2 collective-permute-start.15
  60.0 1.6 %collective-permute-done.8 = bf16[432,128]{1,0:T(8,128)(2,1)S(1)} collective-permute-done((bf16[432,128]{1,0:T(8,128)(2,1)S(1)}, bf16[432,128]{1,0:T(8,128)(2,1)S(1)}, u32[]{:S(2)}, u32[]{:S(2)}) %collective-permute-start.8) | collective-permute-done | bytes 110624 | tf_op jit(solution)/shard_map/ppermute | solution.py:388
  61.6 0.5 collective-permute-start.13
  62.0 0.0 collective-permute-done.10.ixb_ref
  62.0 0.0 collective-permute-done.9.ixa_ref
  62.0 2.4 %backward.7.refs_3_ = f32[256,128]{1,0:T(8,128)S(1)} custom-call(bf16[1024,128]{1,0:T(8,128)(2,1)S(1)} %get-tuple-element.55.grad_ref, s32[27,1024]{1,0:T(8,128)S(1)} %bitcast.46, bf16[27,128,128]{2,1,0:T(8,128)(2,1)S(1)} %bitcast.34), custom_call_target="tpu_custom_call" | custom-call | flops 3000000000 | bytes 2000000 | tf_op jit(solution)/shard_map/backward/pallas_call | solution.py:463
  64.5 1.4 %collective-permute-start.11 = (bf16[320,128]{1,0:T(8,128)(2,1)S(1)}, bf16[320,128]{1,0:T(8,128)(2,1)S(1)}, u32[]{:S(2)}, u32[]{:S(2)}) collective-permute-start(bf16[320,128]{1,0:T(8,128)(2,1)S(1)} %pad_maximum_fusion.4), channel_id=1, source_target_pairs={{0,16},{4,20},{8,24},{12,28},{16,0},{20,4},{24,8},{28,12},{32,48},... | collective-permute-start | bytes 245768 | tf_op jit(solution)/shard_map/ppermute | solution.py:380
  65.9 3.7 %collective-permute-start.12 = (bf16[320,128]{1,0:T(8,128)(2,1)S(1)}, bf16[320,128]{1,0:T(8,128)(2,1)S(1)}, u32[]{:S(2)}, u32[]{:S(2)}) collective-permute-start(bf16[320,128]{1,0:T(8,128)(2,1)S(1)} %pad_maximum_fusion.5), channel_id=1, source_target_pairs={{0,112},{4,116},{8,120},{12,124},{16,32},{20,36},{24,40},{28,44},{... | collective-permute-start | bytes 245768 | tf_op jit(solution)/shard_map/ppermute | solution.py:380
  69.6 0.0 collective-permute-done.13
  69.6 0.3 collective-permute-start.14
  70.0 0.0 collective-permute-done.11.iya_ref
  70.0 2.8 %collective-permute-done.12.iyb_ref = bf16[320,128]{1,0:T(8,128)(2,1)S(1)} collective-permute-done((bf16[320,128]{1,0:T(8,128)(2,1)S(1)}, bf16[320,128]{1,0:T(8,128)(2,1)S(1)}, u32[]{:S(2)}, u32[]{:S(2)}) %collective-permute-start.12) | collective-permute-done | bytes 81952 | tf_op jit(solution)/shard_map/ppermute | solution.py:380
  72.8 3.0 %returning.1.refs_4_ = f32[1152,128]{1,0:T(8,128)S(1)} custom-call(s32[3]{0:T(128)S(1)} %pad_add_fusion.side_ref, bf16[320,128]{1,0:T(8,128)(2,1)S(1)} %collective-permute-done.9.ixa_ref, bf16[320,128]{1,0:T(8,128)(2,1)S(1)} %collective-permute-done.10.ixb_ref, bf16[320,128]{1,0:T(8,128)(2,1)S(1)} %collective-permute-done.11.iya_ref, ...), custom_call_target="tpu_custom_call" | custom-call | flops 3000000000 | bytes 4000000 | tf_op jit(solution)/shard_map/returning/pallas_call | solution.py:498
  75.8 0.0 collective-permute-done.14.one_ref
  75.9 1.4 %collective-permute-start.16 = (bf16[2,432,128]{2,1,0:T(8,128)(2,1)S(1)}, bf16[2,432,128]{2,1,0:T(8,128)(2,1)S(1)}, u32[]{:S(2)}, u32[]{:S(2)}) collective-permute-start(bf16[2,432,128]{2,1,0:T(8,128)(2,1)S(1)} %pad_maximum_fusion.1), channel_id=1, source_target_pairs={{0,8},{4,12},{8,0},{12,4},{16,24},{20,28},{24,16},{28,20},{32,40},... | collective-permute-start | bytes 663560 | tf_op jit(solution)/shard_map/ppermute | solution.py:388
  77.3 0.0 collective-permute-done.15.refs_7_
  77.3 1.7 %final.1 = (bf16[1024,128]{1,0:T(8,128)(2,1)}, bf16[1024,128]{1,0:T(8,128)(2,1)}) custom-call(f32[256,128]{1,0:T(8,128)S(1)} %backward.4.refs_0_, f32[256,128]{1,0:T(8,128)S(1)} %backward.5.refs_1_, f32[256,128]{1,0:T(8,128)S(1)} %backward.6.refs_2_, f32[256,128]{1,0:T(8,128)S(1)} %backward.7.refs_3_, f32[1152,128]{1,0:T(8,128)S(1)} %returning.1.refs_4_, ...), custom_call_target="tpu_custom_call" | custom-call | flops 1000000000 | bytes 3000000 | tf_op jit(solution)/shard_map/final/pallas_call | solution.py:508
  79.0 1.7 %collective-permute-done.16.two_ref = bf16[2,432,128]{2,1,0:T(8,128)(2,1)S(1)} collective-permute-done((bf16[2,432,128]{2,1,0:T(8,128)(2,1)S(1)}, bf16[2,432,128]{2,1,0:T(8,128)(2,1)S(1)}, u32[]{:S(2)}, u32[]{:S(2)}) %collective-permute-start.16) | collective-permute-done | bytes 221216 | tf_op jit(solution)/shard_map/ppermute | solution.py:388
  80.8 6.0 %collective-permute-start.17 = (bf16[4,432,128]{2,1,0:T(8,128)(2,1)S(1)}, bf16[4,432,128]{2,1,0:T(8,128)(2,1)S(1)}, u32[]{:S(2)}, u32[]{:S(2)}) collective-permute-start(bf16[4,432,128]{2,1,0:T(8,128)(2,1)S(1)} %pad_maximum_fusion), channel_id=1, source_target_pairs={{0,4},{4,0},{8,12},{12,8},{16,20},{20,16},{24,28},{28,24},{32,36},... | collective-permute-start | bytes 1327112 | tf_op jit(solution)/shard_map/ppermute | solution.py:388
  86.8 0.1 pad_add_fusion.1.bits_ref
  86.9 1.3 %collective-permute-done.17.four_ref = bf16[4,432,128]{2,1,0:T(8,128)(2,1)S(1)} collective-permute-done((bf16[4,432,128]{2,1,0:T(8,128)(2,1)S(1)}, bf16[4,432,128]{2,1,0:T(8,128)(2,1)S(1)}, u32[]{:S(2)}, u32[]{:S(2)}) %collective-permute-start.17) | collective-permute-done | bytes 442400 | tf_op jit(solution)/shard_map/ppermute | solution.py:388
  88.2 1.9 %assemble.1 = f32[8,432,128]{2,1,0:T(8,128)} custom-call(s32[3]{0:T(128)S(1)} %pad_add_fusion.1.bits_ref, bf16[432,128]{1,0:T(8,128)(2,1)S(1)} %add_convert_fusion.own_ref, bf16[432,128]{1,0:T(8,128)(2,1)S(1)} %collective-permute-done.14.one_ref, bf16[2,432,128]{2,1,0:T(8,128)(2,1)S(1)} %collective-permute-done.16.two_ref, ...), custom_call_target="tpu_custom_call" | custom-call | flops 1000000 | bytes 3000000 | tf_op jit(solution)/shard_map/assemble/pallas_call | solution.py:517
  (15 shorter events, 0.3 us)
Async XLA Ops:
  1.4 1.0 %copy-start.2 = (bf16[1,1024,128]{2,1,0:T(8,128)(2,1)S(1)}, bf16[1,1024,128]{2,1,0:T(8,128)(2,1)}, u32[]{:S(2)}) copy-start(bf16[1,1024,128]{2,1,0:T(8,128)(2,1)} %param.6) | copy-start | bytes 786436
  2.4 0.9 %copy-start.4 = (s32[1152,27]{0,1:T(8,128)S(1)}, s32[1152,27]{0,1:T(8,128)}, u32[]{:S(2)}) copy-start(s32[1152,27]{0,1:T(8,128)} %param.10) | copy-start | bytes 373252
  3.3 3.8 %copy-start.1 = (bf16[1,1024,128]{2,1,0:T(8,128)(2,1)S(1)}, bf16[1,1024,128]{2,1,0:T(8,128)(2,1)}, u32[]{:S(2)}) copy-start(bf16[1,1024,128]{2,1,0:T(8,128)(2,1)} %param.8) | copy-start | bytes 786436
  3.3 17.1 %copy-start = (bf16[1,27,128,128]{3,2,1,0:T(8,128)(2,1)S(1)}, bf16[1,27,128,128]{3,2,1,0:T(8,128)(2,1)}, u32[]{:S(2)}) copy-start(bf16[1,27,128,128]{3,2,1,0:T(8,128)(2,1)} %param.7) | copy-start | bytes 2654212
  3.3 17.1 %copy-start.3 = (bf16[1,1024,128]{2,1,0:T(8,128)(2,1)S(1)}, bf16[1,1024,128]{2,1,0:T(8,128)(2,1)}, u32[]{:S(2)}) copy-start(bf16[1,1024,128]{2,1,0:T(8,128)(2,1)} %param.6) | copy-start | bytes 786436
  3.3 17.1 %copy-start.5 = (s32[1024,27]{0,1:T(8,128)S(1)}, s32[1024,27]{0,1:T(8,128)}, u32[]{:S(2)}) copy-start(s32[1024,27]{0,1:T(8,128)} %param.9) | copy-start | bytes 331780
  5.6 4.4 %collective-permute-start = (bf16[384,128]{1,0:T(8,128)(2,1)S(1)}, bf16[384,128]{1,0:T(8,128)(2,1)S(1)}, u32[]{:S(2)}, u32[]{:S(2)}) collective-permute-start(bf16[384,128]{1,0:T(8,128)(2,1)S(1)} %get-tuple-element.41), channel_id=1, source_target_pairs={{0,4},{4,0},{8,12},{12,8},{16,20},{20,16},{24,28},{28,24},{32,36},... | collective-permute-start | bytes 294920 | tf_op jit(solution)/shard_map/ppermute | solution.py:371
  7.1 24.1 %collective-permute-start.4 = (bf16[1024,128]{1,0:T(8,128)(2,1)S(1)}, bf16[1024,128]{1,0:T(8,128)(2,1)S(1)}, u32[]{:S(2)}, u32[]{:S(2)}) collective-permute-start(bf16[1024,128]{1,0:T(8,128)(2,1)S(1)} %bitcast.36), channel_id=1, source_target_pairs={{0,1},{1,0},{2,3},{3,2},{4,5},{5,4},{6,7},{7,6},{8,9},{9,8},{10,11... | collective-permute-start | bytes 786440 | tf_op jit(solution)/shard_map/ppermute | solution.py:384
  8.5 5.1 %collective-permute-start.1 = (bf16[384,128]{1,0:T(8,128)(2,1)S(1)}, bf16[384,128]{1,0:T(8,128)(2,1)S(1)}, u32[]{:S(2)}, u32[]{:S(2)}) collective-permute-start(bf16[384,128]{1,0:T(8,128)(2,1)S(1)} %get-tuple-element.42), channel_id=1, source_target_pairs={{0,12},{4,8},{8,4},{12,0},{16,28},{20,24},{24,20},{28,16},{32,44},... | collective-permute-start | bytes 294920 | tf_op jit(solution)/shard_map/ppermute | solution.py:371
  13.6 17.6 %collective-permute-start.2 = (bf16[384,128]{1,0:T(8,128)(2,1)S(1)}, bf16[384,128]{1,0:T(8,128)(2,1)S(1)}, u32[]{:S(2)}, u32[]{:S(2)}) collective-permute-start(bf16[384,128]{1,0:T(8,128)(2,1)S(1)} %pad_maximum_fusion.2), channel_id=1, source_target_pairs={{0,16},{4,20},{8,24},{12,28},{16,0},{20,4},{24,8},{28,12},{32,48},... | collective-permute-start | bytes 294920 | tf_op jit(solution)/shard_map/ppermute | solution.py:380
  16.4 14.8 %collective-permute-start.3 = (bf16[384,128]{1,0:T(8,128)(2,1)S(1)}, bf16[384,128]{1,0:T(8,128)(2,1)S(1)}, u32[]{:S(2)}, u32[]{:S(2)}) collective-permute-start(bf16[384,128]{1,0:T(8,128)(2,1)S(1)} %pad_maximum_fusion.3), channel_id=1, source_target_pairs={{0,112},{4,116},{8,120},{12,124},{16,32},{20,36},{24,40},{28,44},{... | collective-permute-start | bytes 294920 | tf_op jit(solution)/shard_map/ppermute | solution.py:380
  42.5 2.3 %collective-permute-start.5 = (bf16[1728,128]{1,0:T(8,128)(2,1)S(1)}, bf16[1728,128]{1,0:T(8,128)(2,1)}, u32[]{:S(2)}, u32[]{:S(2)}) collective-permute-start(bf16[1728,128]{1,0:T(8,128)(2,1)S(1)} %get-tuple-element.49), channel_id=1, source_target_pairs={{0,4},{4,0},{8,12},{12,8},{16,20},{20,16},{24,28},{28,24},{32,36},... | collective-permute-start | bytes 1327112 | tf_op jit(solution)/shard_map/ppermute | solution.py:388
  45.9 6.9 %collective-permute-start.6 = (bf16[2,432,128]{2,1,0:T(8,128)(2,1)S(1)}, bf16[2,432,128]{2,1,0:T(8,128)(2,1)S(1)}, u32[]{:S(2)}, u32[]{:S(2)}) collective-permute-start(bf16[2,432,128]{2,1,0:T(8,128)(2,1)S(1)} %fusion), channel_id=1, source_target_pairs={{0,8},{4,12},{8,0},{12,4},{16,24},{20,28},{24,16},{28,20},{32,40},... | collective-permute-start | bytes 663560 | tf_op jit(solution)/shard_map/ppermute | solution.py:388
  52.9 3.7 %collective-permute-start.7 = (bf16[432,128]{1,0:T(8,128)(2,1)S(1)}, bf16[432,128]{1,0:T(8,128)(2,1)S(1)}, u32[]{:S(2)}, u32[]{:S(2)}) collective-permute-start(bf16[432,128]{1,0:T(8,128)(2,1)S(1)} %fusion.2), channel_id=1, source_target_pairs={{0,32},{4,36},{8,40},{12,44},{16,48},{20,52},{24,56},{28,60},{32,0... | collective-permute-start | bytes 331784 | tf_op jit(solution)/shard_map/ppermute | solution.py:388
  53.0 9.0 %collective-permute-start.9 = (bf16[320,128]{1,0:T(8,128)(2,1)S(1)}, bf16[320,128]{1,0:T(8,128)(2,1)S(1)}, u32[]{:S(2)}, u32[]{:S(2)}) collective-permute-start(bf16[320,128]{1,0:T(8,128)(2,1)S(1)} %get-tuple-element.57), channel_id=1, source_target_pairs={{0,4},{4,0},{8,12},{12,8},{16,20},{20,16},{24,28},{28,24},{32,36},... | collective-permute-start | bytes 245768 | tf_op jit(solution)/shard_map/ppermute | solution.py:371
  54.3 7.7 %collective-permute-start.10 = (bf16[320,128]{1,0:T(8,128)(2,1)S(1)}, bf16[320,128]{1,0:T(8,128)(2,1)S(1)}, u32[]{:S(2)}, u32[]{:S(2)}) collective-permute-start(bf16[320,128]{1,0:T(8,128)(2,1)S(1)} %get-tuple-element.59), channel_id=1, source_target_pairs={{0,12},{4,8},{8,4},{12,0},{16,28},{20,24},{24,20},{28,16},{32,44},... | collective-permute-start | bytes 245768 | tf_op jit(solution)/shard_map/ppermute | solution.py:371
  56.6 4.9 %collective-permute-start.8 = (bf16[432,128]{1,0:T(8,128)(2,1)S(1)}, bf16[432,128]{1,0:T(8,128)(2,1)S(1)}, u32[]{:S(2)}, u32[]{:S(2)}) collective-permute-start(bf16[432,128]{1,0:T(8,128)(2,1)S(1)} %fusion.1), channel_id=1, source_target_pairs={{0,24},{4,28},{8,16},{12,20},{16,8},{20,12},{24,0},{28,4},{32,56},... | collective-permute-start | bytes 331784 | tf_op jit(solution)/shard_map/ppermute | solution.py:388
  59.7 17.6 %collective-permute-start.15 = (bf16[1024,128]{1,0:T(8,128)(2,1)S(1)}, bf16[1024,128]{1,0:T(8,128)(2,1)S(1)}, u32[]{:S(2)}, u32[]{:S(2)}) collective-permute-start(bf16[1024,128]{1,0:T(8,128)(2,1)S(1)} %get-tuple-element.73.refs_6_), channel_id=1, source_target_pairs={{0,1},{1,0},{2,3},{3,2},{4,5},{5,4},{6,7},{7,6},{8,9},{9,8},{10,11... | collective-permute-start | bytes 786440 | tf_op jit(solution)/shard_map/ppermute | solution.py:384
  61.6 8.0 %collective-permute-start.13 = (bf16[432,128]{1,0:T(8,128)(2,1)S(1)}, bf16[432,128]{1,0:T(8,128)(2,1)S(1)}, u32[]{:S(2)}, u32[]{:S(2)}) collective-permute-start(bf16[432,128]{1,0:T(8,128)(2,1)S(1)} %add_convert_fusion.1), channel_id=1, source_target_pairs={{0,96},{4,100},{8,104},{12,108},{16,112},{20,116},{24,120},{28,124... | collective-permute-start | bytes 331784 | tf_op jit(solution)/shard_map/ppermute | solution.py:388
  64.5 5.5 %collective-permute-start.11 = (bf16[320,128]{1,0:T(8,128)(2,1)S(1)}, bf16[320,128]{1,0:T(8,128)(2,1)S(1)}, u32[]{:S(2)}, u32[]{:S(2)}) collective-permute-start(bf16[320,128]{1,0:T(8,128)(2,1)S(1)} %pad_maximum_fusion.4), channel_id=1, source_target_pairs={{0,16},{4,20},{8,24},{12,28},{16,0},{20,4},{24,8},{28,12},{32,48},... | collective-permute-start | bytes 245768 | tf_op jit(solution)/shard_map/ppermute | solution.py:380
  65.9 6.9 %collective-permute-start.12 = (bf16[320,128]{1,0:T(8,128)(2,1)S(1)}, bf16[320,128]{1,0:T(8,128)(2,1)S(1)}, u32[]{:S(2)}, u32[]{:S(2)}) collective-permute-start(bf16[320,128]{1,0:T(8,128)(2,1)S(1)} %pad_maximum_fusion.5), channel_id=1, source_target_pairs={{0,112},{4,116},{8,120},{12,124},{16,32},{20,36},{24,40},{28,44},{... | collective-permute-start | bytes 245768 | tf_op jit(solution)/shard_map/ppermute | solution.py:380
  69.6 6.2 %collective-permute-start.14 = (bf16[432,128]{1,0:T(8,128)(2,1)S(1)}, bf16[432,128]{1,0:T(8,128)(2,1)S(1)}, u32[]{:S(2)}, u32[]{:S(2)}) collective-permute-start(bf16[432,128]{1,0:T(8,128)(2,1)S(1)} %add_convert_fusion.own_ref), channel_id=1, source_target_pairs={{0,32},{4,36},{8,40},{12,44},{16,48},{20,52},{24,56},{28,60},{32,0... | collective-permute-start | bytes 331784 | tf_op jit(solution)/shard_map/ppermute | solution.py:388
  75.9 4.9 %collective-permute-start.16 = (bf16[2,432,128]{2,1,0:T(8,128)(2,1)S(1)}, bf16[2,432,128]{2,1,0:T(8,128)(2,1)S(1)}, u32[]{:S(2)}, u32[]{:S(2)}) collective-permute-start(bf16[2,432,128]{2,1,0:T(8,128)(2,1)S(1)} %pad_maximum_fusion.1), channel_id=1, source_target_pairs={{0,8},{4,12},{8,0},{12,4},{16,24},{20,28},{24,16},{28,20},{32,40},... | collective-permute-start | bytes 663560 | tf_op jit(solution)/shard_map/ppermute | solution.py:388
  80.8 7.4 %collective-permute-start.17 = (bf16[4,432,128]{2,1,0:T(8,128)(2,1)S(1)}, bf16[4,432,128]{2,1,0:T(8,128)(2,1)S(1)}, u32[]{:S(2)}, u32[]{:S(2)}) collective-permute-start(bf16[4,432,128]{2,1,0:T(8,128)(2,1)S(1)} %pad_maximum_fusion), channel_id=1, source_target_pairs={{0,4},{4,0},{8,12},{12,8},{16,20},{20,16},{24,28},{28,24},{32,36},... | collective-permute-start | bytes 1327112 | tf_op jit(solution)/shard_map/ppermute | solution.py:388
